TPU v7x, 256 devices: a whole 4x4x8 slice. The times are simulated.
256 devices in a mesh: blk: 64 (over x, z, core), rep: 4 (over y).
Axes of the slice: x: 4, y: 4, z: 8, core: 2. Of those that a mesh axis runs over, the one named last changes fastest.
Arguments:
- amplitudes: float32 [2, 640, 640], P(None, 'blk', 'rep'), may hold values from -2 to 2
- singles: bfloat16 [100, 640], replicated, may hold values from -2 to 2
- chol_vv: bfloat16 [1536, 640, 640], P('rep', 'blk'), may hold values from -0.3984375 to 0.3984375
- chol_ov: bfloat16 [1536, 100, 640], P('rep', None, 'blk'), may hold values from -1.5 to 1.5
- occ_energy: float32 [100], replicated, may hold values from -2 to -0.3
- vir_energy: float32 [640], replicated, may hold values from 0.2 to 4
- vir_irrep: int32 [640], replicated, may hold values from 0 to 7, as said below
- occ_irrep: int32 [100], replicated, may hold values from 0 to 7, as said below
- chol_irrep: int32 [1536], replicated, may hold values from 0 to 7, as said below
- pair_list: int32 [2, 2], replicated, may hold values from 0 to 99
Outputs:
- residual: float32 [2, 640, 640], P(None, 'blk', 'rep')
- updated: float32 [2, 640, 640], P(None, 'blk', 'rep')
Inputs may be any that keep to these rules, and one draw needn't show every extreme that they name: `vir_irrep`: nondecreasing; each of the 8 irreps labels a run of 64 to 160 orbitals, and one run has exactly 160. `occ_irrep`: nondecreasing; each of the 8 irreps labels a run of orbitals. `chol_irrep`: nondecreasing; each of the 8 irreps labels a run of vectors.
All inputs are finite; a program needn't handle non-finite values.
Results may differ from a plain program's by a relative error of at most 0.0041.
Values may be sent and summed in bfloat16 or wider, within the bound.
No kernel may reach another device: no remote copies, remote signals or barrier semaphores. Data moves between devices by JAX's collectives and lax.ppermute only.
A program may use at most 128 MiB of HBM per device.

v0:
```python
import jax
import jax.numpy as jnp
from jax import lax
from jax.sharding import PartitionSpec as P


def ladder_pair(chol_block, amp_pair):
    halfway = jnp.einsum(
        "qac,cd->qad", chol_block, amp_pair, preferred_element_type=jnp.float32
    ).astype(jnp.bfloat16)
    return jnp.einsum("qad,qbd->ab", halfway, chol_block, preferred_element_type=jnp.float32)


def per_device(
    amplitudes,
    singles,
    chol_vv,
    chol_ov,
    occ_energy,
    vir_energy,
    vir_irrep,
    occ_irrep,
    chol_irrep,
    pair_list,
):
    blk_pos = lax.axis_index("blk")
    rep_pos = lax.axis_index("rep")
    q_local, row_count, vir_total = chol_vv.shape
    pair_count = amplitudes.shape[0]
    col_count = amplitudes.shape[2]
    row_irrep = lax.dynamic_slice_in_dim(vir_irrep, blk_pos * row_count, row_count)
    col_irrep = lax.dynamic_slice_in_dim(vir_irrep, rep_pos * col_count, col_count)
    q_irrep = lax.dynamic_slice_in_dim(chol_irrep, rep_pos * q_local, q_local)
    row_energy = lax.dynamic_slice_in_dim(vir_energy, blk_pos * row_count, row_count)
    col_energy = lax.dynamic_slice_in_dim(vir_energy, rep_pos * col_count, col_count)
    pair_first = pair_list[:, 0]
    pair_second = pair_list[:, 1]
    pair_sym = jnp.bitwise_xor(occ_irrep[pair_first], occ_irrep[pair_second])
    amp_mask = (
        jnp.bitwise_xor(row_irrep[None, :, None], col_irrep[None, None, :])
        == pair_sym[:, None, None]
    )
    amp_local = jnp.where(amp_mask, amplitudes, jnp.zeros((), amplitudes.dtype))
    amp_rows = lax.all_gather(amp_local.astype(jnp.bfloat16), "rep", axis=2, tiled=True)
    amp_whole = lax.all_gather(amp_rows, "blk", axis=1, tiled=True)
    vv_mask = (
        jnp.bitwise_xor(row_irrep[None, :, None], vir_irrep[None, None, :])
        == q_irrep[:, None, None]
    )
    chol_masked = jnp.where(vv_mask, chol_vv, jnp.zeros((), chol_vv.dtype))
    occ_rows = pair_list.reshape(-1)
    occ_labels = occ_irrep[occ_rows]
    single_rows = jnp.where(
        occ_labels[:, None] == vir_irrep[None, :], singles[occ_rows], jnp.zeros((), singles.dtype)
    )
    ov_rows = jnp.take(chol_ov, occ_rows, axis=1).astype(jnp.float32)
    ov_mask = (
        jnp.bitwise_xor(occ_labels[None, :, None], row_irrep[None, None, :])
        == q_irrep[:, None, None]
    )
    dressing = jnp.einsum(
        "qac,mc->qma", chol_masked, single_rows, preferred_element_type=jnp.float32
    )
    dressed = (jnp.where(ov_mask, ov_rows, jnp.zeros((), ov_rows.dtype)) + dressing).astype(
        jnp.bfloat16
    )
    dressed_all = lax.all_gather(dressed, "blk", axis=2, tiled=True)
    cycle_part = jnp.einsum(
        "qpa,qpb->pab",
        dressed[:, 0::2, :],
        dressed_all[:, 1::2, :],
        preferred_element_type=jnp.float32,
    )
    regrouped = lax.all_to_all(chol_masked, "blk", split_axis=0, concat_axis=1, tiled=True)
    partial_value = jnp.stack(
        [ladder_pair(regrouped, amp_whole[pair_index]) for pair_index in range(pair_count)]
    )
    row_sums = lax.psum_scatter(partial_value, "blk", scatter_dimension=1, tiled=True)
    summed = lax.psum_scatter(row_sums + cycle_part, "rep", scatter_dimension=2, tiled=True)
    denominator = (
        (occ_energy[pair_first] + occ_energy[pair_second])[:, None, None]
        - row_energy[None, :, None]
        - col_energy[None, None, :]
    )
    residual = summed + denominator * amp_local
    updated = amp_local - residual / denominator
    return (residual, updated)


def solution(mesh):
    in_specs = (
        P(None, "blk", "rep"),
        P(),
        P("rep", "blk", None),
        P("rep", None, "blk"),
        P(),
        P(),
        P(),
        P(),
        P(),
        P(),
    )
    out_specs = (P(None, "blk", "rep"), P(None, "blk", "rep"))
    return jax.shard_map(
        per_device, mesh=mesh, in_specs=in_specs, out_specs=out_specs, check_vma=False
    )
```

profile of v0, /device:TPU:6, one launch (start us, length us, event | category | flops | bytes accessed | tf_op | source)
XLA Modules:
  0.0 486.0 jit_solution(13491273343317744284)
XLA Ops:
  7.2 0.8 dynamic_slice.15
  8.0 0.8 broadcast_xor_fusion.1
  8.8 0.8 dynamic_slice.16
  9.6 11.2 %compare_select_fusion = bf16[384,10,640]{2,1,0:T(8,128)(2,1)} fusion(bf16[384,10,640]{2,0,1:T(8,128)(2,1)} %param.12, s32[10,640]{1,0:T(8,128)S(1)} %broadcast_xor_fusion.1, s32[384]{0:T(512)S(1)} %dynamic_slice.16), kind=kLoop, calls=%fused_computation.7 | loop fusion | flops 4915200 | bytes 9857536 | tf_op jit(solution)/shard_map/jit(_where)/select_n | solution.py:50
  20.8 12.5 %all-to-all-start = ((bf16[384,10,640]{2,1,0:T(8,128)(2,1)}), bf16[384,10,640]{2,1,0:T(8,128)(2,1)}, u32[]{:S(2)}, u32[]{:S(2)}) async-start(bf16[384,10,640]{2,1,0:T(8,128)(2,1)} %compare_select_fusion), calls=%async_computation | async-start | bytes 15728640 | tf_op jit(solution)/shard_map/all_to_all | solution.py:74
  33.3 0.1 copy.29
  33.5 0.2 fusion.50
  33.7 0.6 gather_fusion
  34.3 0.6 gather_fusion.1
  35.0 0.1 dynamic_slice.17
  35.1 0.1 broadcast_xor_fusion
  35.2 0.2 fusion.54
  35.4 12.9 %all_gather.9 = bf16[2,10,640]{1,0,2:T(2,128)(2,1)S(1)} all-gather(bf16[2,10,160]{1,0,2:T(2,128)(2,1)S(1)} %get-tuple-element.12), channel_id=1, replica_groups=mesh['blk'=64,'rep'=4] {'rep'}, dimensions={2}, use_global_device_ids=true | all-gather | bytes 32000 | tf_op jit(solution)/shard_map/all_gather | solution.py:44
  48.3 0.8 copy.30
  49.1 0.1 reshape.183
  49.2 0.1 reshape.184
  49.3 0.6 gather_fusion.2
  49.9 0.7 gather_fusion.3
  50.6 1.5 gather_fusion.4
  52.2 0.1 broadcast_xor_fusion.2
  52.2 5.4 %fusion.37 = bf16[384,4,10]{0,1,2:T(4,128)(2,1)} fusion(bf16[384,10,640]{2,1,0:T(8,128)(2,1)} %compare_select_fusion, bf16[4,384,10]{1,0,2:T(4,128)(2,1)S(1)} %gather_fusion.3, s32[384]{0:T(512)S(1)} %dynamic_slice.16, s32[4,10]{0,1:T(8,128)S(1)} %broadcast_xor_fusion.2, pred[4]{0:T(512)(128)(4,1)S(1)} %compare_and_fusion, ...), kind=kOutput, calls=%fused_computation.25 | convolution fusion | flops 19758080 | bytes 4986036 | tf_op jit(solution)/shard_map/qac,mc->qma/dot_general | solution.py:61
  57.6 0.0 all-reduce.3.cloned.1.call-start
  57.7 80.2 %all-gather.3.cloned.1.call-done = bf16[2,640,640]{2,0,1:T(2,128)(2,1)} async-done(((bf16[2,10,640]{2,0,1:T(2,128)(2,1)}), bf16[2,640,640]{2,0,1:T(2,128)(2,1)}) %all-gather.3.cloned.1.call-update) | async-done | bytes 1638416 | tf_op jit(solution)/shard_map/all_gather | solution.py:45
  137.9 5.6 %fusion.55 = (bf16[1,640,640]{2,0,1:T(2,128)(2,1)S(1)}, bf16[1,640,640]{2,0,1:T(2,128)(2,1)}) fusion(bf16[2,640,640]{2,0,1:T(2,128)(2,1)} %all-gather.3.cloned.1.call-done), kind=kLoop, calls=%fused_computation.59 | loop fusion | bytes 3276800 | tf_op jit(solution)/shard_map/slice | solution.py:76
  143.5 69.7 %all-to-all-done = bf16[384,10,640]{2,1,0:T(8,128)(2,1)} async-done(((bf16[384,10,640]{2,1,0:T(8,128)(2,1)}), bf16[384,10,640]{2,1,0:T(8,128)(2,1)}, u32[]{:S(2)}, u32[]{:S(2)}) %all-to-all-start) | async-done | bytes 4915232 | tf_op jit(solution)/shard_map/all_to_all | solution.py:74
  213.2 7.8 %copy.28 = bf16[6,64,10,640]{3,0,2,1:T(8,128)(2,1)} copy(bf16[6,64,10,640]{3,2,0,1:T(8,128)(2,1)} %bitcast.2) | data formatting | bytes 9830400 | tf_op jit(solution)/shard_map/all_to_all | solution.py:74
  221.0 16.1 %fusion.24 = f32[1,640,640]{2,1,0:T(8,128)} fusion(bf16[6,640,640]{2,0,1:T(8,128)(2,1)} %bitcast.41, bf16[1,640,640]{2,0,1:T(2,128)(2,1)} %get-tuple-element.15), kind=kOutput, calls=%fused_computation.21 | convolution fusion | flops 6293913600 | bytes 7372800 | tf_op jit(solution)/shard_map/qad,qbd->ab/dot_general | solution.py:11
  237.1 15.8 %fusion.17 = f32[1,640,640]{2,1,0:T(8,128)} fusion(bf16[6,640,640]{2,0,1:T(8,128)(2,1)} %bitcast.42, bf16[1,640,640]{2,0,1:T(2,128)(2,1)S(1)} %get-tuple-element.14), kind=kOutput, calls=%fused_computation.20 | convolution fusion | flops 6293913600 | bytes 7372800 | tf_op jit(solution)/shard_map/qad,qbd->ab/dot_general | solution.py:11
  252.9 2.1 pad_maximum_fusion
  255.1 4.3 copy.37
  259.4 0.0 reduce-scatter.4.cloned.1.call-start
  259.4 0.6 gather_fusion.5
  260.1 0.6 gather_fusion.6
  260.7 0.8 dynamic_slice.18
  261.5 0.6 dynamic-slice
  262.8 25.7 %slice.23 = bf16[384,2,640]{0,1,2:T(2,128)(2,1)S(1)} slice(bf16[384,4,640]{0,1,2:T(4,128)(2,1)} %all-gather.5.cloned.1.call-done), slice={[0:384:1], [1:4:2], [0:640:1]} | slice | bytes 1966080 | tf_op jit(solution)/shard_map/slice | solution.py:71
  288.5 162.3 %all-reduce.3.cloned.1.call-done = f32[2,640,640]{2,0,1:T(2,128)} async-done(((f32[2,640,640]{2,0,1:T(2,128)}), f32[2,640,640]{2,0,1:T(2,128)}) %all-reduce.3.cloned.1.call-update) | async-done | bytes 3276816
  450.8 0.8 constant_dynamic-slice_fusion
  451.6 0.4 convolution_add_fusion
  451.9 0.3 copy.47
  452.3 1.1 reshape.246
  453.4 0.1 broadcast_subtract_fusion
  453.5 0.8 dynamic_slice.19
  454.2 22.5 %reduce-scatter.4.cloned.1.call-done = f32[160,20]{1,0:T(8,128)} async-done(((f32[640,20]{1,0:T(8,128)}), f32[160,20]{1,0:T(8,128)}) %reduce-scatter.4.cloned.1.call-update) | async-done | bytes 12816
  476.7 1.0 reshape.247
  477.7 0.2 fusion.41
  478.0 0.7 copy.43
  478.7 0.7 copy.44
  (30 shorter events, 0.3 us)
Async XLA Ops:
  7.2 42.8 %copy-start = (bf16[384,100,10]{0,1,2:T(8,128)(2,1)S(1)}, bf16[384,100,10]{0,1,2:T(8,128)(2,1)}, u32[]{:S(2)}) copy-start(bf16[384,100,10]{0,1,2:T(8,128)(2,1)} %param.13) | copy-start | bytes 2304004
  20.8 12.6 %copy-start.4 = (f32[2,10,160]{2,0,1:T(2,128)S(1)}, f32[2,10,160]{2,0,1:T(2,128)}, u32[]{:S(2)}) copy-start(f32[2,10,160]{2,0,1:T(2,128)} %param.10) | copy-start | bytes 38404
  20.8 12.7 %copy-start.6 = (s32[2,2]{1,0:T(2,128)S(1)}, s32[2,2]{1,0:T(2,128)}, u32[]{:S(2)}) copy-start(s32[2,2]{1,0:T(2,128)} %param.19) | copy-start | bytes 52
  20.8 12.9 %copy-start.1 = (s32[100]{0:T(128)S(1)}, s32[100]{0:T(128)}, u32[]{:S(2)}) copy-start(s32[100]{0:T(128)} %param.17) | copy-start | bytes 1204
  20.8 14.2 %copy-start.5 = (s32[640]{0:T(1024)S(1)}, s32[640]{0:T(1024)}, u32[]{:S(2)}) copy-start(s32[640]{0:T(1024)} %param.16) | copy-start | bytes 7684
  20.8 192.4 %all-to-all-start = ((bf16[384,10,640]{2,1,0:T(8,128)(2,1)}), bf16[384,10,640]{2,1,0:T(8,128)(2,1)}, u32[]{:S(2)}, u32[]{:S(2)}) async-start(bf16[384,10,640]{2,1,0:T(8,128)(2,1)} %compare_select_fusion), calls=%async_computation | async-start | bytes 15728640 | tf_op jit(solution)/shard_map/all_to_all | solution.py:74
  33.3 104.6 %all-gather.3.cloned.1.call-start = ((), (), s32[]{:S(2)}) async-start(), calls=%async_computation.2 | async-start | bytes 1664000 | tf_op jit(solution)/shard_map/all_gather | solution.py:45
  49.1 213.7 %all-gather.5.cloned.1.call-start = ((), (), s32[]{:S(2)}) async-start(), calls=%async_computation.3 | async-start | bytes 1996800 | tf_op jit(solution)/shard_map/all_gather | solution.py:67
  57.6 393.1 %all-reduce.3.cloned.1.call-start = ((), (), s32[]{:S(2)}) async-start(), calls=%async_computation.5 | async-start | bytes 6553600
  255.0 4.4 copy-start.2
  255.1 5.6 %copy-start.3 = (bf16[384,4,10]{0,1,2:T(4,128)(2,1)S(1)}, bf16[384,4,10]{0,1,2:T(4,128)(2,1)}, u32[]{:S(2)}) copy-start(bf16[384,4,10]{0,1,2:T(4,128)(2,1)} %fusion.37) | copy-start | bytes 92164
  255.1 6.4 %copy-start.7 = (u32[256]{0:T(256)S(1)}, u32[256]{0:T(256)}, u32[]{:S(2)}) copy-start(u32[256]{0:T(256)} %constant.49) | copy-start | bytes 3076
  259.4 217.3 %reduce-scatter.4.cloned.1.call-start = ((), (), s32[]{:S(2)}) async-start(), calls=%async_computation.4 | async-start | bytes 409600
Sparse Core Ops, SparseCore 0:
  49.2 88.6 all-gather.2
  140.5 88.1 all-gather.4
  259.5 191.2 all-reduce.2
  453.5 23.1 reduce-scatter.3
where the time goes:
time: 489 us; the launch traced here: 486 us
  waiting for transfers between devices  335 us (69%)
  local copies, waits for them, and re-layouts  58.4 us (12%)
  matrix products  37.6 us (8%)
  other arithmetic  15 us (3%)
  between operations  14.6 us (3%)
  blocking collectives  12.9 us (3%)
  starting transfers between devices  12.6 us (3%)
    unnamed x6, waiting for transfers between devices  185 us
    all_gather x1, waiting for transfers between devices, per_device(): amp_whole = lax.all_gather(amp_rows, 'blk', axis=1, tiled=True)  80.2 us
    all_to_all x1, waiting for transfers between devices, per_device(): lax.all_to_all(chol_masked, 'blk', split_axis=0, concat_axis=1, tiled=True)  69.7 us
    dot_general x2, matrix products, ladder_pair(): jnp.einsum('qad,qbd->ab', halfway, chol_block, preferred_element_type=jnp...  31.9 us
    slice x1, local copies, waits for them, and re-layouts, per_device(): dressed_all[:, 1::2, :]  25.7 us
    all_gather x1, blocking collectives, per_device(): lax.all_gather(amp_local.astype(jnp.bfloat16), 'rep', axis=2, tiled=True)  12.9 us
    all_to_all x1, starting transfers between devices, per_device(): lax.all_to_all(chol_masked, 'blk', split_axis=0, concat_axis=1, tiled=True)  12.5 us
    select_n x1, other arithmetic, per_device(): chol_masked = jnp.where(vv_mask, chol_vv, jnp.zeros((), chol_vv.dtype))  11.2 us
  transfers between devices with their start and end apart: 5, of which 4 were waited for; matrix products, arithmetic and copies ran while one was open for 19% of the time, Pallas kernels for 0%

commit v1 on v0

v1 whole, which is shorter than its diff:
```python
import jax
import jax.numpy as jnp
from jax import lax
from jax.experimental import pallas as pl
from jax.experimental.pallas import tpu as pltpu
from jax.sharding import PartitionSpec as P

BF = jnp.bfloat16
F32 = jnp.float32
I32 = jnp.int32
RUN = 160
MAIN = 128
STRIDE = 40
GROUPS = 3
REST = RUN - MAIN
CYCLE_LANE = GROUPS * STRIDE
LIMIT = 48 * 1024 * 1024
NT = (((1,), (1,)), ((), ()))


def dot(x, y):
    return jnp.dot(x, y, preferred_element_type=F32)


def pack_kernel(row_irrep, chol, q_irrep, vir_irrep, pos_col, ov, out, fold):
    step = pl.program_id(0)
    vir_total = chol.shape[2]

    @pl.when(step == 0)
    def _():
        lane = lax.broadcasted_iota(I32, (vir_total, 2 * MAIN), 1)
        fold[...] = jnp.where(lane == pos_col[...], 1.0, 0.0).astype(BF)

    want = jnp.bitwise_xor(q_irrep[...], row_irrep[step])
    kept = jnp.where(want == vir_irrep[...], chol[0].astype(F32), 0.0).astype(BF)
    folded = dot(kept, fold[...])
    lane = lax.broadcasted_iota(I32, (8, MAIN), 1)
    slot = lax.broadcasted_iota(I32, (8, MAIN), 0)
    place = jnp.where(lane == slot + REST, 1.0, 0.0).astype(BF)
    rest = folded[:, MAIN:] + lax.dot_general(
        ov[0].astype(BF), place, (((0,), (0,)), ((), ())), preferred_element_type=F32
    )
    own = out.shape[2]
    for q in range(6):
        out[q, 0] = folded[q * own : (q + 1) * own, :MAIN].astype(BF)
    for u in range(2):
        total = rest[u * GROUPS * own : (u * GROUPS + 1) * own]
        for g in range(1, GROUPS):
            part = rest[(u * GROUPS + g) * own : (u * GROUPS + g + 1) * own]
            total = total + pltpu.roll(part, g * STRIDE, 1)
        out[6 + u, 0] = total.astype(BF)


def pair_kernel(
    q_irrep,
    pair_sym,
    got,
    row_irrep,
    col_irrep,
    row_pos,
    col_pos,
    single_rows,
    occ_lanes,
    out,
    ball,
    hall,
    amps,
    unfold,
    weight,
):
    vir_total = row_irrep.shape[0]
    single = single_rows[...].astype(BF)
    rest_amp = got[10].astype(F32)
    lane = lax.broadcasted_iota(I32, (vir_total, MAIN), 1)
    index = lax.broadcasted_iota(I32, (2 * MAIN, vir_total), 0)
    column = col_pos[...]
    for g in range(GROUPS):
        place = jnp.where(column < MAIN, column, column + g * STRIDE)
        unfold[g] = jnp.where(index == place, 1.0, 0.0).astype(BF)
        short = lax.dot_general(single, unfold[g], NT, preferred_element_type=F32)
        slot = lax.broadcasted_iota(I32, short.shape, 0)
        at = lax.broadcasted_iota(I32, short.shape, 1)
        short = short + jnp.where(
            (at == slot + MAIN + g * STRIDE + REST) & (slot < 4), 1.0, 0.0
        )
        row = lax.broadcasted_iota(I32, (MAIN, 2 * MAIN), 0)
        zero = jnp.zeros((MAIN, 2 * MAIN), F32)
        first = CYCLE_LANE
        weight[g, 0:MAIN] = jnp.where(
            row == first, short[1:2], jnp.where(row == first + 1, short[3:4], zero)
        ).astype(BF)
        weight[g, MAIN : 2 * MAIN] = jnp.where(row == first, short[0:1], zero).astype(BF)
        weight[g, 2 * MAIN :] = jnp.where(row == first + 1, short[2:3], zero).astype(BF)
        for p in range(2):
            amps[g, :, p * 256 : p * 256 + MAIN] = got[8 + p]
            shift = (g * STRIDE - p * 64) % MAIN
            moved = pltpu.roll(rest_amp, shift, 1) if shift else rest_amp
            inside = (lane >= g * STRIDE) & (lane < g * STRIDE + REST)
            amps[g, :, p * 256 + MAIN : (p + 1) * 256] = jnp.where(inside, moved, 0.0).astype(BF)

    def one(q, carry):
        u = q // GROUPS
        g = q % GROUPS
        bc = jnp.concatenate([got[q], got[6 + u]], axis=1)
        want = jnp.bitwise_xor(row_irrep[...], q_irrep[q])
        wide = dot(bc, unfold[g])
        wide = jnp.where(want == col_irrep[...], wide, 0.0).astype(BF)
        half = dot(wide, amps[g])
        dressed = lax.dot_general(bc, weight[g], NT, preferred_element_type=F32)
        dressed = jnp.where(want == occ_lanes[...], dressed, 0.0)
        ball[q, :, :MAIN] = bc[:, :MAIN]
        ball[q, :, MAIN:] = (bc[:, MAIN:].astype(F32) + dressed[:, :MAIN]).astype(BF)
        for p in range(2):
            hall[p, q, :, :MAIN] = half[:, p * 256 : p * 256 + MAIN].astype(BF)
            hall[p, q, :, MAIN:] = (
                half[:, p * 256 + MAIN : (p + 1) * 256]
                + dressed[:, (p + 1) * MAIN : (p + 2) * MAIN]
            ).astype(BF)
        return carry

    lax.fori_loop(0, 6, one, 0)

    lane2 = lax.broadcasted_iota(I32, (vir_total, 2 * MAIN), 1)
    rest = None
    for p in range(2):
        value = lax.dot_general(hall[p, 0], ball[0], NT, preferred_element_type=F32)
        for q in range(1, 6):
            value = value + lax.dot_general(
                hall[p, q], ball[q], NT, preferred_element_type=F32
            )
        want = jnp.bitwise_xor(row_irrep[...], pair_sym[p])
        value = jnp.where(want == col_irrep[...], value, 0.0).astype(BF)
        place = row_pos[...]
        place = jnp.where(place < MAIN, place, place + p * 64)
        fold = jnp.where(lane2 == place, 1.0, 0.0).astype(BF)
        short = dot(value, fold)
        out[p] = short[:, :MAIN].astype(BF)
        rest = short[:, MAIN:] if rest is None else rest + short[:, MAIN:]
    out[2] = rest.astype(BF)


def over_rep(value):
    total = value
    for k in (1, 2, 3):
        total = total + lax.ppermute(value, "rep", [(i, (i + k) % 4) for i in range(4)])
    return total


def per_device(
    amplitudes,
    singles,
    chol_vv,
    chol_ov,
    occ_energy,
    vir_energy,
    vir_irrep,
    occ_irrep,
    chol_irrep,
    pair_list,
):
    blk_pos = lax.axis_index("blk")
    rep_pos = lax.axis_index("rep")
    q_local, row_count, vir_total = chol_vv.shape
    col_count = amplitudes.shape[2]
    blk_count = vir_total // row_count
    q_own = q_local // blk_count
    starts = jnp.sum(
        (vir_irrep[None, :] < jnp.arange(8, dtype=I32)[:, None]).astype(I32), axis=1
    )
    vir_pos = jnp.arange(vir_total, dtype=I32) - jnp.sum(
        jnp.where(vir_irrep[:, None] == jnp.arange(8, dtype=I32)[None, :], starts[None, :], 0),
        axis=1,
    )
    row_irrep = lax.dynamic_slice_in_dim(vir_irrep, blk_pos * row_count, row_count)
    col_irrep = lax.dynamic_slice_in_dim(vir_irrep, rep_pos * col_count, col_count)
    col_pos = lax.dynamic_slice_in_dim(vir_pos, rep_pos * col_count, col_count)
    q_irrep = lax.dynamic_slice_in_dim(chol_irrep, rep_pos * q_local, q_local)
    row_energy = lax.dynamic_slice_in_dim(vir_energy, blk_pos * row_count, row_count)
    col_energy = lax.dynamic_slice_in_dim(vir_energy, rep_pos * col_count, col_count)
    pair_first = pair_list[:, 0]
    pair_second = pair_list[:, 1]
    pair_sym = jnp.bitwise_xor(occ_irrep[pair_first], occ_irrep[pair_second])
    occ_rows = pair_list.reshape(-1)
    occ_labels = occ_irrep[occ_rows]

    amp_mask = (
        jnp.bitwise_xor(row_irrep[None, :, None], col_irrep[None, None, :])
        == pair_sym[:, None, None]
    )
    amp_local = jnp.where(amp_mask, amplitudes, jnp.zeros((), amplitudes.dtype))
    lanes = jnp.arange(2 * MAIN, dtype=I32)
    fold_cols = (col_pos[:, None] == lanes[None, :]).astype(BF)
    amp_short = jnp.einsum(
        "prc,cj->prj", amp_local.astype(BF), fold_cols, preferred_element_type=F32
    )
    amp_rest = jnp.concatenate(
        [
            amp_short[0, :, MAIN : MAIN + 64],
            amp_short[1, :, MAIN : MAIN + 64],
        ],
        axis=1,
    )
    amp_send = jnp.concatenate([amp_short[:, :, :MAIN], amp_rest[None]], axis=0)
    amp_send = over_rep(amp_send.reshape(3 * row_count, MAIN)).astype(BF)

    ov_rows = jnp.take(chol_ov, occ_rows, axis=1).astype(F32)
    ov_mask = (
        jnp.bitwise_xor(occ_labels[None, :, None], row_irrep[None, None, :])
        == q_irrep[:, None, None]
    )
    ov_rows = jnp.where(ov_mask, ov_rows, 0.0).transpose(2, 1, 0)
    ov_rows = jnp.pad(ov_rows, ((0, 0), (0, 4), (0, 0)))
    packed = pl.pallas_call(
        pack_kernel,
        grid_spec=pltpu.PrefetchScalarGridSpec(
            num_scalar_prefetch=1,
            grid=(row_count,),
            in_specs=[
                pl.BlockSpec((1, q_local, vir_total), lambda i, s: (i, 0, 0)),
                pl.BlockSpec((q_local, 1), lambda i, s: (0, 0)),
                pl.BlockSpec((1, vir_total), lambda i, s: (0, 0)),
                pl.BlockSpec((vir_total, 1), lambda i, s: (0, 0)),
                pl.BlockSpec((1, 8, q_local), lambda i, s: (i, 0, 0)),
            ],
            out_specs=pl.BlockSpec((8, 1, blk_count, MAIN), lambda i, s: (0, i, 0, 0)),
            scratch_shapes=[pltpu.VMEM((vir_total, 2 * MAIN), BF)],
        ),
        out_shape=jax.ShapeDtypeStruct((8, row_count, blk_count, MAIN), BF),
        compiler_params=pltpu.CompilerParams(vmem_limit_bytes=LIMIT),
        name="pack",
    )(
        row_irrep,
        chol_vv.transpose(1, 0, 2),
        q_irrep[:, None],
        vir_irrep[None, :],
        vir_pos[:, None],
        ov_rows,
    )
    packed = packed.reshape(8 * row_count, blk_count, MAIN).transpose(1, 0, 2)
    send = jnp.concatenate(
        [packed, jnp.broadcast_to(amp_send[None], (blk_count, 3 * row_count, MAIN))], axis=1
    )
    got = lax.all_to_all(send, "blk", split_axis=0, concat_axis=0, tiled=False)
    got = got.transpose(1, 0, 2).reshape(11, vir_total, MAIN)

    def mixed(x):
        return x.reshape(blk_count, row_count).T.reshape(vir_total)

    irrep_mixed = mixed(vir_irrep)
    pos_mixed = mixed(vir_pos)
    own_irrep = lax.dynamic_index_in_dim(
        q_irrep.reshape(q_own, blk_count), blk_pos, axis=1, keepdims=False
    )
    single_rows = jnp.where(
        occ_labels[:, None] == vir_irrep[None, :], singles[occ_rows], jnp.zeros((), singles.dtype)
    ).astype(F32)
    single_rows = single_rows.reshape(4, blk_count, row_count).transpose(0, 2, 1)
    single_rows = jnp.pad(single_rows.reshape(4, vir_total), ((0, 4), (0, 0)))
    first = CYCLE_LANE
    lane_row = jnp.arange(3 * MAIN, dtype=I32)
    occ_lanes = jnp.where(
        lane_row == first,
        occ_labels[1],
        jnp.where(
            lane_row == first + 1,
            occ_labels[3],
            jnp.where(lane_row == MAIN + first, occ_labels[0], occ_labels[2]),
        ),
    )[None, :]
    smem = pl.BlockSpec(memory_space=pltpu.SMEM)
    vmem = pl.BlockSpec(memory_space=pltpu.VMEM)
    part = pl.pallas_call(
        pair_kernel,
        in_specs=[smem, smem] + [vmem] * 7,
        out_specs=vmem,
        out_shape=jax.ShapeDtypeStruct((3, vir_total, MAIN), BF),
        scratch_shapes=[
            pltpu.VMEM((q_own, vir_total, 2 * MAIN), BF),
            pltpu.VMEM((2, q_own, vir_total, 2 * MAIN), BF),
            pltpu.VMEM((GROUPS, vir_total, 4 * MAIN), BF),
            pltpu.VMEM((GROUPS, 2 * MAIN, vir_total), BF),
            pltpu.VMEM((GROUPS, 3 * MAIN, 2 * MAIN), BF),
        ],
        compiler_params=pltpu.CompilerParams(vmem_limit_bytes=LIMIT),
        name="ladder",
    )(
        own_irrep,
        pair_sym,
        got,
        irrep_mixed[:, None],
        irrep_mixed[None, :],
        pos_mixed[:, None],
        pos_mixed[None, :],
        single_rows,
        occ_lanes,
    )
    part = part.reshape(3 * row_count, blk_count, MAIN).transpose(1, 0, 2)
    part = lax.all_to_all(part, "blk", split_axis=0, concat_axis=0, tiled=False)
    summed = over_rep(jnp.sum(part.astype(F32), axis=0))
    summed = summed.reshape(3, row_count, MAIN)
    short = jnp.stack(
        [
            jnp.concatenate([summed[p], summed[2, :, p * 64 : p * 64 + REST]], axis=1)
            for p in range(2)
        ]
    )
    spread = (jnp.arange(RUN, dtype=I32)[:, None] == col_pos[None, :]).astype(F32)
    total = jnp.einsum("prj,jc->prc", short, spread, precision=lax.Precision.HIGHEST)
    total = jnp.where(amp_mask, total, 0.0)
    denominator = (
        (occ_energy[pair_first] + occ_energy[pair_second])[:, None, None]
        - row_energy[None, :, None]
        - col_energy[None, None, :]
    )
    residual = total + denominator * amp_local
    updated = amp_local - residual / denominator
    return (residual, updated)


def solution(mesh):
    in_specs = (
        P(None, "blk", "rep"),
        P(),
        P("rep", "blk", None),
        P("rep", None, "blk"),
        P(),
        P(),
        P(),
        P(),
        P(),
        P(),
    )
    out_specs = (P(None, "blk", "rep"), P(None, "blk", "rep"))
    return jax.shard_map(
        per_device, mesh=mesh, in_specs=in_specs, out_specs=out_specs, check_vma=False
    )
```

time: 489 us -> 137 us (0.28)
  waiting for transfers between devices: 335 us -> 55.3 us
  local copies, waits for them, and re-layouts: 58.4 us -> 19.2 us
  matrix products: 37.6 us -> 1.12 us
  Pallas kernels: 0 us -> 23.5 us
  starting transfers between devices: 12.6 us -> 29.3 us
  between operations: 14.6 us -> 0.93 us
  blocking collectives: 12.9 us -> 0 us
  other arithmetic: 15 us -> 7.3 us
    unnamed x6 -> x0, waiting for transfers between devices: 185 us -> none
    all_gather x2 -> x0, waiting for transfers between devices: 80.2 us -> none  [the longest x1 80.2 us: per_device(): amp_whole = lax.all_gather(amp_rows, 'blk', axis=1, tiled=True)]
    dot_general x4 -> x2, matrix products: 37.6 us -> 1.12 us  [the longest x1 0.94 us: per_device(): jnp.einsum('prc,cj->prj', amp_local.astype(BF), fold_cols, preferred_elem...]
    slice x3, local copies, waits for them, and re-layouts: 31.3 us -> 0.68 us  [the longest x1 0.67 us: per_device(): occ_labels[1]]
    pallas_call x0 -> x2, Pallas kernels: none -> 23.5 us  [the longest x1 14.5 us: per_device(): pl.pallas_call(pair_kernel, in_specs=[smem, smem] + [vmem] * 7, out_specs...]
    all_to_all x1 -> x2, waiting for transfers between devices: 69.7 us -> 51.2 us  [the longest x1 36.5 us: per_device(): got = lax.all_to_all(send, 'blk', split_axis=0, concat_axis=0, tiled=False)]
    all_gather x1 -> x0, blocking collectives: 12.9 us -> none  [per_device(): lax.all_gather(amp_local.astype(jnp.bfloat16), 'rep', axis=2, tiled=True)]
    ppermute x0 -> x6, starting transfers between devices: none -> 8.71 us  [over_rep(): lax.ppermute(value, 'rep', [(i, (i + k) % 4) for i in range(4)])]
  transfers between devices with their start and end apart: 5 -> 8, of which waited for: 4 -> 4; matrix products, arithmetic and copies ran while one was open for 19% -> 11% of each run, Pallas kernels for 0% -> 7%
where the time goes in v1:
time: 137 us
  waiting for transfers between devices  55.3 us (40%)
  starting transfers between devices  29.3 us (21%)
  Pallas kernels  23.5 us (17%)
  local copies, waits for them, and re-layouts  19.2 us (14%)
  other arithmetic  7.3 us (5%)
    all_to_all x1, waiting for transfers between devices, per_device(): got = lax.all_to_all(send, 'blk', split_axis=0, concat_axis=0, tiled=False)  36.5 us
    all_to_all x1, waiting for transfers between devices, per_device(): part = lax.all_to_all(part, 'blk', split_axis=0, concat_axis=0, tiled=False)  14.7 us
    pallas_call x1, Pallas kernels, per_device(): pl.pallas_call(pair_kernel, in_specs=[smem, smem] + [vmem] * 7, out_specs...  14.5 us
    all_to_all x1, starting transfers between devices, per_device(): got = lax.all_to_all(send, 'blk', split_axis=0, concat_axis=0, tiled=False)  12.2 us
    pallas_call x1, Pallas kernels, per_device(): pl.pallas_call(pack_kernel, grid_spec=pltpu.PrefetchScalarGridSpec(num_sc...  8.93 us
    ppermute x6, starting transfers between devices, over_rep(): lax.ppermute(value, 'rep', [(i, (i + k) % 4) for i in range(4)])  8.71 us
    all_to_all x1, starting transfers between devices, per_device(): part = lax.all_to_all(part, 'blk', split_axis=0, concat_axis=0, tiled=False)  8.39 us
    ppermute x6, waiting for transfers between devices, over_rep(): lax.ppermute(value, 'rep', [(i, (i + k) % 4) for i in range(4)])  4.12 us
  transfers between devices with their start and end apart: 8, of which 4 were waited for; matrix products, arithmetic and copies ran while one was open for 11% of the time, Pallas kernels for 7%

profile of v1, /device:TPU:6, one launch (start us, length us, event | category | flops | bytes accessed | tf_op | source)
XLA Modules:
  0.0 136.5 jit_solution(2556290438475504389)
XLA Ops:
  0.7 1.0 fusion.19
  1.6 0.8 convert_reduce_fusion.1
  2.4 0.8 dynamic_slice.23
  3.2 0.8 dynamic_slice.22.row_irrep
  4.0 1.3 gather_fusion
  5.3 1.3 gather_fusion.1
  6.6 0.8 select_reduce_fusion
  7.5 0.9 fusion.4
  8.5 3.1 %collective-permute-start.2 = (f32[30,128]{1,0:T(8,128)S(1)}, f32[30,128]{1,0:T(8,128)S(1)}, u32[]{:S(2)}, u32[]{:S(2)}) collective-permute-start(f32[30,128]{1,0:T(8,128)S(1)} %reshape.243), channel_id=1, source_target_pairs={{0,3},{1,0},{2,1},{3,2},{4,7},{5,4},{6,5},{7,6},{8,11},{9,8},{10,9... | collective-permute-start | bytes 46088 | tf_op jit(solution)/shard_map/ppermute | solution.py:145
  11.6 0.6 collective-permute-start.1
  12.3 1.0 collective-permute-start
  13.2 0.8 reshape.240
  14.0 0.8 reshape.241
  14.8 1.3 gather_fusion.2
  16.1 0.7 gather_fusion.3
  16.8 0.8 dynamic_slice.24
  17.7 0.1 reshape_subtract_fusion.pos_col
  18.0 8.9 %pack.1 = bf16[8,10,64,128]{3,2,1,0:T(8,128)(2,1)S(1)} custom-call(s32[10]{0:T(128)S(1)} %dynamic_slice.22.row_irrep, bf16[10,384,640]{2,1,0:T(8,128)(2,1)} %bitcast.51, s32[384,1]{1,0:T(8,128)S(1)} %broadcast_in_dim.109.q_irrep, s32[1,640]{1,0:T(1,128)S(1)} %broadcast_in_dim.60.vir_irrep, s32[640,1]{1,0:T(8,128)S(1)} %reshape_subtract_fusion.pos_col, ...), custom_call_target="tpu_custom_call" | custom-call | tf_op jit(solution)/shard_map/pack/pallas_call | solution.py:213
  27.0 0.8 copy.80
  27.9 1.4 %pad_maximum_fusion = bf16[64,110,128]{2,1,0:T(8,128)(2,1)} fusion(bf16[64,30,128]{2,1,0:T(8,128)(2,1)S(1)} %broadcast_in_dim.103, bf16[64,80,128]{2,1,0:T(8,128)(2,1)S(1)} %bitcast.50), kind=kLoop, calls=%fused_computation.7 | loop fusion | flops 3604480 | bytes 3604480 | tf_op jit(solution)/shard_map/concatenate | solution.py:240
  29.3 12.2 %all-to-all-start = ((bf16[64,110,128]{2,1,0:T(8,128)(2,1)}), bf16[64,110,128]{2,1,0:T(8,128)(2,1)S(1)}, u32[]{:S(2)}, u32[]{:S(2)}) async-start(bf16[64,110,128]{2,1,0:T(8,128)(2,1)} %pad_maximum_fusion), calls=%async_computation | async-start | bytes 3670016 | tf_op jit(solution)/shard_map/all_to_all | solution.py:243
  41.6 0.1 reshape.245
  41.8 0.3 broadcast_in_dim_reshape.16.row_irrep
  42.2 0.1 reduce_sum.34
  42.4 0.3 broadcast_in_dim_reshape.17.row_pos
  42.8 1.5 %gather_fusion.4 = bf16[4,640]{1,0:T(4,128)(2,1)S(1)} fusion(bf16[100,640]{1,0:T(8,128)(2,1)} %param.11, s32[1024]{0:T(1024)S(1)} %pad_clamp_fusion), kind=kCustom, calls=%fused_computation.4 | custom fusion | bytes 10256 | tf_op jit(solution)/shard_map/gather | solution.py:255
  44.3 0.2 gather.29
  44.7 0.2 dynamic-slice_reduce_fusion.q_irrep
  44.9 0.7 fusion.24
  45.6 2.5 %compare_select_fusion.4.occ_lanes = s32[1,384]{1,0:T(1,128)S(1)} fusion(s32[]{:T(128)} %bitcast.17, s32[]{:T(128)} %bitcast.16, s32[]{:T(128)} %bitcast.15, s32[]{:T(128)} %bitcast.14), kind=kLoop, calls=%fused_computation.54 | loop fusion | flops 2304 | bytes 1552 | tf_op jit(solution)/shard_map/jit(_where)/select_n | solution.py:261
  48.1 36.5 %all-to-all-done = bf16[64,110,128]{2,1,0:T(8,128)(2,1)S(1)} async-done(((bf16[64,110,128]{2,1,0:T(8,128)(2,1)}), bf16[64,110,128]{2,1,0:T(8,128)(2,1)S(1)}, u32[]{:S(2)}, u32[]{:S(2)}) %all-to-all-start) | async-done | bytes 1802272 | tf_op jit(solution)/shard_map/all_to_all | solution.py:243
  84.6 0.5 copy.59
  85.1 14.5 %ladder.1 = bf16[3,640,128]{2,1,0:T(8,128)(2,1)S(1)} custom-call(s32[6]{0:T(128)S(1)} %dynamic-slice_reduce_fusion.q_irrep, s32[2]{0:T(128)S(1)} %xor.43.pair_sym, bf16[11,640,128]{2,1,0:T(8,128)(2,1)S(1)} %bitcast.46, s32[640,1]{1,0:T(8,128)S(1)} %broadcast_in_dim_reshape.16.row_irrep, s32[1,640]{1,0:T(1,128)S(1)} %broadcast_in_dim_reshape.13.col_irrep, ...), custom_call_target="tpu_custom_call" | custom-call | tf_op jit(solution)/shard_map/ladder/pallas_call | solution.py:272
  99.6 1.1 copy.81
  100.8 8.4 %all-to-all-start.1 = ((bf16[64,30,128]{2,1,0:T(8,128)(2,1)}), bf16[64,30,128]{2,1,0:T(8,128)(2,1)S(1)}, u32[]{:S(2)}, u32[]{:S(2)}) async-start(bf16[64,30,128]{2,1,0:T(8,128)(2,1)} %bitcast.45), calls=%async_computation.1 | async-start | bytes 1048576 | tf_op jit(solution)/shard_map/all_to_all | solution.py:298
  109.2 0.6 gather_fusion.5
  109.8 0.6 gather_fusion.6
  110.4 0.8 dynamic_slice.27
  111.2 14.7 %all-to-all-done.1 = bf16[64,30,128]{2,1,0:T(8,128)(2,1)S(1)} async-done(((bf16[64,30,128]{2,1,0:T(8,128)(2,1)}), bf16[64,30,128]{2,1,0:T(8,128)(2,1)S(1)}, u32[]{:S(2)}, u32[]{:S(2)}) %all-to-all-start.1) | async-done | bytes 491552 | tf_op jit(solution)/shard_map/all_to_all | solution.py:298
  125.9 0.1 convert_reduce_fusion
  126.0 2.3 %collective-permute-start.5 = (f32[30,128]{1,0:T(8,128)S(1)}, f32[30,128]{1,0:T(8,128)S(1)}, u32[]{:S(2)}, u32[]{:S(2)}) collective-permute-start(f32[30,128]{1,0:T(8,128)S(1)} %convert_reduce_fusion), channel_id=1, source_target_pairs={{0,3},{1,0},{2,1},{3,2},{4,7},{5,4},{6,5},{7,6},{8,11},{9,8},{10,9... | collective-permute-start | bytes 46088 | tf_op jit(solution)/shard_map/ppermute | solution.py:145
  128.3 1.7 %collective-permute-start.4 = (f32[30,128]{1,0:T(8,128)S(1)}, f32[30,128]{1,0:T(8,128)S(1)}, u32[]{:S(2)}, u32[]{:S(2)}) collective-permute-start(f32[30,128]{1,0:T(8,128)S(1)} %convert_reduce_fusion), channel_id=1, source_target_pairs={{0,2},{1,3},{2,0},{3,1},{4,6},{5,7},{6,4},{7,5},{8,10},{9,11},{10,... | collective-permute-start | bytes 46088 | tf_op jit(solution)/shard_map/ppermute | solution.py:145
  130.1 0.8 dynamic_slice.28
  130.8 2.7 %collective-permute-done.4 = f32[30,128]{1,0:T(8,128)S(1)} collective-permute-done((f32[30,128]{1,0:T(8,128)S(1)}, f32[30,128]{1,0:T(8,128)S(1)}, u32[]{:S(2)}, u32[]{:S(2)}) %collective-permute-start.4) | collective-permute-done | bytes 15392 | tf_op jit(solution)/shard_map/ppermute | solution.py:145
  133.5 1.4 %collective-permute-done.3 = f32[30,128]{1,0:T(8,128)S(1)} collective-permute-done((f32[30,128]{1,0:T(8,128)S(1)}, f32[30,128]{1,0:T(8,128)S(1)}, u32[]{:S(2)}, u32[]{:S(2)}) %collective-permute-start.3) | collective-permute-done | bytes 15392 | tf_op jit(solution)/shard_map/ppermute | solution.py:145
  135.1 0.2 fusion.9
  135.3 0.6 copy.68
  135.9 0.6 copy.69
  (51 shorter events, 1.5 us)
Async XLA Ops:
  0.6 15.4 %copy-start = (bf16[384,100,10]{0,1,2:T(8,128)(2,1)S(1)}, bf16[384,100,10]{0,1,2:T(8,128)(2,1)}, u32[]{:S(2)}) copy-start(bf16[384,100,10]{0,1,2:T(8,128)(2,1)} %param.13) | copy-start | bytes 2304004
  8.5 19.3 %collective-permute-start.2 = (f32[30,128]{1,0:T(8,128)S(1)}, f32[30,128]{1,0:T(8,128)S(1)}, u32[]{:S(2)}, u32[]{:S(2)}) collective-permute-start(f32[30,128]{1,0:T(8,128)S(1)} %reshape.243), channel_id=1, source_target_pairs={{0,3},{1,0},{2,1},{3,2},{4,7},{5,4},{6,5},{7,6},{8,11},{9,8},{10,9... | collective-permute-start | bytes 46088 | tf_op jit(solution)/shard_map/ppermute | solution.py:145
  11.6 16.2 %collective-permute-start.1 = (f32[30,128]{1,0:T(8,128)S(1)}, f32[30,128]{1,0:T(8,128)S(1)}, u32[]{:S(2)}, u32[]{:S(2)}) collective-permute-start(f32[30,128]{1,0:T(8,128)S(1)} %reshape.243), channel_id=1, source_target_pairs={{0,2},{1,3},{2,0},{3,1},{4,6},{5,7},{6,4},{7,5},{8,10},{9,11},{10,... | collective-permute-start | bytes 46088 | tf_op jit(solution)/shard_map/ppermute | solution.py:145
  12.3 15.6 %collective-permute-start = (f32[30,128]{1,0:T(8,128)S(1)}, f32[30,128]{1,0:T(8,128)S(1)}, u32[]{:S(2)}, u32[]{:S(2)}) collective-permute-start(f32[30,128]{1,0:T(8,128)S(1)} %reshape.243), channel_id=1, source_target_pairs={{0,1},{1,2},{2,3},{3,0},{4,5},{5,6},{6,7},{7,4},{8,9},{9,10},{10,1... | collective-permute-start | bytes 46088 | tf_op jit(solution)/shard_map/ppermute | solution.py:145
  16.1 1.9 %copy-start.2 = (s32[640]{0:T(1024)S(1)}, s32[640]{0:T(1024)}, u32[]{:S(2)}) copy-start(s32[640]{0:T(1024)} %param.16) | copy-start | bytes 7684
  29.3 55.3 %all-to-all-start = ((bf16[64,110,128]{2,1,0:T(8,128)(2,1)}), bf16[64,110,128]{2,1,0:T(8,128)(2,1)S(1)}, u32[]{:S(2)}, u32[]{:S(2)}) async-start(bf16[64,110,128]{2,1,0:T(8,128)(2,1)} %pad_maximum_fusion), calls=%async_computation | async-start | bytes 3670016 | tf_op jit(solution)/shard_map/all_to_all | solution.py:243
  85.1 24.1 %copy-start.1 = (f32[100]{0:T(128)S(1)}, f32[100]{0:T(128)}, u32[]{:S(2)}) copy-start(f32[100]{0:T(128)} %param.14) | copy-start | bytes 1204
  99.6 35.4 %copy-start.3 = (f32[2,10,160]{2,0,1:T(2,128)S(1)}, f32[2,10,160]{2,0,1:T(2,128)}, u32[]{:S(2)}) copy-start(f32[2,10,160]{2,0,1:T(2,128)} %param.10) | copy-start | bytes 38404
  100.8 25.1 %all-to-all-start.1 = ((bf16[64,30,128]{2,1,0:T(8,128)(2,1)}), bf16[64,30,128]{2,1,0:T(8,128)(2,1)S(1)}, u32[]{:S(2)}, u32[]{:S(2)}) async-start(bf16[64,30,128]{2,1,0:T(8,128)(2,1)} %bitcast.45), calls=%async_computation.1 | async-start | bytes 1048576 | tf_op jit(solution)/shard_map/all_to_all | solution.py:298
  126.0 4.9 %collective-permute-start.5 = (f32[30,128]{1,0:T(8,128)S(1)}, f32[30,128]{1,0:T(8,128)S(1)}, u32[]{:S(2)}, u32[]{:S(2)}) collective-permute-start(f32[30,128]{1,0:T(8,128)S(1)} %convert_reduce_fusion), channel_id=1, source_target_pairs={{0,3},{1,0},{2,1},{3,2},{4,7},{5,4},{6,5},{7,6},{8,11},{9,8},{10,9... | collective-permute-start | bytes 46088 | tf_op jit(solution)/shard_map/ppermute | solution.py:145
  128.3 5.2 %collective-permute-start.4 = (f32[30,128]{1,0:T(8,128)S(1)}, f32[30,128]{1,0:T(8,128)S(1)}, u32[]{:S(2)}, u32[]{:S(2)}) collective-permute-start(f32[30,128]{1,0:T(8,128)S(1)} %convert_reduce_fusion), channel_id=1, source_target_pairs={{0,2},{1,3},{2,0},{3,1},{4,6},{5,7},{6,4},{7,5},{8,10},{9,11},{10,... | collective-permute-start | bytes 46088 | tf_op jit(solution)/shard_map/ppermute | solution.py:145
  130.0 4.9 %collective-permute-start.3 = (f32[30,128]{1,0:T(8,128)S(1)}, f32[30,128]{1,0:T(8,128)S(1)}, u32[]{:S(2)}, u32[]{:S(2)}) collective-permute-start(f32[30,128]{1,0:T(8,128)S(1)} %convert_reduce_fusion), channel_id=1, source_target_pairs={{0,1},{1,2},{2,3},{3,0},{4,5},{5,6},{6,7},{7,4},{8,9},{9,10},{10,1... | collective-permute-start | bytes 46088 | tf_op jit(solution)/shard_map/ppermute | solution.py:145

commit v2 on v1

--- a/solution.py
+++ b/solution.py
@@ -22,24 +22,47 @@
     return jnp.dot(x, y, preferred_element_type=F32)
 
 
-def pack_kernel(row_irrep, chol, q_irrep, vir_irrep, pos_col, ov, out, fold):
+def run_positions(irrep):
+    place = lax.broadcasted_iota(I32, irrep.shape, 1)
+    for label in range(7):
+        count = jnp.sum(jnp.where(irrep == label, 1.0, 0.0), axis=1, keepdims=True)
+        place = place - jnp.where(irrep > label, count.astype(I32), 0)
+    return place
+
+
+def pack_kernel(vir_s, occ_s, pair_s, chol, ov, vir_irrep, chol_irrep, out, fold, labels, pick):
     step = pl.program_id(0)
-    vir_total = chol.shape[2]
+    q_local, vir_total = chol.shape[1:]
+    occ_total = ov.shape[1]
 
     @pl.when(step == 0)
     def _():
-        lane = lax.broadcasted_iota(I32, (vir_total, 2 * MAIN), 1)
-        fold[...] = jnp.where(lane == pos_col[...], 1.0, 0.0).astype(BF)
-
-    want = jnp.bitwise_xor(q_irrep[...], row_irrep[step])
-    kept = jnp.where(want == vir_irrep[...], chol[0].astype(F32), 0.0).astype(BF)
+        place = run_positions(vir_irrep[...])
+        row = lax.broadcasted_iota(I32, (2 * MAIN, vir_total), 0)
+        fold[...] = jnp.where(row == place, 1.0, 0.0).T.astype(BF)
+        first = pl.multiple_of(lax.axis_index("rep") * q_local, MAIN)
+        mine = chol_irrep[:, pl.ds(first, q_local)].astype(F32)
+        labels[...] = jnp.broadcast_to(mine, (MAIN, q_local)).T.astype(I32)
+        row = lax.broadcasted_iota(I32, (occ_total, MAIN), 0)
+        lane = lax.broadcasted_iota(I32, (occ_total, MAIN), 1)
+        taken = jnp.zeros((occ_total, MAIN), F32)
+        for m in range(4):
+            hit = (row == pair_s[m // 2, m % 2]) & (lane == REST + m)
+            taken = jnp.where(hit, 1.0, taken)
+        pick[...] = taken.astype(BF)
+
+    row_irrep = vir_s[lax.axis_index("blk") * pl.num_programs(0) + step]
+    want = jnp.bitwise_xor(labels[...], row_irrep)
+    kept = jnp.where(want[:, :1] == vir_irrep[...], chol[0].astype(F32), 0.0).astype(BF)
     folded = dot(kept, fold[...])
-    lane = lax.broadcasted_iota(I32, (8, MAIN), 1)
-    slot = lax.broadcasted_iota(I32, (8, MAIN), 0)
-    place = jnp.where(lane == slot + REST, 1.0, 0.0).astype(BF)
-    rest = folded[:, MAIN:] + lax.dot_general(
-        ov[0].astype(BF), place, (((0,), (0,)), ((), ())), preferred_element_type=F32
-    )
+    lane = lax.broadcasted_iota(I32, (1, MAIN), 1)
+    occ_label = jnp.zeros((1, MAIN), I32)
+    for m in range(4):
+        occ_label = jnp.where(lane == REST + m, occ_s[pair_s[m // 2, m % 2]], occ_label)
+    extra = lax.dot_general(
+        ov[0], pick[...], (((0,), (0,)), ((), ())), preferred_element_type=F32
+    )
+    rest = folded[:, MAIN:] + jnp.where(want == occ_label, extra, 0.0)
     own = out.shape[2]
     for q in range(6):
         out[q, 0] = folded[q * own : (q + 1) * own, :MAIN].astype(BF)
@@ -55,6 +78,7 @@
     q_irrep,
     pair_sym,
     got,
+    amp,
     row_irrep,
     col_irrep,
     row_pos,
@@ -70,7 +94,7 @@
 ):
     vir_total = row_irrep.shape[0]
     single = single_rows[...].astype(BF)
-    rest_amp = got[10].astype(F32)
+    rest_amp = amp[2].astype(F32)
     lane = lax.broadcasted_iota(I32, (vir_total, MAIN), 1)
     index = lax.broadcasted_iota(I32, (2 * MAIN, vir_total), 0)
     column = col_pos[...]
@@ -92,7 +116,7 @@
         weight[g, MAIN : 2 * MAIN] = jnp.where(row == first, short[0:1], zero).astype(BF)
         weight[g, 2 * MAIN :] = jnp.where(row == first + 1, short[2:3], zero).astype(BF)
         for p in range(2):
-            amps[g, :, p * 256 : p * 256 + MAIN] = got[8 + p]
+            amps[g, :, p * 256 : p * 256 + MAIN] = amp[p]
             shift = (g * STRIDE - p * 64) % MAIN
             moved = pltpu.roll(rest_amp, shift, 1) if shift else rest_amp
             inside = (lane >= g * STRIDE) & (lane < g * STRIDE + REST)
@@ -146,6 +170,25 @@
     return total
 
 
+def gather_blk(value, blk_pos, blk_count):
+    held = value[None]
+    for low in range(0, 6, 2):
+        came = [held] + [
+            lax.ppermute(held, "blk", [(i, i ^ (k << low)) for i in range(blk_count)])
+            for k in (1, 2, 3)
+        ]
+        mine = (blk_pos >> low) & 3
+        one = (mine & 1) == 1
+        two = (mine & 2) == 2
+        parts = []
+        for k in range(4):
+            near = jnp.where(one, came[k ^ 1], came[k])
+            far = jnp.where(one, came[k ^ 3], came[k ^ 2])
+            parts.append(jnp.where(two, far, near))
+        held = jnp.concatenate(parts, axis=0)
+    return held
+
+
 def per_device(
     amplitudes,
     singles,
@@ -164,6 +207,7 @@
     col_count = amplitudes.shape[2]
     blk_count = vir_total // row_count
     q_own = q_local // blk_count
+    occ_total = chol_ov.shape[1]
     starts = jnp.sum(
         (vir_irrep[None, :] < jnp.arange(8, dtype=I32)[:, None]).astype(I32), axis=1
     )
@@ -183,6 +227,41 @@
     occ_rows = pair_list.reshape(-1)
     occ_labels = occ_irrep[occ_rows]
 
+    packed = pl.pallas_call(
+        pack_kernel,
+        grid_spec=pltpu.PrefetchScalarGridSpec(
+            num_scalar_prefetch=3,
+            grid=(row_count,),
+            in_specs=[
+                pl.BlockSpec((1, q_local, vir_total), lambda i, *s: (i, 0, 0)),
+                pl.BlockSpec((1, occ_total, q_local), lambda i, *s: (i, 0, 0)),
+                pl.BlockSpec((1, vir_total), lambda i, *s: (0, 0)),
+                pl.BlockSpec((1, chol_irrep.shape[0]), lambda i, *s: (0, 0)),
+            ],
+            out_specs=pl.BlockSpec((8, 1, blk_count, MAIN), lambda i, *s: (0, i, 0, 0)),
+            scratch_shapes=[
+                pltpu.VMEM((vir_total, 2 * MAIN), BF),
+                pltpu.VMEM((q_local, MAIN), I32),
+                pltpu.VMEM((occ_total, MAIN), BF),
+            ],
+        ),
+        out_shape=jax.ShapeDtypeStruct((8, row_count, blk_count, MAIN), BF),
+        compiler_params=pltpu.CompilerParams(vmem_limit_bytes=LIMIT),
+        name="pack",
+    )(
+        vir_irrep,
+        occ_irrep,
+        pair_list,
+        chol_vv.transpose(1, 0, 2),
+        chol_ov.transpose(2, 1, 0),
+        vir_irrep[None, :],
+        chol_irrep[None, :],
+    )
+    packed = packed.reshape(8 * row_count, blk_count, MAIN).transpose(1, 0, 2)
+    packed, amplitudes = lax.optimization_barrier((packed, amplitudes))
+    got = lax.all_to_all(packed, "blk", split_axis=0, concat_axis=0, tiled=False)
+    got = got.transpose(1, 0, 2).reshape(8, vir_total, MAIN)
+
     amp_mask = (
         jnp.bitwise_xor(row_irrep[None, :, None], col_irrep[None, None, :])
         == pair_sym[:, None, None]
@@ -202,46 +281,8 @@
     )
     amp_send = jnp.concatenate([amp_short[:, :, :MAIN], amp_rest[None]], axis=0)
     amp_send = over_rep(amp_send.reshape(3 * row_count, MAIN)).astype(BF)
-
-    ov_rows = jnp.take(chol_ov, occ_rows, axis=1).astype(F32)
-    ov_mask = (
-        jnp.bitwise_xor(occ_labels[None, :, None], row_irrep[None, None, :])
-        == q_irrep[:, None, None]
-    )
-    ov_rows = jnp.where(ov_mask, ov_rows, 0.0).transpose(2, 1, 0)
-    ov_rows = jnp.pad(ov_rows, ((0, 0), (0, 4), (0, 0)))
-    packed = pl.pallas_call(
-        pack_kernel,
-        grid_spec=pltpu.PrefetchScalarGridSpec(
-            num_scalar_prefetch=1,
-            grid=(row_count,),
-            in_specs=[
-                pl.BlockSpec((1, q_local, vir_total), lambda i, s: (i, 0, 0)),
-                pl.BlockSpec((q_local, 1), lambda i, s: (0, 0)),
-                pl.BlockSpec((1, vir_total), lambda i, s: (0, 0)),
-                pl.BlockSpec((vir_total, 1), lambda i, s: (0, 0)),
-                pl.BlockSpec((1, 8, q_local), lambda i, s: (i, 0, 0)),
-            ],
-            out_specs=pl.BlockSpec((8, 1, blk_count, MAIN), lambda i, s: (0, i, 0, 0)),
-            scratch_shapes=[pltpu.VMEM((vir_total, 2 * MAIN), BF)],
-        ),
-        out_shape=jax.ShapeDtypeStruct((8, row_count, blk_count, MAIN), BF),
-        compiler_params=pltpu.CompilerParams(vmem_limit_bytes=LIMIT),
-        name="pack",
-    )(
-        row_irrep,
-        chol_vv.transpose(1, 0, 2),
-        q_irrep[:, None],
-        vir_irrep[None, :],
-        vir_pos[:, None],
-        ov_rows,
-    )
-    packed = packed.reshape(8 * row_count, blk_count, MAIN).transpose(1, 0, 2)
-    send = jnp.concatenate(
-        [packed, jnp.broadcast_to(amp_send[None], (blk_count, 3 * row_count, MAIN))], axis=1
-    )
-    got = lax.all_to_all(send, "blk", split_axis=0, concat_axis=0, tiled=False)
-    got = got.transpose(1, 0, 2).reshape(11, vir_total, MAIN)
+    amp_all = gather_blk(amp_send, blk_pos, blk_count)
+    amp_all = amp_all.transpose(1, 0, 2).reshape(3, vir_total, MAIN)
 
     def mixed(x):
         return x.reshape(blk_count, row_count).T.reshape(vir_total)
@@ -271,7 +312,7 @@
     vmem = pl.BlockSpec(memory_space=pltpu.VMEM)
     part = pl.pallas_call(
         pair_kernel,
-        in_specs=[smem, smem] + [vmem] * 7,
+        in_specs=[smem, smem] + [vmem] * 8,
         out_specs=vmem,
         out_shape=jax.ShapeDtypeStruct((3, vir_total, MAIN), BF),
         scratch_shapes=[
@@ -287,6 +328,7 @@
         own_irrep,
         pair_sym,
         got,
+        amp_all,
         irrep_mixed[:, None],
         irrep_mixed[None, :],
         pos_mixed[:, None],
@@ -305,16 +347,18 @@
         ]
     )
     spread = (jnp.arange(RUN, dtype=I32)[:, None] == col_pos[None, :]).astype(F32)
-    total = jnp.einsum("prj,jc->prc", short, spread, precision=lax.Precision.HIGHEST)
-    total = jnp.where(amp_mask, total, 0.0)
+    total = jnp.einsum("prj,jc->rpc", short, spread, precision=lax.Precision.HIGHEST)
+    mask_rpc = amp_mask.transpose(1, 0, 2)
+    amp_rpc = jnp.where(mask_rpc, amplitudes.transpose(1, 0, 2), 0.0)
+    total = jnp.where(mask_rpc, total, 0.0)
     denominator = (
-        (occ_energy[pair_first] + occ_energy[pair_second])[:, None, None]
-        - row_energy[None, :, None]
+        (occ_energy[pair_first] + occ_energy[pair_second])[None, :, None]
+        - row_energy[:, None, None]
         - col_energy[None, None, :]
     )
-    residual = total + denominator * amp_local
-    updated = amp_local - residual / denominator
-    return (residual, updated)
+    residual = total + denominator * amp_rpc
+    updated = amp_rpc - residual / denominator
+    return (residual.transpose(1, 0, 2), updated.transpose(1, 0, 2))
 
 
 def solution(mesh):

time: 137 us -> 141 us (1.029)
  starting transfers between devices: 29.3 us -> 42.2 us
  waiting for transfers between devices: 55.3 us -> 49.3 us
  other arithmetic: 7.3 us -> 5.17 us
    all_to_all x1, waiting for transfers between devices: 36.5 us -> 0.01 us  [per_device(): lax.all_to_all(packed, 'blk', split_axis=0, concat_axis=0, tiled=False)]
    ppermute x0 -> x9, waiting for transfers between devices: none -> 30.5 us  [gather_blk(): lax.ppermute(held, 'blk', [(i, i ^ k << low) for i in range(blk_count)])]
    ppermute x0 -> x9, starting transfers between devices: none -> 12.1 us  [gather_blk(): lax.ppermute(held, 'blk', [(i, i ^ k << low) for i in range(blk_count)])]
    unnamed x10 -> x22, local copies, waits for them, and re-layouts: 1.27 us -> 4.45 us
    reshape x2 -> x1, local copies, waits for them, and re-layouts: 1.52 us -> 0.08 us  [per_device(): occ_rows = pair_list.reshape(-1)]
  transfers between devices with their start and end apart: 8 -> 17, of which waited for: 4 -> 8; matrix products, arithmetic and copies ran while one was open for 11% -> 7% of each run, Pallas kernels for 7% -> 0%
where the time goes in v2:
time: 141 us; the launch traced here: 140 us
  waiting for transfers between devices  49.3 us (35%)
  starting transfers between devices  42.2 us (30%)
  Pallas kernels  23.7 us (17%)
  local copies, waits for them, and re-layouts  18.3 us (13%)
  other arithmetic  5.17 us (4%)
    ppermute x9, waiting for transfers between devices, gather_blk(): lax.ppermute(held, 'blk', [(i, i ^ k << low) for i in range(blk_count)])  30.5 us
    all_to_all x1, waiting for transfers between devices, per_device(): part = lax.all_to_all(part, 'blk', split_axis=0, concat_axis=0, tiled=False)  14.7 us
    pallas_call x1, Pallas kernels, per_device(): pl.pallas_call(pair_kernel, in_specs=[smem, smem] + [vmem] * 8, out_specs...  14.6 us
    all_to_all x1, starting transfers between devices, per_device(): lax.all_to_all(packed, 'blk', split_axis=0, concat_axis=0, tiled=False)  12.2 us
    ppermute x9, starting transfers between devices, gather_blk(): lax.ppermute(held, 'blk', [(i, i ^ k << low) for i in range(blk_count)])  12.1 us
    all_to_all x1, starting transfers between devices, per_device(): part = lax.all_to_all(part, 'blk', split_axis=0, concat_axis=0, tiled=False)  9.16 us
    pallas_call x1, Pallas kernels, per_device(): pl.pallas_call(pack_kernel, grid_spec=pltpu.PrefetchScalarGridSpec(num_sc...  9.15 us
    ppermute x6, starting transfers between devices, over_rep(): lax.ppermute(value, 'rep', [(i, (i + k) % 4) for i in range(4)])  8.72 us
  transfers between devices with their start and end apart: 17, of which 8 were waited for; matrix products, arithmetic and copies ran while one was open for 7% of the time, Pallas kernels for 0%

profile of v2, /device:TPU:6, one launch (start us, length us, event | category | flops | bytes accessed | tf_op | source)
XLA Modules:
  0.0 140.1 jit_solution(10075010650295584853)
XLA Ops:
  0.7 0.7 broadcast_in_dim.46.vir_irrep
  1.4 0.8 convert_reduce_fusion.1
  2.2 0.7 broadcast_in_dim.47.chol_irrep
  2.9 1.0 fusion.20
  3.9 0.7 copy-done.1
  4.5 1.1 copy-done.3
  5.7 0.7 copy-done.4
  6.3 0.7 copy-done.6
  7.0 9.1 %pack.1 = bf16[8,10,64,128]{3,2,1,0:T(8,128)(2,1)S(1)} custom-call(s32[640]{0:T(1024)S(1)} %copy-done.4, s32[100]{0:T(128)S(1)} %copy-done.1, s32[2,2]{1,0:T(2,128)S(1)} %copy-done.6, bf16[10,384,640]{2,1,0:T(8,128)(2,1)} %bitcast.56, bf16[10,100,384]{2,1,0:T(8,128)(2,1)S(1)} %bitcast.54, s32[1,640]{1,0:T(1,128)S(1)} %broadcast_in_dim.46.vir_irrep, ...), custom_call_target="tpu_custom_call" | custom-call | tf_op jit(solution)/shard_map/pack/pallas_call | solution.py:230
  16.2 1.9 %copy.76 = bf16[80,64,128]{2,0,1:T(8,128)(2,1)} copy(bf16[80,64,128]{2,1,0:T(8,128)(2,1)S(1)} %bitcast.50) | data formatting | bytes 2621440 | tf_op jit(solution)/shard_map/reshape | solution.py:260
  18.3 0.6 gather_fusion
  18.9 0.6 gather_fusion.1
  20.2 3.1 %collective-permute-start.2 = (f32[30,128]{1,0:T(8,128)S(1)}, f32[30,128]{1,0:T(8,128)S(1)}, u32[]{:S(2)}, u32[]{:S(2)}) collective-permute-start(f32[30,128]{1,0:T(8,128)S(1)} %reshape.194), channel_id=1, source_target_pairs={{0,3},{1,0},{2,1},{3,2},{4,7},{5,4},{6,5},{7,6},{8,11},{9,8},{10,9... | collective-permute-start | bytes 46088 | tf_op jit(solution)/shard_map/ppermute | solution.py:169
  23.3 0.6 collective-permute-start.1
  23.9 1.0 collective-permute-start
  24.9 12.2 %all-to-all-start = ((bf16[64,80,128]{2,1,0:T(8,128)(2,1)}), bf16[64,80,128]{2,1,0:T(8,128)(2,1)S(1)}, u32[]{:S(2)}, u32[]{:S(2)}) async-start(bf16[64,80,128]{2,1,0:T(8,128)(2,1)} %bitcast.48), calls=%async_computation | async-start | bytes 2621440 | tf_op jit(solution)/shard_map/all_to_all | solution.py:262
  37.3 0.6 gather_fusion.2
  37.9 0.6 gather_fusion.3
  38.9 1.3 collective-permute-start.3
  40.2 0.6 collective-permute-start.4
  40.9 26.0 %collective-permute-done.3 = bf16[1,30,128]{2,1,0:T(8,128)(2,1)S(1)} collective-permute-done((bf16[1,30,128]{2,1,0:T(8,128)(2,1)S(1)}, bf16[1,30,128]{2,1,0:T(8,128)(2,1)S(1)}, u32[]{:S(2)}, u32[]{:S(2)}) %collective-permute-start.3) | collective-permute-done | bytes 7712 | tf_op jit(solution)/shard_map/ppermute | solution.py:177
  66.9 0.9 collective-permute-done.4
  67.8 4.6 %collective-permute-start.7 = (bf16[4,30,128]{2,1,0:T(8,128)(2,1)S(1)}, bf16[4,30,128]{2,1,0:T(8,128)(2,1)S(1)}, u32[]{:S(2)}, u32[]{:S(2)}) collective-permute-start(bf16[4,30,128]{2,1,0:T(8,128)(2,1)S(1)} %pad_maximum_fusion.1), channel_id=1, source_target_pairs={{0,32},{4,36},{8,40},{12,44},{16,48},{20,52},{24,56},{28,60},{32,0... | collective-permute-start | bytes 92168 | tf_op jit(solution)/shard_map/ppermute | solution.py:177
  72.4 2.0 %collective-permute-start.8 = (bf16[4,30,128]{2,1,0:T(8,128)(2,1)S(1)}, bf16[4,30,128]{2,1,0:T(8,128)(2,1)S(1)}, u32[]{:S(2)}, u32[]{:S(2)}) collective-permute-start(bf16[4,30,128]{2,1,0:T(8,128)(2,1)S(1)} %pad_maximum_fusion.1), channel_id=1, source_target_pairs={{0,16},{4,20},{8,24},{12,28},{16,0},{20,4},{24,8},{28,12},{32,48},... | collective-permute-start | bytes 92168 | tf_op jit(solution)/shard_map/ppermute | solution.py:177
  74.4 0.6 fusion.25
  75.0 0.7 collective-permute-done.7
  75.7 2.8 %collective-permute-done.6 = bf16[4,30,128]{2,1,0:T(8,128)(2,1)S(1)} collective-permute-done((bf16[4,30,128]{2,1,0:T(8,128)(2,1)S(1)}, bf16[4,30,128]{2,1,0:T(8,128)(2,1)S(1)}, u32[]{:S(2)}, u32[]{:S(2)}) %collective-permute-start.6) | collective-permute-done | bytes 30752 | tf_op jit(solution)/shard_map/ppermute | solution.py:177
  78.6 1.3 collective-permute-start.10
  79.9 2.2 %collective-permute-start.9 = (bf16[16,30,128]{2,1,0:T(8,128)(2,1)S(1)}, bf16[16,30,128]{2,1,0:T(8,128)(2,1)S(1)}, u32[]{:S(2)}, u32[]{:S(2)}) collective-permute-start(bf16[16,30,128]{2,1,0:T(8,128)(2,1)S(1)} %pad_maximum_fusion), channel_id=1, source_target_pairs={{0,192},{4,196},{8,200},{12,204},{16,208},{20,212},{24,216},{28,22... | collective-permute-start | bytes 368648 | tf_op jit(solution)/shard_map/ppermute | solution.py:177
  82.2 2.5 %compare_select_fusion.4.occ_lanes = s32[1,384]{1,0:T(1,128)S(1)} fusion(s32[]{:T(128)} %bitcast.20, s32[]{:T(128)} %bitcast.19, s32[]{:T(128)} %bitcast.18, s32[]{:T(128)} %bitcast.17), kind=kLoop, calls=%fused_computation.78 | loop fusion | flops 2304 | bytes 1552 | tf_op jit(solution)/shard_map/jit(_where)/select_n | solution.py:302
  84.8 0.3 broadcast_in_dim_reshape.16.row_irrep
  85.3 0.3 broadcast_in_dim_reshape.17.row_pos
  85.6 0.8 dynamic_slice.24
  87.5 0.3 copy.53
  87.8 14.6 %ladder.1 = bf16[3,640,128]{2,1,0:T(8,128)(2,1)S(1)} custom-call(s32[6]{0:T(128)S(1)} %dynamic-slice_reduce_fusion.q_irrep, s32[2]{0:T(128)S(1)} %xor.24.pair_sym, bf16[8,640,128]{2,1,0:T(8,128)(2,1)S(1)} %bitcast.51, bf16[3,640,128]{2,1,0:T(8,128)(2,1)S(1)} %bitcast.52, s32[640,1]{1,0:T(8,128)S(1)} %broadcast_in_dim_reshape.16.row_irrep, ...), custom_call_target="tpu_custom_call" | custom-call | tf_op jit(solution)/shard_map/ladder/pallas_call | solution.py:313
  102.4 1.1 copy.77
  103.6 9.2 %all-to-all-start.1 = ((bf16[64,30,128]{2,1,0:T(8,128)(2,1)}), bf16[64,30,128]{2,1,0:T(8,128)(2,1)S(1)}, u32[]{:S(2)}, u32[]{:S(2)}) async-start(bf16[64,30,128]{2,1,0:T(8,128)(2,1)} %bitcast.49), calls=%async_computation.1 | async-start | bytes 1048576 | tf_op jit(solution)/shard_map/all_to_all | solution.py:340
  112.7 0.6 gather_fusion.4
  113.4 0.6 gather_fusion.5
  114.0 0.8 dynamic_slice.27
  114.8 14.7 %all-to-all-done.1 = bf16[64,30,128]{2,1,0:T(8,128)(2,1)S(1)} async-done(((bf16[64,30,128]{2,1,0:T(8,128)(2,1)}), bf16[64,30,128]{2,1,0:T(8,128)(2,1)S(1)}, u32[]{:S(2)}, u32[]{:S(2)}) %all-to-all-start.1) | async-done | bytes 491552 | tf_op jit(solution)/shard_map/all_to_all | solution.py:340
  129.6 2.3 %collective-permute-start.14 = (f32[30,128]{1,0:T(8,128)S(1)}, f32[30,128]{1,0:T(8,128)S(1)}, u32[]{:S(2)}, u32[]{:S(2)}) collective-permute-start(f32[30,128]{1,0:T(8,128)S(1)} %convert_reduce_fusion), channel_id=1, source_target_pairs={{0,3},{1,0},{2,1},{3,2},{4,7},{5,4},{6,5},{7,6},{8,11},{9,8},{10,9... | collective-permute-start | bytes 46088 | tf_op jit(solution)/shard_map/ppermute | solution.py:169
  131.9 1.7 %collective-permute-start.13 = (f32[30,128]{1,0:T(8,128)S(1)}, f32[30,128]{1,0:T(8,128)S(1)}, u32[]{:S(2)}, u32[]{:S(2)}) collective-permute-start(f32[30,128]{1,0:T(8,128)S(1)} %convert_reduce_fusion), channel_id=1, source_target_pairs={{0,2},{1,3},{2,0},{3,1},{4,6},{5,7},{6,4},{7,5},{8,10},{9,11},{10,... | collective-permute-start | bytes 46088 | tf_op jit(solution)/shard_map/ppermute | solution.py:169
  133.6 0.8 dynamic_slice.28
  134.4 2.7 %collective-permute-done.13 = f32[30,128]{1,0:T(8,128)S(1)} collective-permute-done((f32[30,128]{1,0:T(8,128)S(1)}, f32[30,128]{1,0:T(8,128)S(1)}, u32[]{:S(2)}, u32[]{:S(2)}) %collective-permute-start.13) | collective-permute-done | bytes 15392 | tf_op jit(solution)/shard_map/ppermute | solution.py:169
  137.1 1.4 %collective-permute-done.12 = f32[30,128]{1,0:T(8,128)S(1)} collective-permute-done((f32[30,128]{1,0:T(8,128)S(1)}, f32[30,128]{1,0:T(8,128)S(1)}, u32[]{:S(2)}, u32[]{:S(2)}) %collective-permute-start.12) | collective-permute-done | bytes 15392 | tf_op jit(solution)/shard_map/ppermute | solution.py:169
  138.8 0.6 copy.64
  139.5 0.6 copy.65
  (81 shorter events, 3.4 us)
Async XLA Ops:
  0.6 37.3 %copy-start = (bf16[100,640]{1,0:T(8,128)(2,1)S(1)}, bf16[100,640]{1,0:T(8,128)(2,1)}, u32[]{:S(2)}) copy-start(bf16[100,640]{1,0:T(8,128)(2,1)} %param.11) | copy-start | bytes 384004
  3.9 0.7 copy-start.1
  4.5 1.1 copy-start.3
  5.7 0.7 copy-start.4
  6.3 0.7 copy-start.6
  16.2 2.0 %copy-start.5 = (s32[640]{0:T(1024)S(1)}, s32[640]{0:T(1024)}, u32[]{:S(2)}) copy-start(s32[640]{0:T(1024)} %vir_s.1) | copy-start | bytes 7684
  16.2 2.1 %copy-start.2 = (s32[100]{0:T(128)S(1)}, s32[100]{0:T(128)}, u32[]{:S(2)}) copy-start(s32[100]{0:T(128)} %occ_s.1) | copy-start | bytes 1204
  16.2 3.6 %copy-start.9 = (f32[2,10,160]{2,0,1:T(2,128)S(1)}, f32[2,10,160]{2,0,1:T(2,128)}, u32[]{:S(2)}) copy-start(f32[2,10,160]{2,0,1:T(2,128)} %param.10) | copy-start | bytes 38404
  20.1 16.9 %copy-start.7 = (s32[2,2]{1,0:T(2,128)S(1)}, s32[2,2]{1,0:T(2,128)}, u32[]{:S(2)}) copy-start(s32[2,2]{1,0:T(2,128)} %pair_s.1) | copy-start | bytes 52
  20.2 18.7 %collective-permute-start.2 = (f32[30,128]{1,0:T(8,128)S(1)}, f32[30,128]{1,0:T(8,128)S(1)}, u32[]{:S(2)}, u32[]{:S(2)}) collective-permute-start(f32[30,128]{1,0:T(8,128)S(1)} %reshape.194), channel_id=1, source_target_pairs={{0,3},{1,0},{2,1},{3,2},{4,7},{5,4},{6,5},{7,6},{8,11},{9,8},{10,9... | collective-permute-start | bytes 46088 | tf_op jit(solution)/shard_map/ppermute | solution.py:169
  23.3 15.6 %collective-permute-start.1 = (f32[30,128]{1,0:T(8,128)S(1)}, f32[30,128]{1,0:T(8,128)S(1)}, u32[]{:S(2)}, u32[]{:S(2)}) collective-permute-start(f32[30,128]{1,0:T(8,128)S(1)} %reshape.194), channel_id=1, source_target_pairs={{0,2},{1,3},{2,0},{3,1},{4,6},{5,7},{6,4},{7,5},{8,10},{9,11},{10,... | collective-permute-start | bytes 46088 | tf_op jit(solution)/shard_map/ppermute | solution.py:169
  23.9 15.0 %collective-permute-start = (f32[30,128]{1,0:T(8,128)S(1)}, f32[30,128]{1,0:T(8,128)S(1)}, u32[]{:S(2)}, u32[]{:S(2)}) collective-permute-start(f32[30,128]{1,0:T(8,128)S(1)} %reshape.194), channel_id=1, source_target_pairs={{0,1},{1,2},{2,3},{3,0},{4,5},{5,6},{6,7},{7,4},{8,9},{9,10},{10,1... | collective-permute-start | bytes 46088 | tf_op jit(solution)/shard_map/ppermute | solution.py:169
  24.9 62.6 %all-to-all-start = ((bf16[64,80,128]{2,1,0:T(8,128)(2,1)}), bf16[64,80,128]{2,1,0:T(8,128)(2,1)S(1)}, u32[]{:S(2)}, u32[]{:S(2)}) async-start(bf16[64,80,128]{2,1,0:T(8,128)(2,1)} %bitcast.48), calls=%async_computation | async-start | bytes 2621440 | tf_op jit(solution)/shard_map/all_to_all | solution.py:262
  38.9 27.9 %collective-permute-start.3 = (bf16[1,30,128]{2,1,0:T(8,128)(2,1)S(1)}, bf16[1,30,128]{2,1,0:T(8,128)(2,1)S(1)}, u32[]{:S(2)}, u32[]{:S(2)}) collective-permute-start(bf16[1,30,128]{2,1,0:T(8,128)(2,1)S(1)} %fusion.18), channel_id=1, source_target_pairs={{0,12},{4,8},{8,4},{12,0},{16,28},{20,24},{24,20},{28,16},{32,44},... | collective-permute-start | bytes 23048 | tf_op jit(solution)/shard_map/ppermute | solution.py:177
  40.2 27.5 %collective-permute-start.4 = (bf16[1,30,128]{2,1,0:T(8,128)(2,1)S(1)}, bf16[1,30,128]{2,1,0:T(8,128)(2,1)S(1)}, u32[]{:S(2)}, u32[]{:S(2)}) collective-permute-start(bf16[1,30,128]{2,1,0:T(8,128)(2,1)S(1)} %fusion.18), channel_id=1, source_target_pairs={{0,8},{4,12},{8,0},{12,4},{16,24},{20,28},{24,16},{28,20},{32,40},... | collective-permute-start | bytes 23048 | tf_op jit(solution)/shard_map/ppermute | solution.py:177
  40.8 27.0 %collective-permute-start.5 = (bf16[1,30,128]{2,1,0:T(8,128)(2,1)S(1)}, bf16[1,30,128]{2,1,0:T(8,128)(2,1)S(1)}, u32[]{:S(2)}, u32[]{:S(2)}) collective-permute-start(bf16[1,30,128]{2,1,0:T(8,128)(2,1)S(1)} %fusion.18), channel_id=1, source_target_pairs={{0,4},{4,0},{8,12},{12,8},{16,20},{20,16},{24,28},{28,24},{32,36},... | collective-permute-start | bytes 23048 | tf_op jit(solution)/shard_map/ppermute | solution.py:177
  67.8 7.9 %collective-permute-start.7 = (bf16[4,30,128]{2,1,0:T(8,128)(2,1)S(1)}, bf16[4,30,128]{2,1,0:T(8,128)(2,1)S(1)}, u32[]{:S(2)}, u32[]{:S(2)}) collective-permute-start(bf16[4,30,128]{2,1,0:T(8,128)(2,1)S(1)} %pad_maximum_fusion.1), channel_id=1, source_target_pairs={{0,32},{4,36},{8,40},{12,44},{16,48},{20,52},{24,56},{28,60},{32,0... | collective-permute-start | bytes 92168 | tf_op jit(solution)/shard_map/ppermute | solution.py:177
  72.4 6.1 %collective-permute-start.6 = (bf16[4,30,128]{2,1,0:T(8,128)(2,1)S(1)}, bf16[4,30,128]{2,1,0:T(8,128)(2,1)S(1)}, u32[]{:S(2)}, u32[]{:S(2)}) collective-permute-start(bf16[4,30,128]{2,1,0:T(8,128)(2,1)S(1)} %pad_maximum_fusion.1), channel_id=1, source_target_pairs={{0,48},{4,52},{8,56},{12,60},{16,32},{20,36},{24,40},{28,44},{32,1... | collective-permute-start | bytes 92168 | tf_op jit(solution)/shard_map/ppermute | solution.py:177
  72.4 6.1 %collective-permute-start.8 = (bf16[4,30,128]{2,1,0:T(8,128)(2,1)S(1)}, bf16[4,30,128]{2,1,0:T(8,128)(2,1)S(1)}, u32[]{:S(2)}, u32[]{:S(2)}) collective-permute-start(bf16[4,30,128]{2,1,0:T(8,128)(2,1)S(1)} %pad_maximum_fusion.1), channel_id=1, source_target_pairs={{0,16},{4,20},{8,24},{12,28},{16,0},{20,4},{24,8},{28,12},{32,48},... | collective-permute-start | bytes 92168 | tf_op jit(solution)/shard_map/ppermute | solution.py:177
  78.6 8.3 %collective-permute-start.10 = (bf16[16,30,128]{2,1,0:T(8,128)(2,1)S(1)}, bf16[16,30,128]{2,1,0:T(8,128)(2,1)S(1)}, u32[]{:S(2)}, u32[]{:S(2)}) collective-permute-start(bf16[16,30,128]{2,1,0:T(8,128)(2,1)S(1)} %pad_maximum_fusion), channel_id=1, source_target_pairs={{0,128},{4,132},{8,136},{12,140},{16,144},{20,148},{24,152},{28,15... | collective-permute-start | bytes 368648 | tf_op jit(solution)/shard_map/ppermute | solution.py:177
  79.9 7.1 %collective-permute-start.9 = (bf16[16,30,128]{2,1,0:T(8,128)(2,1)S(1)}, bf16[16,30,128]{2,1,0:T(8,128)(2,1)S(1)}, u32[]{:S(2)}, u32[]{:S(2)}) collective-permute-start(bf16[16,30,128]{2,1,0:T(8,128)(2,1)S(1)} %pad_maximum_fusion), channel_id=1, source_target_pairs={{0,192},{4,196},{8,200},{12,204},{16,208},{20,212},{24,216},{28,22... | collective-permute-start | bytes 368648 | tf_op jit(solution)/shard_map/ppermute | solution.py:177
  82.1 5.0 %collective-permute-start.11 = (bf16[16,30,128]{2,1,0:T(8,128)(2,1)S(1)}, bf16[16,30,128]{2,1,0:T(8,128)(2,1)S(1)}, u32[]{:S(2)}, u32[]{:S(2)}) collective-permute-start(bf16[16,30,128]{2,1,0:T(8,128)(2,1)S(1)} %pad_maximum_fusion), channel_id=1, source_target_pairs={{0,64},{4,68},{8,72},{12,76},{16,80},{20,84},{24,88},{28,92},{32,9... | collective-permute-start | bytes 368648 | tf_op jit(solution)/shard_map/ppermute | solution.py:177
  102.4 10.3 %copy-start.8 = (f32[100]{0:T(128)S(1)}, f32[100]{0:T(128)}, u32[]{:S(2)}) copy-start(f32[100]{0:T(128)} %param.14) | copy-start | bytes 1204
  103.6 25.9 %all-to-all-start.1 = ((bf16[64,30,128]{2,1,0:T(8,128)(2,1)}), bf16[64,30,128]{2,1,0:T(8,128)(2,1)S(1)}, u32[]{:S(2)}, u32[]{:S(2)}) async-start(bf16[64,30,128]{2,1,0:T(8,128)(2,1)} %bitcast.49), calls=%async_computation.1 | async-start | bytes 1048576 | tf_op jit(solution)/shard_map/all_to_all | solution.py:340
  129.6 4.9 %collective-permute-start.14 = (f32[30,128]{1,0:T(8,128)S(1)}, f32[30,128]{1,0:T(8,128)S(1)}, u32[]{:S(2)}, u32[]{:S(2)}) collective-permute-start(f32[30,128]{1,0:T(8,128)S(1)} %convert_reduce_fusion), channel_id=1, source_target_pairs={{0,3},{1,0},{2,1},{3,2},{4,7},{5,4},{6,5},{7,6},{8,11},{9,8},{10,9... | collective-permute-start | bytes 46088 | tf_op jit(solution)/shard_map/ppermute | solution.py:169
  131.9 5.2 %collective-permute-start.13 = (f32[30,128]{1,0:T(8,128)S(1)}, f32[30,128]{1,0:T(8,128)S(1)}, u32[]{:S(2)}, u32[]{:S(2)}) collective-permute-start(f32[30,128]{1,0:T(8,128)S(1)} %convert_reduce_fusion), channel_id=1, source_target_pairs={{0,2},{1,3},{2,0},{3,1},{4,6},{5,7},{6,4},{7,5},{8,10},{9,11},{10,... | collective-permute-start | bytes 46088 | tf_op jit(solution)/shard_map/ppermute | solution.py:169
  133.6 4.9 %collective-permute-start.12 = (f32[30,128]{1,0:T(8,128)S(1)}, f32[30,128]{1,0:T(8,128)S(1)}, u32[]{:S(2)}, u32[]{:S(2)}) collective-permute-start(f32[30,128]{1,0:T(8,128)S(1)} %convert_reduce_fusion), channel_id=1, source_target_pairs={{0,1},{1,2},{2,3},{3,0},{4,5},{5,6},{6,7},{7,4},{8,9},{9,10},{10,1... | collective-permute-start | bytes 46088 | tf_op jit(solution)/shard_map/ppermute | solution.py:169

commit v3 on v2

v3 whole, which is shorter than its diff:
```python
import jax
import jax.numpy as jnp
from jax import lax
from jax.experimental import pallas as pl
from jax.experimental.pallas import tpu as pltpu
from jax.sharding import PartitionSpec as P

BF = jnp.bfloat16
F32 = jnp.float32
I32 = jnp.int32
RUN = 160
MAIN = 128
STRIDE = 40
GROUPS = 3
REST = RUN - MAIN
CYCLE_LANE = GROUPS * STRIDE
LIMIT = 48 * 1024 * 1024
NT = (((1,), (1,)), ((), ()))


def dot(x, y):
    return jnp.dot(x, y, preferred_element_type=F32)


def run_positions(irrep):
    place = lax.broadcasted_iota(I32, irrep.shape, 1)
    for label in range(7):
        count = jnp.sum(jnp.where(irrep == label, 1.0, 0.0), axis=1, keepdims=True)
        place = place - jnp.where(irrep > label, count.astype(I32), 0)
    return place


def pack_kernel(
    vir_s, occ_s, pair_s, chol, ov, vir_irrep, chol_irrep, out, fold, labels, pick
):
    step = pl.program_id(0)
    rows, q_local, vir_total = chol.shape
    occ_total = ov.shape[1]
    own = out.shape[2]

    @pl.when(step == 0)
    def _():
        place = run_positions(vir_irrep[...])
        row = lax.broadcasted_iota(I32, (2 * MAIN, vir_total), 0)
        fold[...] = jnp.where(row == place, 1.0, 0.0).T.astype(BF)
        first = pl.multiple_of(lax.axis_index("rep") * q_local, MAIN)
        mine = chol_irrep[:, pl.ds(first, q_local)].astype(F32)
        labels[...] = jnp.broadcast_to(mine, (MAIN, q_local)).T.astype(I32)
        row = lax.broadcasted_iota(I32, (occ_total, MAIN), 0)
        lane = lax.broadcasted_iota(I32, (occ_total, MAIN), 1)
        taken = jnp.zeros((occ_total, MAIN), F32)
        for m in range(4):
            hit = (row == pair_s[m // 2, m % 2]) & (lane == REST + m)
            taken = jnp.where(hit, 1.0, taken)
        pick[...] = taken.astype(BF)

    lane = lax.broadcasted_iota(I32, (1, MAIN), 1)
    occ_label = jnp.zeros((1, MAIN), I32)
    for m in range(4):
        occ_label = jnp.where(lane == REST + m, occ_s[pair_s[m // 2, m % 2]], occ_label)
    first_row = (lax.axis_index("blk") * pl.num_programs(0) + step) * rows
    wants = [jnp.bitwise_xor(labels[...], vir_s[first_row + k]) for k in range(rows)]
    kept = [
        jnp.where(wants[k][:, :1] == vir_irrep[...], chol[k].astype(F32), 0.0).astype(BF)
        for k in range(rows)
    ]
    folded = dot(jnp.concatenate(kept, axis=0), fold[...])
    for k in range(rows):
        mine = folded[k * q_local : (k + 1) * q_local]
        extra = lax.dot_general(
            ov[k], pick[...], (((0,), (0,)), ((), ())), preferred_element_type=F32
        )
        rest = mine[:, MAIN:] + jnp.where(wants[k] == occ_label, extra, 0.0)
        for q in range(2 * GROUPS):
            out[q, k] = mine[q * own : (q + 1) * own, :MAIN].astype(BF)
        for u in range(2):
            total = rest[u * GROUPS * own : (u * GROUPS + 1) * own]
            for g in range(1, GROUPS):
                part = rest[(u * GROUPS + g) * own : (u * GROUPS + g + 1) * own]
                total = total + pltpu.roll(part, g * STRIDE, 1)
            out[2 * GROUPS + u, k] = total.astype(BF)


def amp_kernel(vir_s, occ_s, pair_s, amp, vir_irrep, out):
    row_count, pair_count, col_count = amp.shape
    rep_pos = lax.axis_index("rep")
    first_row = lax.axis_index("blk") * row_count
    place = run_positions(vir_irrep[...])
    col_irrep = vir_irrep[:, :col_count]
    col_place = place[:, :col_count]
    for k in range(1, 4):
        cols = slice(k * col_count, (k + 1) * col_count)
        col_irrep = jnp.where(rep_pos == k, vir_irrep[:, cols], col_irrep)
        col_place = jnp.where(rep_pos == k, place[:, cols], col_place)
    lane = lax.broadcasted_iota(I32, (2 * MAIN, col_count), 0)
    fold = jnp.where(lane == col_place, 1.0, 0.0).astype(BF)
    row = lax.broadcasted_iota(I32, (row_count, 1), 0)
    row_irrep = jnp.zeros((row_count, 1), I32)
    for k in range(row_count):
        row_irrep = jnp.where(row == k, vir_s[first_row + k], row_irrep)
    for p in range(pair_count):
        sym = jnp.bitwise_xor(occ_s[pair_s[p, 0]], occ_s[pair_s[p, 1]])
        want = jnp.bitwise_xor(row_irrep, sym)
        kept = jnp.where(want == col_irrep, amp[:, p, :], 0.0).astype(BF)
        short = lax.dot_general(kept, fold, NT, preferred_element_type=F32)
        out[p] = short[:, :MAIN]
        out[2, :, p * 64 : (p + 1) * 64] = short[:, MAIN : MAIN + 64]


def pair_kernel(
    q_irrep,
    pair_sym,
    got,
    row_irrep,
    col_irrep,
    row_pos,
    col_pos,
    single_rows,
    occ_lanes,
    out,
    ball,
    hall,
    amps,
    unfold,
    weight,
):
    vir_total = row_irrep.shape[0]
    single = single_rows[...].astype(BF)
    rest_amp = got[10].astype(F32)
    lane = lax.broadcasted_iota(I32, (vir_total, MAIN), 1)
    index = lax.broadcasted_iota(I32, (2 * MAIN, vir_total), 0)
    column = col_pos[...]
    for g in range(GROUPS):
        place = jnp.where(column < MAIN, column, column + g * STRIDE)
        unfold[g] = jnp.where(index == place, 1.0, 0.0).astype(BF)
        short = lax.dot_general(single, unfold[g], NT, preferred_element_type=F32)
        slot = lax.broadcasted_iota(I32, short.shape, 0)
        at = lax.broadcasted_iota(I32, short.shape, 1)
        short = short + jnp.where(
            (at == slot + MAIN + g * STRIDE + REST) & (slot < 4), 1.0, 0.0
        )
        row = lax.broadcasted_iota(I32, (MAIN, 2 * MAIN), 0)
        zero = jnp.zeros((MAIN, 2 * MAIN), F32)
        first = CYCLE_LANE
        for m in range(2):
            weight[g, m * MAIN : (m + 1) * MAIN] = jnp.where(
                row == first,
                short[1 - m : 2 - m],
                jnp.where(row == first + 1, short[3 - m : 4 - m], zero),
            ).astype(BF)
        for p in range(2):
            amps[g, :, p * 256 : p * 256 + MAIN] = got[8 + p]
            shift = (g * STRIDE - p * 64) % MAIN
            moved = pltpu.roll(rest_amp, shift, 1) if shift else rest_amp
            inside = (lane >= g * STRIDE) & (lane < g * STRIDE + REST)
            amps[g, :, p * 256 + MAIN : (p + 1) * 256] = jnp.where(inside, moved, 0.0).astype(BF)

    def one(q, carry):
        g = q % GROUPS
        bc = jnp.concatenate([got[q], got[2 * GROUPS + q // GROUPS]], axis=1)
        want = jnp.bitwise_xor(row_irrep[...], q_irrep[q])
        wide = dot(bc, unfold[g])
        wide = jnp.where(want == col_irrep[...], wide, 0.0).astype(BF)
        halfway = dot(wide, amps[g])
        dressed = lax.dot_general(bc, weight[g], NT, preferred_element_type=F32)
        dressed = jnp.where(want == occ_lanes[...], dressed, 0.0)
        ball[q, :, :MAIN] = bc[:, :MAIN]
        ball[q, :, MAIN:] = (bc[:, MAIN:].astype(F32) + dressed[:, :MAIN]).astype(BF)
        for p in range(2):
            hall[p, q, :, :MAIN] = halfway[:, p * 256 : p * 256 + MAIN].astype(BF)
            own = jnp.where(lane == CYCLE_LANE + p, dressed[:, MAIN:], 0.0)
            hall[p, q, :, MAIN:] = (
                halfway[:, p * 256 + MAIN : (p + 1) * 256] + own
            ).astype(BF)
        return carry

    lax.fori_loop(0, 2 * GROUPS, one, 0)

    lane2 = lax.broadcasted_iota(I32, (vir_total, 2 * MAIN), 1)
    tail = None
    for p in range(2):
        value = lax.dot_general(hall[p, 0], ball[0], NT, preferred_element_type=F32)
        for q in range(1, 2 * GROUPS):
            value = value + lax.dot_general(
                hall[p, q], ball[q], NT, preferred_element_type=F32
            )
        want = jnp.bitwise_xor(row_irrep[...], pair_sym[p])
        value = jnp.where(want == col_irrep[...], value, 0.0).astype(BF)
        place = row_pos[...]
        place = jnp.where(place < MAIN, place, place + p * 64)
        fold = jnp.where(lane2 == place, 1.0, 0.0).astype(BF)
        short = dot(value, fold)
        out[p] = short[:, :MAIN].astype(BF)
        tail = short[:, MAIN:] if tail is None else tail + short[:, MAIN:]
    out[2] = tail.astype(BF)


def over_rep(value):
    total = value
    for k in (1, 2, 3):
        total = total + lax.ppermute(value, "rep", [(i, (i + k) % 4) for i in range(4)])
    return total


def per_device(
    amplitudes,
    singles,
    chol_vv,
    chol_ov,
    occ_energy,
    vir_energy,
    vir_irrep,
    occ_irrep,
    chol_irrep,
    pair_list,
):
    blk_pos = lax.axis_index("blk")
    rep_pos = lax.axis_index("rep")
    q_local, row_count, vir_total = chol_vv.shape
    col_count = amplitudes.shape[2]
    blk_count = vir_total // row_count
    q_own = q_local // blk_count
    occ_total = chol_ov.shape[1]
    vir_line = vir_irrep[None, :]
    amp_send = pl.pallas_call(
        amp_kernel,
        grid_spec=pltpu.PrefetchScalarGridSpec(
            num_scalar_prefetch=3,
            grid=(1,),
            in_specs=[
                pl.BlockSpec((row_count, 2, col_count), lambda i, *s: (0, 0, 0)),
                pl.BlockSpec((1, vir_total), lambda i, *s: (0, 0)),
            ],
            out_specs=pl.BlockSpec((3, row_count, MAIN), lambda i, *s: (0, 0, 0)),
        ),
        out_shape=jax.ShapeDtypeStruct((3, row_count, MAIN), F32),
        name="amp",
    )(vir_irrep, occ_irrep, pair_list, amplitudes.transpose(1, 0, 2), vir_line)
    amp_send = over_rep(amp_send).astype(BF).reshape(3 * row_count, MAIN)

    rows = 2
    packed = pl.pallas_call(
        pack_kernel,
        grid_spec=pltpu.PrefetchScalarGridSpec(
            num_scalar_prefetch=3,
            grid=(row_count // rows,),
            in_specs=[
                pl.BlockSpec((rows, q_local, vir_total), lambda i, *s: (i, 0, 0)),
                pl.BlockSpec((rows, occ_total, q_local), lambda i, *s: (i, 0, 0)),
                pl.BlockSpec((1, vir_total), lambda i, *s: (0, 0)),
                pl.BlockSpec((1, chol_irrep.shape[0]), lambda i, *s: (0, 0)),
            ],
            out_specs=pl.BlockSpec((8, rows, blk_count, MAIN), lambda i, *s: (0, i, 0, 0)),
            scratch_shapes=[
                pltpu.VMEM((vir_total, 2 * MAIN), BF),
                pltpu.VMEM((q_local, MAIN), I32),
                pltpu.VMEM((occ_total, MAIN), BF),
            ],
        ),
        out_shape=jax.ShapeDtypeStruct((8, row_count, blk_count, MAIN), BF),
        compiler_params=pltpu.CompilerParams(vmem_limit_bytes=LIMIT),
        cost_estimate=pl.CostEstimate(
            flops=2 * q_local * row_count * vir_total * 256,
            bytes_accessed=2 * q_local * row_count * vir_total,
            transcendentals=0,
        ),
        name="pack",
    )(
        vir_irrep,
        occ_irrep,
        pair_list,
        chol_vv.transpose(1, 0, 2),
        chol_ov.transpose(2, 1, 0),
        vir_line,
        chol_irrep[None, :],
    )
    packed = packed.reshape(8 * row_count, blk_count, MAIN).transpose(1, 0, 2)

    def swap(value):
        return lax.all_to_all(value, "blk", split_axis=0, concat_axis=0, tiled=False)

    got = swap(
        jnp.concatenate(
            [packed, jnp.broadcast_to(amp_send[None], (blk_count,) + amp_send.shape)], axis=1
        )
    )
    vir_irrep, singles, pair_list = lax.optimization_barrier(
        (vir_irrep, singles, pair_list, packed)
    )[:3]
    starts = jnp.sum(
        (vir_irrep[None, :] < jnp.arange(8, dtype=I32)[:, None]).astype(I32), axis=1
    )
    vir_pos = jnp.arange(vir_total, dtype=I32) - jnp.sum(
        jnp.where(vir_irrep[:, None] == jnp.arange(8, dtype=I32)[None, :], starts[None, :], 0),
        axis=1,
    )
    row_irrep = lax.dynamic_slice_in_dim(vir_irrep, blk_pos * row_count, row_count)
    col_irrep = lax.dynamic_slice_in_dim(vir_irrep, rep_pos * col_count, col_count)
    col_pos = lax.dynamic_slice_in_dim(vir_pos, rep_pos * col_count, col_count)
    q_irrep = lax.dynamic_slice_in_dim(chol_irrep, rep_pos * q_local, q_local)
    row_energy = lax.dynamic_slice_in_dim(vir_energy, blk_pos * row_count, row_count)
    col_energy = lax.dynamic_slice_in_dim(vir_energy, rep_pos * col_count, col_count)
    pair_first = pair_list[:, 0]
    pair_second = pair_list[:, 1]
    pair_sym = jnp.bitwise_xor(occ_irrep[pair_first], occ_irrep[pair_second])
    occ_rows = pair_list.reshape(-1)
    occ_labels = occ_irrep[occ_rows]
    amp_mask = (
        jnp.bitwise_xor(row_irrep[None, :, None], col_irrep[None, None, :])
        == pair_sym[:, None, None]
    )
    got = got.transpose(1, 0, 2).reshape(11, vir_total, MAIN)

    def mixed(x):
        return x.reshape(blk_count, row_count).T.reshape(vir_total)

    irrep_mixed = mixed(vir_irrep)
    pos_mixed = mixed(vir_pos)
    own_irrep = lax.dynamic_index_in_dim(
        q_irrep.reshape(q_own, blk_count), blk_pos, axis=1, keepdims=False
    )
    single_rows = jnp.where(
        occ_labels[:, None] == vir_irrep[None, :], singles[occ_rows], jnp.zeros((), singles.dtype)
    ).astype(F32)
    single_rows = single_rows.reshape(4, blk_count, row_count).transpose(0, 2, 1)
    single_rows = jnp.pad(single_rows.reshape(4, vir_total), ((0, 4), (0, 0)))
    first = CYCLE_LANE
    lane_row = jnp.arange(2 * MAIN, dtype=I32)
    occ_lanes = jnp.where(
        lane_row == first,
        occ_labels[1],
        jnp.where(
            lane_row == first + 1,
            occ_labels[3],
            jnp.where(lane_row == MAIN + first, occ_labels[0], occ_labels[2]),
        ),
    )[None, :]
    smem = pl.BlockSpec(memory_space=pltpu.SMEM)
    vmem = pl.BlockSpec(memory_space=pltpu.VMEM)
    tables = (
        irrep_mixed[:, None],
        irrep_mixed[None, :],
        pos_mixed[:, None],
        pos_mixed[None, :],
        single_rows,
        occ_lanes,
    )

    part = pl.pallas_call(
        pair_kernel,
        in_specs=[smem, smem] + [vmem] * 7,
        out_specs=vmem,
        out_shape=jax.ShapeDtypeStruct((3, vir_total, MAIN), BF),
        scratch_shapes=[
            pltpu.VMEM((2 * GROUPS, vir_total, 2 * MAIN), BF),
            pltpu.VMEM((2, 2 * GROUPS, vir_total, 2 * MAIN), BF),
            pltpu.VMEM((GROUPS, vir_total, 4 * MAIN), BF),
            pltpu.VMEM((GROUPS, 2 * MAIN, vir_total), BF),
            pltpu.VMEM((GROUPS, 2 * MAIN, 2 * MAIN), BF),
        ],
        compiler_params=pltpu.CompilerParams(vmem_limit_bytes=LIMIT),
        name="ladder",
    )(own_irrep, pair_sym, got, *tables)
    part = part.reshape(3 * row_count, blk_count, MAIN).transpose(1, 0, 2)
    part = swap(part)
    summed = over_rep(jnp.sum(part.astype(F32), axis=0))
    summed = summed.reshape(3, row_count, MAIN)
    short = jnp.stack(
        [
            jnp.concatenate([summed[p], summed[2, :, p * 64 : p * 64 + REST]], axis=1)
            for p in range(2)
        ]
    )
    spread = (jnp.arange(RUN, dtype=I32)[:, None] == col_pos[None, :]).astype(F32)
    total = jnp.einsum("prj,jc->rpc", short, spread, precision=lax.Precision.HIGHEST)
    mask_rpc = amp_mask.transpose(1, 0, 2)
    amp_rpc = jnp.where(mask_rpc, amplitudes.transpose(1, 0, 2), 0.0)
    total = jnp.where(mask_rpc, total, 0.0)
    denominator = (
        (occ_energy[pair_first] + occ_energy[pair_second])[None, :, None]
        - row_energy[:, None, None]
        - col_energy[None, None, :]
    )
    residual = total + denominator * amp_rpc
    updated = amp_rpc - residual / denominator
    return (residual.transpose(1, 0, 2), updated.transpose(1, 0, 2))


def solution(mesh):
    in_specs = (
        P(None, "blk", "rep"),
        P(),
        P("rep", "blk", None),
        P("rep", None, "blk"),
        P(),
        P(),
        P(),
        P(),
        P(),
        P(),
    )
    out_specs = (P(None, "blk", "rep"), P(None, "blk", "rep"))
    return jax.shard_map(
        per_device, mesh=mesh, in_specs=in_specs, out_specs=out_specs, check_vma=False
    )
```

time: 141 us -> 130 us (0.922)
  starting transfers between devices: 42.2 us -> 29.3 us
  waiting for transfers between devices: 49.3 us -> 52.6 us
    all_to_all x2, waiting for transfers between devices: 14.7 us -> 48.6 us  [swap(): lax.all_to_all(value, 'blk', split_axis=0, concat_axis=0, tiled=False)]
    ppermute x9 -> x0, waiting for transfers between devices: 30.5 us -> none  [gather_blk(): lax.ppermute(held, 'blk', [(i, i ^ k << low) for i in range(blk_count)])]
    ppermute x9 -> x0, starting transfers between devices: 12.1 us -> none  [gather_blk(): lax.ppermute(held, 'blk', [(i, i ^ k << low) for i in range(blk_count)])]
    pallas_call x1, Pallas kernels: 9.15 us -> 6.53 us  [per_device(): pl.pallas_call(pack_kernel, grid_spec=pltpu.PrefetchScalarGridSpec(num_sc...]
    pallas_call x1 -> x2, Pallas kernels: 14.6 us -> 16.8 us  [the longest x1 14 us: per_device(): pl.pallas_call(pair_kernel, in_specs=[smem, smem] + [vmem] * 7, out_specs...]
    unnamed x22 -> x26, local copies, waits for them, and re-layouts: 4.45 us -> 5.12 us
  transfers between devices with their start and end apart: 17 -> 8, of which waited for: 8 -> 4; matrix products, arithmetic and copies ran while one was open for 7% -> 10% of each run, Pallas kernels for 0% -> 5%
where the time goes in v3:
time: 130 us
  waiting for transfers between devices  52.6 us (40%)
  starting transfers between devices  29.3 us (23%)
  Pallas kernels  23.3 us (18%)
  local copies, waits for them, and re-layouts  18.5 us (14%)
  other arithmetic  4.82 us (4%)
    all_to_all x2, waiting for transfers between devices, swap(): lax.all_to_all(value, 'blk', split_axis=0, concat_axis=0, tiled=False)  48.6 us
    all_to_all x2, starting transfers between devices, swap(): lax.all_to_all(value, 'blk', split_axis=0, concat_axis=0, tiled=False)  20.7 us
    pallas_call x1, Pallas kernels, per_device(): pl.pallas_call(pair_kernel, in_specs=[smem, smem] + [vmem] * 7, out_specs...  14 us
    ppermute x6, starting transfers between devices, over_rep(): lax.ppermute(value, 'rep', [(i, (i + k) % 4) for i in range(4)])  8.64 us
    pallas_call x1, Pallas kernels, per_device(): pl.pallas_call(pack_kernel, grid_spec=pltpu.PrefetchScalarGridSpec(num_sc...  6.53 us
    unnamed x26, local copies, waits for them, and re-layouts  5.12 us
    ppermute x6, waiting for transfers between devices, over_rep(): lax.ppermute(value, 'rep', [(i, (i + k) % 4) for i in range(4)])  4.05 us
    pallas_call x1, Pallas kernels, per_device(): pl.pallas_call(amp_kernel, grid_spec=pltpu.PrefetchScalarGridSpec(num_sca...  2.72 us
  transfers between devices with their start and end apart: 8, of which 4 were waited for; matrix products, arithmetic and copies ran while one was open for 10% of the time, Pallas kernels for 5%

profile of v3, /device:TPU:6, one launch (start us, length us, event | category | flops | bytes accessed | tf_op | source)
XLA Modules:
  0.0 129.6 jit_solution(7405594740696821819)
XLA Ops:
  0.6 1.3 %broadcast_in_dim.44.vir_irrep = s32[1,640]{1,0:T(1,128)} reshape(s32[640]{0:T(1024)} %vir_s.3) | data formatting | bytes 5120 | tf_op jit(solution)/shard_map/broadcast_in_dim | solution.py:224
  1.9 2.7 %amp.1 = f32[3,10,128]{2,1,0:T(8,128)} custom-call(s32[640]{0:T(1024)} %vir_s.3, s32[100]{0:T(128)} %occ_s.3, s32[2,2]{1,0:T(2,128)} %pair_s.3, f32[10,2,160]{2,1,0:T(2,128)} %bitcast.45, s32[1,640]{1,0:T(1,128)} %broadcast_in_dim.44.vir_irrep), custom_call_target="tpu_custom_call" | custom-call | tf_op jit(solution)/shard_map/amp/pallas_call | solution.py:225
  4.7 3.0 %collective-permute-start.2 = (f32[3,10,128]{2,1,0:T(8,128)}, f32[3,10,128]{2,1,0:T(8,128)S(1)}, u32[]{:S(2)}, u32[]{:S(2)}) collective-permute-start(f32[3,10,128]{2,1,0:T(8,128)} %amp.1), channel_id=1, source_target_pairs={{0,3},{1,0},{2,1},{3,2},{4,7},{5,4},{6,5},{7,6},{8,11},{9,8},{10,9... | collective-permute-start | bytes 46088 | tf_op jit(solution)/shard_map/ppermute | solution.py:201
  7.7 0.6 collective-permute-start.1
  8.3 1.0 collective-permute-start
  9.3 0.7 broadcast_in_dim.72.chol_irrep
  10.0 0.7 copy-done.1
  10.6 1.1 copy-done.3
  11.8 0.7 copy-done.4
  12.5 0.7 copy-done.6
  13.2 0.7 copy-done.7
  13.8 6.5 %pack.1 = bf16[8,10,64,128]{3,2,1,0:T(8,128)(2,1)S(1)} custom-call(s32[640]{0:T(1024)S(1)} %copy-done.4, s32[100]{0:T(128)S(1)} %copy-done.1, s32[2,2]{1,0:T(2,128)S(1)} %copy-done.7, bf16[10,384,640]{2,1,0:T(8,128)(2,1)} %bitcast.43, bf16[10,100,384]{2,1,0:T(8,128)(2,1)S(1)} %bitcast.40, s32[1,640]{1,0:T(1,128)S(1)} %copy-done.6, ...), custom_call_target="tpu_custom_call" | custom-call | flops 1258291200 | bytes 4915200 | tf_op jit(solution)/shard_map/pack/pallas_call | solution.py:242
  20.4 0.8 copy.69
  21.4 1.4 %pad_maximum_fusion = bf16[64,110,128]{2,1,0:T(8,128)(2,1)} fusion(bf16[64,30,128]{2,1,0:T(8,128)(2,1)S(1)} %broadcast_in_dim.74, bf16[64,80,128]{2,1,0:T(8,128)(2,1)S(1)} %bitcast.42), kind=kLoop, calls=%fused_computation.6 | loop fusion | flops 3604480 | bytes 3604480 | tf_op jit(solution)/shard_map/concatenate | solution.py:283
  22.8 12.3 %all-to-all-start = ((bf16[64,110,128]{2,1,0:T(8,128)(2,1)}), bf16[64,110,128]{2,1,0:T(8,128)(2,1)S(1)}, u32[]{:S(2)}, u32[]{:S(2)}) async-start(bf16[64,110,128]{2,1,0:T(8,128)(2,1)} %pad_maximum_fusion), calls=%async_computation | async-start | bytes 3670016 | tf_op jit(solution)/shard_map/all_to_all | solution.py:280
  35.1 0.1 reshape.188
  35.3 0.3 broadcast_in_dim_reshape.17.row_irrep
  35.7 0.1 convert_reduce_fusion.1
  35.9 0.1 reduce_sum.31
  36.1 0.3 broadcast_in_dim_reshape.18.row_pos
  36.6 0.2 fusion.10
  36.8 0.6 gather_fusion
  37.4 0.6 gather_fusion.1
  38.1 0.8 dynamic_slice.24
  38.9 0.6 gather_fusion.2
  39.6 0.6 gather_fusion.3
  40.1 0.2 gather.24
  40.6 0.2 dynamic-slice_reduce_fusion.q_irrep
  40.8 0.7 fusion.14
  41.5 2.6 %compare_select_fusion.4.occ_lanes = s32[1,256]{1,0:T(1,128)S(1)} fusion(s32[]{:T(128)} %bitcast.14, s32[]{:T(128)} %bitcast.13, s32[]{:T(128)} %bitcast.12, s32[]{:T(128)} %bitcast.11), kind=kLoop, calls=%fused_computation.44 | loop fusion | flops 1536 | bytes 1040 | tf_op jit(solution)/shard_map/jit(_where)/select_n | solution.py:329
  44.1 34.1 %all-to-all-done = bf16[64,110,128]{2,1,0:T(8,128)(2,1)S(1)} async-done(((bf16[64,110,128]{2,1,0:T(8,128)(2,1)}), bf16[64,110,128]{2,1,0:T(8,128)(2,1)S(1)}, u32[]{:S(2)}, u32[]{:S(2)}) %all-to-all-start) | async-done | bytes 1802272 | tf_op jit(solution)/shard_map/all_to_all | solution.py:280
  78.2 0.5 copy.50
  78.7 14.0 %ladder.1 = bf16[3,640,128]{2,1,0:T(8,128)(2,1)S(1)} custom-call(s32[6]{0:T(128)S(1)} %dynamic-slice_reduce_fusion.q_irrep, s32[2]{0:T(128)S(1)} %xor.24.pair_sym, bf16[11,640,128]{2,1,0:T(8,128)(2,1)S(1)} %bitcast.37, s32[640,1]{1,0:T(8,128)S(1)} %broadcast_in_dim_reshape.17.row_irrep, s32[1,640]{1,0:T(1,128)S(1)} %broadcast_in_dim_reshape.14.col_irrep, ...), custom_call_target="tpu_custom_call" | custom-call | tf_op jit(solution)/shard_map/ladder/pallas_call | solution.py:349
  92.7 1.1 copy.70
  93.9 8.4 %all-to-all-start.1 = ((bf16[64,30,128]{2,1,0:T(8,128)(2,1)}), bf16[64,30,128]{2,1,0:T(8,128)(2,1)S(1)}, u32[]{:S(2)}, u32[]{:S(2)}) async-start(bf16[64,30,128]{2,1,0:T(8,128)(2,1)} %bitcast.36), calls=%async_computation.1 | async-start | bytes 1048576 | tf_op jit(solution)/shard_map/all_to_all | solution.py:280
  102.3 0.6 gather_fusion.4
  102.9 0.6 gather_fusion.5
  103.6 0.8 dynamic_slice.27
  104.5 14.4 %all-to-all-done.1 = bf16[64,30,128]{2,1,0:T(8,128)(2,1)S(1)} async-done(((bf16[64,30,128]{2,1,0:T(8,128)(2,1)}), bf16[64,30,128]{2,1,0:T(8,128)(2,1)S(1)}, u32[]{:S(2)}, u32[]{:S(2)}) %all-to-all-start.1) | async-done | bytes 491552 | tf_op jit(solution)/shard_map/all_to_all | solution.py:280
  119.0 0.1 convert_reduce_fusion
  119.1 2.3 %collective-permute-start.5 = (f32[30,128]{1,0:T(8,128)S(1)}, f32[30,128]{1,0:T(8,128)S(1)}, u32[]{:S(2)}, u32[]{:S(2)}) collective-permute-start(f32[30,128]{1,0:T(8,128)S(1)} %convert_reduce_fusion), channel_id=1, source_target_pairs={{0,3},{1,0},{2,1},{3,2},{4,7},{5,4},{6,5},{7,6},{8,11},{9,8},{10,9... | collective-permute-start | bytes 46088 | tf_op jit(solution)/shard_map/ppermute | solution.py:201
  121.4 1.7 %collective-permute-start.4 = (f32[30,128]{1,0:T(8,128)S(1)}, f32[30,128]{1,0:T(8,128)S(1)}, u32[]{:S(2)}, u32[]{:S(2)}) collective-permute-start(f32[30,128]{1,0:T(8,128)S(1)} %convert_reduce_fusion), channel_id=1, source_target_pairs={{0,2},{1,3},{2,0},{3,1},{4,6},{5,7},{6,4},{7,5},{8,10},{9,11},{10,... | collective-permute-start | bytes 46088 | tf_op jit(solution)/shard_map/ppermute | solution.py:201
  123.2 0.8 dynamic_slice.28
  124.0 2.6 %collective-permute-done.4 = f32[30,128]{1,0:T(8,128)S(1)} collective-permute-done((f32[30,128]{1,0:T(8,128)S(1)}, f32[30,128]{1,0:T(8,128)S(1)}, u32[]{:S(2)}, u32[]{:S(2)}) %collective-permute-start.4) | collective-permute-done | bytes 15392 | tf_op jit(solution)/shard_map/ppermute | solution.py:201
  126.7 1.4 %collective-permute-done.3 = f32[30,128]{1,0:T(8,128)S(1)} collective-permute-done((f32[30,128]{1,0:T(8,128)S(1)}, f32[30,128]{1,0:T(8,128)S(1)}, u32[]{:S(2)}, u32[]{:S(2)}) %collective-permute-start.3) | collective-permute-done | bytes 15392 | tf_op jit(solution)/shard_map/ppermute | solution.py:201
  128.2 0.2 fusion.5
  128.4 0.6 copy.60
  129.0 0.6 copy.61
  (56 shorter events, 1.5 us)
Async XLA Ops:
  0.6 38.9 %copy-start = (bf16[100,640]{1,0:T(8,128)(2,1)S(1)}, bf16[100,640]{1,0:T(8,128)(2,1)}, u32[]{:S(2)}) copy-start(bf16[100,640]{1,0:T(8,128)(2,1)} %param.11) | copy-start | bytes 384004
  4.7 16.6 %collective-permute-start.2 = (f32[3,10,128]{2,1,0:T(8,128)}, f32[3,10,128]{2,1,0:T(8,128)S(1)}, u32[]{:S(2)}, u32[]{:S(2)}) collective-permute-start(f32[3,10,128]{2,1,0:T(8,128)} %amp.1), channel_id=1, source_target_pairs={{0,3},{1,0},{2,1},{3,2},{4,7},{5,4},{6,5},{7,6},{8,11},{9,8},{10,9... | collective-permute-start | bytes 46088 | tf_op jit(solution)/shard_map/ppermute | solution.py:201
  7.7 13.6 %collective-permute-start.1 = (f32[3,10,128]{2,1,0:T(8,128)}, f32[3,10,128]{2,1,0:T(8,128)S(1)}, u32[]{:S(2)}, u32[]{:S(2)}) collective-permute-start(f32[3,10,128]{2,1,0:T(8,128)} %amp.1), channel_id=1, source_target_pairs={{0,2},{1,3},{2,0},{3,1},{4,6},{5,7},{6,4},{7,5},{8,10},{9,11},{10,... | collective-permute-start | bytes 46088 | tf_op jit(solution)/shard_map/ppermute | solution.py:201
  8.3 12.9 %collective-permute-start = (f32[3,10,128]{2,1,0:T(8,128)}, f32[3,10,128]{2,1,0:T(8,128)S(1)}, u32[]{:S(2)}, u32[]{:S(2)}) collective-permute-start(f32[3,10,128]{2,1,0:T(8,128)} %amp.1), channel_id=1, source_target_pairs={{0,1},{1,2},{2,3},{3,0},{4,5},{5,6},{6,7},{7,4},{8,9},{9,10},{10,1... | collective-permute-start | bytes 46088 | tf_op jit(solution)/shard_map/ppermute | solution.py:201
  10.0 0.7 copy-start.1
  10.6 1.1 copy-start.3
  11.8 0.7 copy-start.4
  12.5 0.7 copy-start.6
  13.2 0.7 copy-start.7
  20.4 0.9 copy-start.10
  22.8 12.3 %copy-start.5 = (s32[640]{0:T(1024)S(1)}, s32[640]{0:T(1024)}, u32[]{:S(2)}) copy-start(s32[640]{0:T(1024)} %vir_s.3) | copy-start | bytes 7684
  22.8 13.7 %copy-start.8 = (s32[2,2]{1,0:T(2,128)S(1)}, s32[2,2]{1,0:T(2,128)}, u32[]{:S(2)}) copy-start(s32[2,2]{1,0:T(2,128)} %pair_s.3) | copy-start | bytes 52
  22.8 14.0 %copy-start.2 = (s32[100]{0:T(128)S(1)}, s32[100]{0:T(128)}, u32[]{:S(2)}) copy-start(s32[100]{0:T(128)} %occ_s.3) | copy-start | bytes 1204
  22.8 55.4 %all-to-all-start = ((bf16[64,110,128]{2,1,0:T(8,128)(2,1)}), bf16[64,110,128]{2,1,0:T(8,128)(2,1)S(1)}, u32[]{:S(2)}, u32[]{:S(2)}) async-start(bf16[64,110,128]{2,1,0:T(8,128)(2,1)} %pad_maximum_fusion), calls=%async_computation | async-start | bytes 3670016 | tf_op jit(solution)/shard_map/all_to_all | solution.py:280
  78.7 23.6 %copy-start.9 = (f32[100]{0:T(128)S(1)}, f32[100]{0:T(128)}, u32[]{:S(2)}) copy-start(f32[100]{0:T(128)} %param.14) | copy-start | bytes 1204
  92.7 35.5 %copy-start.11 = (f32[2,10,160]{2,0,1:T(2,128)S(1)}, f32[2,10,160]{2,0,1:T(2,128)}, u32[]{:S(2)}) copy-start(f32[2,10,160]{2,0,1:T(2,128)} %param.10) | copy-start | bytes 38404
  93.9 25.1 %all-to-all-start.1 = ((bf16[64,30,128]{2,1,0:T(8,128)(2,1)}), bf16[64,30,128]{2,1,0:T(8,128)(2,1)S(1)}, u32[]{:S(2)}, u32[]{:S(2)}) async-start(bf16[64,30,128]{2,1,0:T(8,128)(2,1)} %bitcast.36), calls=%async_computation.1 | async-start | bytes 1048576 | tf_op jit(solution)/shard_map/all_to_all | solution.py:280
  119.1 4.9 %collective-permute-start.5 = (f32[30,128]{1,0:T(8,128)S(1)}, f32[30,128]{1,0:T(8,128)S(1)}, u32[]{:S(2)}, u32[]{:S(2)}) collective-permute-start(f32[30,128]{1,0:T(8,128)S(1)} %convert_reduce_fusion), channel_id=1, source_target_pairs={{0,3},{1,0},{2,1},{3,2},{4,7},{5,4},{6,5},{7,6},{8,11},{9,8},{10,9... | collective-permute-start | bytes 46088 | tf_op jit(solution)/shard_map/ppermute | solution.py:201
  121.4 5.2 %collective-permute-start.4 = (f32[30,128]{1,0:T(8,128)S(1)}, f32[30,128]{1,0:T(8,128)S(1)}, u32[]{:S(2)}, u32[]{:S(2)}) collective-permute-start(f32[30,128]{1,0:T(8,128)S(1)} %convert_reduce_fusion), channel_id=1, source_target_pairs={{0,2},{1,3},{2,0},{3,1},{4,6},{5,7},{6,4},{7,5},{8,10},{9,11},{10,... | collective-permute-start | bytes 46088 | tf_op jit(solution)/shard_map/ppermute | solution.py:201
  123.1 4.9 %collective-permute-start.3 = (f32[30,128]{1,0:T(8,128)S(1)}, f32[30,128]{1,0:T(8,128)S(1)}, u32[]{:S(2)}, u32[]{:S(2)}) collective-permute-start(f32[30,128]{1,0:T(8,128)S(1)} %convert_reduce_fusion), channel_id=1, source_target_pairs={{0,1},{1,2},{2,3},{3,0},{4,5},{5,6},{6,7},{7,4},{8,9},{9,10},{10,1... | collective-permute-start | bytes 46088 | tf_op jit(solution)/shard_map/ppermute | solution.py:201

commit v4 on v3

--- a/solution.py
+++ b/solution.py
@@ -34,17 +34,18 @@
     vir_s, occ_s, pair_s, chol, ov, vir_irrep, chol_irrep, out, fold, labels, pick
 ):
     step = pl.program_id(0)
+    vir_line = vir_irrep[...][None, :]
     rows, q_local, vir_total = chol.shape
     occ_total = ov.shape[1]
     own = out.shape[2]
 
     @pl.when(step == 0)
     def _():
-        place = run_positions(vir_irrep[...])
+        place = run_positions(vir_line)
         row = lax.broadcasted_iota(I32, (2 * MAIN, vir_total), 0)
         fold[...] = jnp.where(row == place, 1.0, 0.0).T.astype(BF)
         first = pl.multiple_of(lax.axis_index("rep") * q_local, MAIN)
-        mine = chol_irrep[:, pl.ds(first, q_local)].astype(F32)
+        mine = chol_irrep[pl.ds(first, q_local)][None, :].astype(F32)
         labels[...] = jnp.broadcast_to(mine, (MAIN, q_local)).T.astype(I32)
         row = lax.broadcasted_iota(I32, (occ_total, MAIN), 0)
         lane = lax.broadcasted_iota(I32, (occ_total, MAIN), 1)
@@ -61,7 +62,7 @@
     first_row = (lax.axis_index("blk") * pl.num_programs(0) + step) * rows
     wants = [jnp.bitwise_xor(labels[...], vir_s[first_row + k]) for k in range(rows)]
     kept = [
-        jnp.where(wants[k][:, :1] == vir_irrep[...], chol[k].astype(F32), 0.0).astype(BF)
+        jnp.where(wants[k][:, :1] == vir_line, chol[k].astype(F32), 0.0).astype(BF)
         for k in range(rows)
     ]
     folded = dot(jnp.concatenate(kept, axis=0), fold[...])
@@ -85,12 +86,13 @@
     row_count, pair_count, col_count = amp.shape
     rep_pos = lax.axis_index("rep")
     first_row = lax.axis_index("blk") * row_count
-    place = run_positions(vir_irrep[...])
-    col_irrep = vir_irrep[:, :col_count]
+    vir_line = vir_irrep[...][None, :]
+    place = run_positions(vir_line)
+    col_irrep = vir_line[:, :col_count]
     col_place = place[:, :col_count]
     for k in range(1, 4):
         cols = slice(k * col_count, (k + 1) * col_count)
-        col_irrep = jnp.where(rep_pos == k, vir_irrep[:, cols], col_irrep)
+        col_irrep = jnp.where(rep_pos == k, vir_line[:, cols], col_irrep)
         col_place = jnp.where(rep_pos == k, place[:, cols], col_place)
     lane = lax.broadcasted_iota(I32, (2 * MAIN, col_count), 0)
     fold = jnp.where(lane == col_place, 1.0, 0.0).astype(BF)
@@ -164,26 +166,23 @@
         halfway = dot(wide, amps[g])
         dressed = lax.dot_general(bc, weight[g], NT, preferred_element_type=F32)
         dressed = jnp.where(want == occ_lanes[...], dressed, 0.0)
-        ball[q, :, :MAIN] = bc[:, :MAIN]
-        ball[q, :, MAIN:] = (bc[:, MAIN:].astype(F32) + dressed[:, :MAIN]).astype(BF)
+        ball[:, q * 256 : q * 256 + MAIN] = bc[:, :MAIN]
+        ball[:, q * 256 + MAIN : (q + 1) * 256] = (bc[:, MAIN:].astype(F32) + dressed[:, :MAIN]).astype(BF)
         for p in range(2):
-            hall[p, q, :, :MAIN] = halfway[:, p * 256 : p * 256 + MAIN].astype(BF)
+            hall[p, :, q * 256 : q * 256 + MAIN] = halfway[:, p * 256 : p * 256 + MAIN].astype(BF)
             own = jnp.where(lane == CYCLE_LANE + p, dressed[:, MAIN:], 0.0)
-            hall[p, q, :, MAIN:] = (
+            hall[p, :, q * 256 + MAIN : (q + 1) * 256] = (
                 halfway[:, p * 256 + MAIN : (p + 1) * 256] + own
             ).astype(BF)
         return carry
 
-    lax.fori_loop(0, 2 * GROUPS, one, 0)
+    for q in range(2 * GROUPS):
+        one(q, 0)
 
     lane2 = lax.broadcasted_iota(I32, (vir_total, 2 * MAIN), 1)
     tail = None
     for p in range(2):
-        value = lax.dot_general(hall[p, 0], ball[0], NT, preferred_element_type=F32)
-        for q in range(1, 2 * GROUPS):
-            value = value + lax.dot_general(
-                hall[p, q], ball[q], NT, preferred_element_type=F32
-            )
+        value = lax.dot_general(hall[p], ball[...], NT, preferred_element_type=F32)
         want = jnp.bitwise_xor(row_irrep[...], pair_sym[p])
         value = jnp.where(want == col_irrep[...], value, 0.0).astype(BF)
         place = row_pos[...]
@@ -221,7 +220,6 @@
     blk_count = vir_total // row_count
     q_own = q_local // blk_count
     occ_total = chol_ov.shape[1]
-    vir_line = vir_irrep[None, :]
     amp_send = pl.pallas_call(
         amp_kernel,
         grid_spec=pltpu.PrefetchScalarGridSpec(
@@ -229,13 +227,13 @@
             grid=(1,),
             in_specs=[
                 pl.BlockSpec((row_count, 2, col_count), lambda i, *s: (0, 0, 0)),
-                pl.BlockSpec((1, vir_total), lambda i, *s: (0, 0)),
+                pl.BlockSpec((vir_total,), lambda i, *s: (0,)),
             ],
             out_specs=pl.BlockSpec((3, row_count, MAIN), lambda i, *s: (0, 0, 0)),
         ),
         out_shape=jax.ShapeDtypeStruct((3, row_count, MAIN), F32),
         name="amp",
-    )(vir_irrep, occ_irrep, pair_list, amplitudes.transpose(1, 0, 2), vir_line)
+    )(vir_irrep, occ_irrep, pair_list, amplitudes.transpose(1, 0, 2), vir_irrep)
     amp_send = over_rep(amp_send).astype(BF).reshape(3 * row_count, MAIN)
 
     rows = 2
@@ -247,8 +245,8 @@
             in_specs=[
                 pl.BlockSpec((rows, q_local, vir_total), lambda i, *s: (i, 0, 0)),
                 pl.BlockSpec((rows, occ_total, q_local), lambda i, *s: (i, 0, 0)),
-                pl.BlockSpec((1, vir_total), lambda i, *s: (0, 0)),
-                pl.BlockSpec((1, chol_irrep.shape[0]), lambda i, *s: (0, 0)),
+                pl.BlockSpec((vir_total,), lambda i, *s: (0,)),
+                pl.BlockSpec(chol_irrep.shape, lambda i, *s: (0,)),
             ],
             out_specs=pl.BlockSpec((8, rows, blk_count, MAIN), lambda i, *s: (0, i, 0, 0)),
             scratch_shapes=[
@@ -258,7 +256,6 @@
             ],
         ),
         out_shape=jax.ShapeDtypeStruct((8, row_count, blk_count, MAIN), BF),
-        compiler_params=pltpu.CompilerParams(vmem_limit_bytes=LIMIT),
         cost_estimate=pl.CostEstimate(
             flops=2 * q_local * row_count * vir_total * 256,
             bytes_accessed=2 * q_local * row_count * vir_total,
@@ -271,8 +268,8 @@
         pair_list,
         chol_vv.transpose(1, 0, 2),
         chol_ov.transpose(2, 1, 0),
-        vir_line,
-        chol_irrep[None, :],
+        vir_irrep,
+        chol_irrep,
     )
     packed = packed.reshape(8 * row_count, blk_count, MAIN).transpose(1, 0, 2)
 
@@ -352,8 +349,8 @@
         out_specs=vmem,
         out_shape=jax.ShapeDtypeStruct((3, vir_total, MAIN), BF),
         scratch_shapes=[
-            pltpu.VMEM((2 * GROUPS, vir_total, 2 * MAIN), BF),
-            pltpu.VMEM((2, 2 * GROUPS, vir_total, 2 * MAIN), BF),
+            pltpu.VMEM((vir_total, 4 * GROUPS * MAIN), BF),
+            pltpu.VMEM((2, vir_total, 4 * GROUPS * MAIN), BF),
             pltpu.VMEM((GROUPS, vir_total, 4 * MAIN), BF),
             pltpu.VMEM((GROUPS, 2 * MAIN, vir_total), BF),
             pltpu.VMEM((GROUPS, 2 * MAIN, 2 * MAIN), BF),
@@ -373,6 +370,7 @@
     )
     spread = (jnp.arange(RUN, dtype=I32)[:, None] == col_pos[None, :]).astype(F32)
     total = jnp.einsum("prj,jc->rpc", short, spread, precision=lax.Precision.HIGHEST)
+    total = lax.optimization_barrier(total)
     mask_rpc = amp_mask.transpose(1, 0, 2)
     amp_rpc = jnp.where(mask_rpc, amplitudes.transpose(1, 0, 2), 0.0)
     total = jnp.where(mask_rpc, total, 0.0)

time: 130 us -> 123 us (0.946)
  local copies, waits for them, and re-layouts: 18.5 us -> 12.7 us
  Pallas kernels: 23.3 us -> 21.2 us
    unnamed x26 -> x14, local copies, waits for them, and re-layouts: 5.12 us -> 0.04 us
    pallas_call x1, Pallas kernels: 14 us -> 10.8 us  [per_device(): pl.pallas_call(pair_kernel, in_specs=[smem, smem] + [vmem] * 7, out_specs...]
    broadcast_in_dim x2 -> x0, local copies, waits for them, and re-layouts: 2 us -> none  [the longest x1 1.3 us: per_device(): vir_line = vir_irrep[None, :]]
    reshape x1, local copies, waits for them, and re-layouts: 0.85 us -> 2.17 us  [per_device(): packed = packed.reshape(8 * row_count, blk_count, MAIN).transpose(1, 0, 2)]
  transfers between devices with their start and end apart: 8 -> 8, of which waited for: 4 -> 4; matrix products, arithmetic and copies ran while one was open for 10% -> 12% of each run, Pallas kernels for 5% -> 6%
where the time goes in v4:
time: 123 us
  waiting for transfers between devices  52.7 us (43%)
  starting transfers between devices  29.3 us (24%)
  Pallas kernels  21.2 us (17%)
  local copies, waits for them, and re-layouts  12.7 us (10%)
  other arithmetic  5.47 us (4%)
    all_to_all x2, waiting for transfers between devices, swap(): lax.all_to_all(value, 'blk', split_axis=0, concat_axis=0, tiled=False)  48.5 us
    all_to_all x2, starting transfers between devices, swap(): lax.all_to_all(value, 'blk', split_axis=0, concat_axis=0, tiled=False)  20.7 us
    pallas_call x1, Pallas kernels, per_device(): pl.pallas_call(pair_kernel, in_specs=[smem, smem] + [vmem] * 7, out_specs...  10.8 us
    ppermute x6, starting transfers between devices, over_rep(): lax.ppermute(value, 'rep', [(i, (i + k) % 4) for i in range(4)])  8.64 us
    pallas_call x1, Pallas kernels, per_device(): pl.pallas_call(pack_kernel, grid_spec=pltpu.PrefetchScalarGridSpec(num_sc...  7.61 us
    ppermute x6, waiting for transfers between devices, over_rep(): lax.ppermute(value, 'rep', [(i, (i + k) % 4) for i in range(4)])  4.12 us
    pallas_call x1, Pallas kernels, per_device(): pl.pallas_call(amp_kernel, grid_spec=pltpu.PrefetchScalarGridSpec(num_sca...  2.83 us
    select_n x1, other arithmetic, per_device(): jnp.where(lane_row == first, occ_labels[1], jnp.where(lane_row == first +...  2.55 us
  transfers between devices with their start and end apart: 8, of which 4 were waited for; matrix products, arithmetic and copies ran while one was open for 12% of the time, Pallas kernels for 6%

profile of v4, /device:TPU:6, one launch (start us, length us, event | category | flops | bytes accessed | tf_op | source)
XLA Modules:
  0.0 122.5 jit_solution(7304295111297487627)
XLA Ops:
  0.6 2.8 %amp.1 = f32[3,10,128]{2,1,0:T(8,128)} custom-call(s32[640]{0:T(1024)} %vir_irrep.3, s32[100]{0:T(128)} %occ_s.3, s32[2,2]{1,0:T(2,128)} %pair_s.3, f32[10,2,160]{2,1,0:T(2,128)} %bitcast.52, s32[640]{0:T(1024)} %vir_irrep.3), custom_call_target="tpu_custom_call" | custom-call | tf_op jit(solution)/shard_map/amp/pallas_call | solution.py:223
  3.5 3.0 %collective-permute-start.2 = (f32[3,10,128]{2,1,0:T(8,128)}, f32[3,10,128]{2,1,0:T(8,128)S(1)}, u32[]{:S(2)}, u32[]{:S(2)}) collective-permute-start(f32[3,10,128]{2,1,0:T(8,128)} %amp.1), channel_id=1, source_target_pairs={{0,3},{1,0},{2,1},{3,2},{4,7},{5,4},{6,5},{7,6},{8,11},{9,8},{10,9... | collective-permute-start | bytes 46088 | tf_op jit(solution)/shard_map/ppermute | solution.py:200
  6.5 0.6 collective-permute-start.1
  7.1 1.0 collective-permute-start
  8.1 7.6 %pack.1 = bf16[8,10,64,128]{3,2,1,0:T(8,128)(2,1)} custom-call(s32[640]{0:T(1024)} %vir_irrep.3, s32[100]{0:T(128)} %occ_s.3, s32[2,2]{1,0:T(2,128)} %pair_s.3, bf16[10,384,640]{2,1,0:T(8,128)(2,1)} %bitcast.49, bf16[10,100,384]{2,1,0:T(8,128)(2,1)} %bitcast.50, s32[640]{0:T(1024)} %vir_irrep.3, s32[1536]{0:T(1024)} %chol_irrep.1), custom_call_target="tpu_custom_call" | custom-call | flops 1258291200 | bytes 4915200 | tf_op jit(solution)/shard_map/pack/pallas_call | solution.py:240
  15.7 2.2 %copy.55 = bf16[80,64,128]{2,0,1:T(8,128)(2,1)S(1)} copy(bf16[80,64,128]{2,1,0:T(8,128)(2,1)} %bitcast.48) | data formatting | bytes 2621440 | tf_op jit(solution)/shard_map/reshape | solution.py:274
  18.0 1.4 %pad_maximum_fusion = bf16[64,110,128]{2,1,0:T(8,128)(2,1)} fusion(bf16[64,30,128]{2,1,0:T(8,128)(2,1)S(1)} %broadcast_in_dim.68, bf16[64,80,128]{2,1,0:T(8,128)(2,1)S(1)} %bitcast.47), kind=kLoop, calls=%fused_computation.6 | loop fusion | flops 3604480 | bytes 3604480 | tf_op jit(solution)/shard_map/concatenate | solution.py:280
  19.4 12.3 %all-to-all-start = ((bf16[64,110,128]{2,1,0:T(8,128)(2,1)}), bf16[64,110,128]{2,1,0:T(8,128)(2,1)S(1)}, u32[]{:S(2)}, u32[]{:S(2)}) async-start(bf16[64,110,128]{2,1,0:T(8,128)(2,1)} %pad_maximum_fusion), calls=%async_computation | async-start | bytes 3670016 | tf_op jit(solution)/shard_map/all_to_all | solution.py:277
  31.8 0.1 reshape.188
  32.0 0.3 broadcast_in_dim_reshape.17.row_irrep
  32.3 0.1 broadcast_in_dim_reshape.14.col_irrep
  32.3 0.1 convert_reduce_fusion.1
  32.5 0.1 select_reduce_fusion
  32.6 0.1 reduce_sum.31
  32.8 0.3 broadcast_in_dim_reshape.18.row_pos
  33.1 0.1 broadcast_in_dim_reshape.16.col_pos
  33.1 0.1 reshape.189
  33.2 0.2 fusion.12
  33.4 0.6 gather_fusion
  34.1 0.6 gather_fusion.1
  34.7 0.8 dynamic_slice.25
  35.5 0.1 reshape.186
  35.6 0.6 gather_fusion.2
  36.2 0.6 gather_fusion.3
  36.8 0.2 gather.24
  36.9 0.1 fusion.4
  37.0 0.1 copy.47
  37.2 0.1 reshape.190
  37.2 0.2 dynamic-slice_reduce_fusion.q_irrep
  37.4 0.7 fusion.17
  38.1 2.5 %compare_select_fusion.5.occ_lanes = s32[1,256]{1,0:T(1,128)S(1)} fusion(s32[]{:T(128)} %bitcast.15, s32[]{:T(128)} %bitcast.14, s32[]{:T(128)} %bitcast.13, s32[]{:T(128)} %bitcast.12), kind=kLoop, calls=%fused_computation.48 | loop fusion | flops 1536 | bytes 1040 | tf_op jit(solution)/shard_map/jit(_where)/select_n | solution.py:326
  40.7 34.2 %all-to-all-done = bf16[64,110,128]{2,1,0:T(8,128)(2,1)S(1)} async-done(((bf16[64,110,128]{2,1,0:T(8,128)(2,1)}), bf16[64,110,128]{2,1,0:T(8,128)(2,1)S(1)}, u32[]{:S(2)}, u32[]{:S(2)}) %all-to-all-start) | async-done | bytes 1802272 | tf_op jit(solution)/shard_map/all_to_all | solution.py:277
  74.8 0.5 copy.42
  75.3 10.8 %ladder.1 = bf16[3,640,128]{2,1,0:T(8,128)(2,1)S(1)} custom-call(s32[6]{0:T(128)S(1)} %dynamic-slice_reduce_fusion.q_irrep, s32[2]{0:T(128)S(1)} %xor.24.pair_sym, bf16[11,640,128]{2,1,0:T(8,128)(2,1)S(1)} %bitcast.44, s32[640,1]{1,0:T(8,128)S(1)} %broadcast_in_dim_reshape.17.row_irrep, s32[1,640]{1,0:T(1,128)S(1)} %broadcast_in_dim_reshape.14.col_irrep, ...), custom_call_target="tpu_custom_call" | custom-call | tf_op jit(solution)/shard_map/ladder/pallas_call | solution.py:346
  86.2 1.1 copy.56
  87.3 8.4 %all-to-all-start.1 = ((bf16[64,30,128]{2,1,0:T(8,128)(2,1)}), bf16[64,30,128]{2,1,0:T(8,128)(2,1)S(1)}, u32[]{:S(2)}, u32[]{:S(2)}) async-start(bf16[64,30,128]{2,1,0:T(8,128)(2,1)} %bitcast.42), calls=%async_computation.1 | async-start | bytes 1048576 | tf_op jit(solution)/shard_map/all_to_all | solution.py:277
  95.7 0.6 gather_fusion.4
  96.3 0.6 gather_fusion.5
  97.0 0.8 dynamic_slice.27
  98.0 14.4 %all-to-all-done.1 = bf16[64,30,128]{2,1,0:T(8,128)(2,1)S(1)} async-done(((bf16[64,30,128]{2,1,0:T(8,128)(2,1)}), bf16[64,30,128]{2,1,0:T(8,128)(2,1)S(1)}, u32[]{:S(2)}, u32[]{:S(2)}) %all-to-all-start.1) | async-done | bytes 491552 | tf_op jit(solution)/shard_map/all_to_all | solution.py:277
  112.4 0.1 convert_reduce_fusion
  112.5 2.3 %collective-permute-start.5 = (f32[30,128]{1,0:T(8,128)S(1)}, f32[30,128]{1,0:T(8,128)S(1)}, u32[]{:S(2)}, u32[]{:S(2)}) collective-permute-start(f32[30,128]{1,0:T(8,128)S(1)} %convert_reduce_fusion), channel_id=1, source_target_pairs={{0,3},{1,0},{2,1},{3,2},{4,7},{5,4},{6,5},{7,6},{8,11},{9,8},{10,9... | collective-permute-start | bytes 46088 | tf_op jit(solution)/shard_map/ppermute | solution.py:200
  114.8 1.7 %collective-permute-start.4 = (f32[30,128]{1,0:T(8,128)S(1)}, f32[30,128]{1,0:T(8,128)S(1)}, u32[]{:S(2)}, u32[]{:S(2)}) collective-permute-start(f32[30,128]{1,0:T(8,128)S(1)} %convert_reduce_fusion), channel_id=1, source_target_pairs={{0,2},{1,3},{2,0},{3,1},{4,6},{5,7},{6,4},{7,5},{8,10},{9,11},{10,... | collective-permute-start | bytes 46088 | tf_op jit(solution)/shard_map/ppermute | solution.py:200
  116.5 0.8 dynamic_slice.28
  117.4 2.7 %collective-permute-done.4 = f32[30,128]{1,0:T(8,128)S(1)} collective-permute-done((f32[30,128]{1,0:T(8,128)S(1)}, f32[30,128]{1,0:T(8,128)S(1)}, u32[]{:S(2)}, u32[]{:S(2)}) %collective-permute-start.4) | collective-permute-done | bytes 15392 | tf_op jit(solution)/shard_map/ppermute | solution.py:200
  120.1 1.4 %collective-permute-done.3 = f32[30,128]{1,0:T(8,128)S(1)} collective-permute-done((f32[30,128]{1,0:T(8,128)S(1)}, f32[30,128]{1,0:T(8,128)S(1)}, u32[]{:S(2)}, u32[]{:S(2)}) %collective-permute-start.3) | collective-permute-done | bytes 15392 | tf_op jit(solution)/shard_map/ppermute | solution.py:200
  121.6 0.2 fusion.1
  121.8 0.7 fusion.10
  (44 shorter events, 0.8 us)
Async XLA Ops:
  0.6 35.6 %copy-start = (bf16[100,640]{1,0:T(8,128)(2,1)S(1)}, bf16[100,640]{1,0:T(8,128)(2,1)}, u32[]{:S(2)}) copy-start(bf16[100,640]{1,0:T(8,128)(2,1)} %param.11) | copy-start | bytes 384004
  3.5 14.4 %collective-permute-start.2 = (f32[3,10,128]{2,1,0:T(8,128)}, f32[3,10,128]{2,1,0:T(8,128)S(1)}, u32[]{:S(2)}, u32[]{:S(2)}) collective-permute-start(f32[3,10,128]{2,1,0:T(8,128)} %amp.1), channel_id=1, source_target_pairs={{0,3},{1,0},{2,1},{3,2},{4,7},{5,4},{6,5},{7,6},{8,11},{9,8},{10,9... | collective-permute-start | bytes 46088 | tf_op jit(solution)/shard_map/ppermute | solution.py:200
  6.5 11.4 %collective-permute-start.1 = (f32[3,10,128]{2,1,0:T(8,128)}, f32[3,10,128]{2,1,0:T(8,128)S(1)}, u32[]{:S(2)}, u32[]{:S(2)}) collective-permute-start(f32[3,10,128]{2,1,0:T(8,128)} %amp.1), channel_id=1, source_target_pairs={{0,2},{1,3},{2,0},{3,1},{4,6},{5,7},{6,4},{7,5},{8,10},{9,11},{10,... | collective-permute-start | bytes 46088 | tf_op jit(solution)/shard_map/ppermute | solution.py:200
  7.1 10.8 %collective-permute-start = (f32[3,10,128]{2,1,0:T(8,128)}, f32[3,10,128]{2,1,0:T(8,128)S(1)}, u32[]{:S(2)}, u32[]{:S(2)}) collective-permute-start(f32[3,10,128]{2,1,0:T(8,128)} %amp.1), channel_id=1, source_target_pairs={{0,1},{1,2},{2,3},{3,0},{4,5},{5,6},{6,7},{7,4},{8,9},{9,10},{10,1... | collective-permute-start | bytes 46088 | tf_op jit(solution)/shard_map/ppermute | solution.py:200
  15.7 2.2 %copy-start.4 = (f32[3,10,128]{2,1,0:T(8,128)S(1)}, f32[3,10,128]{2,1,0:T(8,128)}, u32[]{:S(2)}) copy-start(f32[3,10,128]{2,1,0:T(8,128)} %amp.1) | copy-start | bytes 46084
  19.4 12.3 %copy-start.3 = (s32[640]{0:T(1024)S(1)}, s32[640]{0:T(1024)}, u32[]{:S(2)}) copy-start(s32[640]{0:T(1024)} %vir_irrep.3) | copy-start | bytes 7684
  19.4 13.7 %copy-start.6 = (s32[2,2]{1,0:T(2,128)S(1)}, s32[2,2]{1,0:T(2,128)}, u32[]{:S(2)}) copy-start(s32[2,2]{1,0:T(2,128)} %pair_s.3) | copy-start | bytes 52
  19.4 14.0 %copy-start.1 = (s32[100]{0:T(128)S(1)}, s32[100]{0:T(128)}, u32[]{:S(2)}) copy-start(s32[100]{0:T(128)} %occ_s.3) | copy-start | bytes 1204
  19.4 55.4 %all-to-all-start = ((bf16[64,110,128]{2,1,0:T(8,128)(2,1)}), bf16[64,110,128]{2,1,0:T(8,128)(2,1)S(1)}, u32[]{:S(2)}, u32[]{:S(2)}) async-start(bf16[64,110,128]{2,1,0:T(8,128)(2,1)} %pad_maximum_fusion), calls=%async_computation | async-start | bytes 3670016 | tf_op jit(solution)/shard_map/all_to_all | solution.py:277
  75.3 20.4 %copy-start.2 = (f32[100]{0:T(128)S(1)}, f32[100]{0:T(128)}, u32[]{:S(2)}) copy-start(f32[100]{0:T(128)} %param.14) | copy-start | bytes 1204
  86.1 35.7 %copy-start.5 = (f32[2,10,160]{2,0,1:T(2,128)S(1)}, f32[2,10,160]{2,0,1:T(2,128)}, u32[]{:S(2)}) copy-start(f32[2,10,160]{2,0,1:T(2,128)} %param.10) | copy-start | bytes 38404
  87.3 25.1 %all-to-all-start.1 = ((bf16[64,30,128]{2,1,0:T(8,128)(2,1)}), bf16[64,30,128]{2,1,0:T(8,128)(2,1)S(1)}, u32[]{:S(2)}, u32[]{:S(2)}) async-start(bf16[64,30,128]{2,1,0:T(8,128)(2,1)} %bitcast.42), calls=%async_computation.1 | async-start | bytes 1048576 | tf_op jit(solution)/shard_map/all_to_all | solution.py:277
  112.5 4.9 %collective-permute-start.5 = (f32[30,128]{1,0:T(8,128)S(1)}, f32[30,128]{1,0:T(8,128)S(1)}, u32[]{:S(2)}, u32[]{:S(2)}) collective-permute-start(f32[30,128]{1,0:T(8,128)S(1)} %convert_reduce_fusion), channel_id=1, source_target_pairs={{0,3},{1,0},{2,1},{3,2},{4,7},{5,4},{6,5},{7,6},{8,11},{9,8},{10,9... | collective-permute-start | bytes 46088 | tf_op jit(solution)/shard_map/ppermute | solution.py:200
  114.8 5.2 %collective-permute-start.4 = (f32[30,128]{1,0:T(8,128)S(1)}, f32[30,128]{1,0:T(8,128)S(1)}, u32[]{:S(2)}, u32[]{:S(2)}) collective-permute-start(f32[30,128]{1,0:T(8,128)S(1)} %convert_reduce_fusion), channel_id=1, source_target_pairs={{0,2},{1,3},{2,0},{3,1},{4,6},{5,7},{6,4},{7,5},{8,10},{9,11},{10,... | collective-permute-start | bytes 46088 | tf_op jit(solution)/shard_map/ppermute | solution.py:200
  116.5 4.9 %collective-permute-start.3 = (f32[30,128]{1,0:T(8,128)S(1)}, f32[30,128]{1,0:T(8,128)S(1)}, u32[]{:S(2)}, u32[]{:S(2)}) collective-permute-start(f32[30,128]{1,0:T(8,128)S(1)} %convert_reduce_fusion), channel_id=1, source_target_pairs={{0,1},{1,2},{2,3},{3,0},{4,5},{5,6},{6,7},{7,4},{8,9},{9,10},{10,1... | collective-permute-start | bytes 46088 | tf_op jit(solution)/shard_map/ppermute | solution.py:200

commit v5 on v4

--- a/solution.py
+++ b/solution.py
@@ -13,7 +13,6 @@
 STRIDE = 40
 GROUPS = 3
 REST = RUN - MAIN
-CYCLE_LANE = GROUPS * STRIDE
 LIMIT = 48 * 1024 * 1024
 NT = (((1,), (1,)), ((), ()))
 
@@ -31,19 +30,45 @@
 
 
 def pack_kernel(
-    vir_s, occ_s, pair_s, chol, ov, vir_irrep, chol_irrep, out, fold, labels, pick
+    vir_s,
+    occ_s,
+    pair_s,
+    chol,
+    ov,
+    singles,
+    vir_irrep,
+    chol_irrep,
+    out,
+    fold,
+    labels,
+    pick,
+    stage,
 ):
     step = pl.program_id(0)
     vir_line = vir_irrep[...][None, :]
     rows, q_local, vir_total = chol.shape
     occ_total = ov.shape[1]
-    own = out.shape[2]
+    own = out.shape[0]
+    per_row = out.shape[1] // rows
 
     @pl.when(step == 0)
     def _():
         place = run_positions(vir_line)
-        row = lax.broadcasted_iota(I32, (2 * MAIN, vir_total), 0)
-        fold[...] = jnp.where(row == place, 1.0, 0.0).T.astype(BF)
+        row = lax.broadcasted_iota(I32, (RUN, vir_total), 0)
+        runs = jnp.where(row == place, 1.0, 0.0)
+        slot = lax.broadcasted_iota(I32, (8, occ_total), 0)
+        orbital = lax.broadcasted_iota(I32, (8, occ_total), 1)
+        taken = jnp.zeros((8, occ_total), F32)
+        slot_label = jnp.full((8, 1), -1, I32)
+        for m in range(4):
+            hit = (slot == m) & (orbital == pair_s[m // 2, m % 2])
+            taken = jnp.where(hit, 1.0, taken)
+            label = occ_s[pair_s[m // 2, m % 2]]
+            slot_label = jnp.where(slot[:, :1] == m, label, slot_label)
+        rows8 = dot(taken.astype(BF), singles[...])
+        rows8 = jnp.where(slot_label == vir_line, rows8, 0.0)
+        none = jnp.zeros((2 * MAIN - RUN - 8, vir_total), F32)
+        fold[...] = jnp.concatenate([runs, rows8, none], axis=0).T.astype(BF)
         first = pl.multiple_of(lax.axis_index("rep") * q_local, MAIN)
         mine = chol_irrep[pl.ds(first, q_local)][None, :].astype(F32)
         labels[...] = jnp.broadcast_to(mine, (MAIN, q_local)).T.astype(I32)
@@ -73,13 +98,17 @@
         )
         rest = mine[:, MAIN:] + jnp.where(wants[k] == occ_label, extra, 0.0)
         for q in range(2 * GROUPS):
-            out[q, k] = mine[q * own : (q + 1) * own, :MAIN].astype(BF)
+            stage[pl.ds(k * per_row + q, own, stride=rows * per_row), :] = mine[
+                q * own : (q + 1) * own, :MAIN
+            ]
         for u in range(2):
             total = rest[u * GROUPS * own : (u * GROUPS + 1) * own]
             for g in range(1, GROUPS):
                 part = rest[(u * GROUPS + g) * own : (u * GROUPS + g + 1) * own]
                 total = total + pltpu.roll(part, g * STRIDE, 1)
-            out[2 * GROUPS + u, k] = total.astype(BF)
+            at = k * per_row + 2 * GROUPS + u
+            stage[pl.ds(at, own, stride=rows * per_row), :] = total
+    out[...] = stage[...].reshape(out.shape).astype(BF)
 
 
 def amp_kernel(vir_s, occ_s, pair_s, amp, vir_irrep, out):
@@ -117,68 +146,63 @@
     col_irrep,
     row_pos,
     col_pos,
-    single_rows,
-    occ_lanes,
     out,
     ball,
     hall,
     amps,
     unfold,
-    weight,
+    stage,
 ):
     vir_total = row_irrep.shape[0]
-    single = single_rows[...].astype(BF)
-    rest_amp = got[10].astype(F32)
-    lane = lax.broadcasted_iota(I32, (vir_total, MAIN), 1)
+    own = got.shape[1]
+    row_count = vir_total // own
+    per_row = 2 * GROUPS + 2
+    lane = lax.broadcasted_iota(I32, (own, MAIN), 1)
     index = lax.broadcasted_iota(I32, (2 * MAIN, vir_total), 0)
     column = col_pos[...]
     for g in range(GROUPS):
         place = jnp.where(column < MAIN, column, column + g * STRIDE)
         unfold[g] = jnp.where(index == place, 1.0, 0.0).astype(BF)
-        short = lax.dot_general(single, unfold[g], NT, preferred_element_type=F32)
-        slot = lax.broadcasted_iota(I32, short.shape, 0)
-        at = lax.broadcasted_iota(I32, short.shape, 1)
-        short = short + jnp.where(
-            (at == slot + MAIN + g * STRIDE + REST) & (slot < 4), 1.0, 0.0
-        )
-        row = lax.broadcasted_iota(I32, (MAIN, 2 * MAIN), 0)
-        zero = jnp.zeros((MAIN, 2 * MAIN), F32)
-        first = CYCLE_LANE
-        for m in range(2):
-            weight[g, m * MAIN : (m + 1) * MAIN] = jnp.where(
-                row == first,
-                short[1 - m : 2 - m],
-                jnp.where(row == first + 1, short[3 - m : 4 - m], zero),
-            ).astype(BF)
+    amp_at = row_count * per_row
+    for r in range(row_count):
+        here = slice(r * own, (r + 1) * own)
+        rest_amp = got[amp_at + 2 * row_count + r].astype(F32)
         for p in range(2):
-            amps[g, :, p * 256 : p * 256 + MAIN] = got[8 + p]
-            shift = (g * STRIDE - p * 64) % MAIN
-            moved = pltpu.roll(rest_amp, shift, 1) if shift else rest_amp
-            inside = (lane >= g * STRIDE) & (lane < g * STRIDE + REST)
-            amps[g, :, p * 256 + MAIN : (p + 1) * 256] = jnp.where(inside, moved, 0.0).astype(BF)
-
-    def one(q, carry):
-        g = q % GROUPS
-        bc = jnp.concatenate([got[q], got[2 * GROUPS + q // GROUPS]], axis=1)
-        want = jnp.bitwise_xor(row_irrep[...], q_irrep[q])
-        wide = dot(bc, unfold[g])
-        wide = jnp.where(want == col_irrep[...], wide, 0.0).astype(BF)
-        halfway = dot(wide, amps[g])
-        dressed = lax.dot_general(bc, weight[g], NT, preferred_element_type=F32)
-        dressed = jnp.where(want == occ_lanes[...], dressed, 0.0)
-        ball[:, q * 256 : q * 256 + MAIN] = bc[:, :MAIN]
-        ball[:, q * 256 + MAIN : (q + 1) * 256] = (bc[:, MAIN:].astype(F32) + dressed[:, :MAIN]).astype(BF)
-        for p in range(2):
-            hall[p, :, q * 256 : q * 256 + MAIN] = halfway[:, p * 256 : p * 256 + MAIN].astype(BF)
-            own = jnp.where(lane == CYCLE_LANE + p, dressed[:, MAIN:], 0.0)
-            hall[p, :, q * 256 + MAIN : (q + 1) * 256] = (
-                halfway[:, p * 256 + MAIN : (p + 1) * 256] + own
-            ).astype(BF)
-        return carry
-
-    for q in range(2 * GROUPS):
-        one(q, 0)
-
+            main_amp = got[amp_at + p * row_count + r]
+            for g in range(GROUPS):
+                shift = (g * STRIDE - p * 64) % MAIN
+                moved = pltpu.roll(rest_amp, shift, 1) if shift else rest_amp
+                inside = (lane >= g * STRIDE) & (lane < g * STRIDE + REST)
+                amps[g, here, p * 256 : p * 256 + MAIN] = main_amp
+                amps[g, here, p * 256 + MAIN : (p + 1) * 256] = jnp.where(
+                    inside, moved, 0.0
+                ).astype(BF)
+        for q in range(2 * GROUPS):
+            ball[here, q * 256 : q * 256 + MAIN] = got[r * per_row + q]
+            ball[here, q * 256 + MAIN : (q + 1) * 256] = got[
+                r * per_row + 2 * GROUPS + q // GROUPS
+            ]
+
+    lane = lax.broadcasted_iota(I32, (vir_total, MAIN), 1)
+    for u in range(2):
+        at = u * GROUPS * 256 + MAIN
+        shifted = pltpu.roll(ball[:, at : at + MAIN].astype(F32), 1, 1)
+        for g in range(GROUPS):
+            q = u * GROUPS + g
+            want = jnp.bitwise_xor(row_irrep[...], q_irrep[q])
+            wide = dot(ball[:, q * 256 : (q + 1) * 256], unfold[g])
+            wide = jnp.where(want == col_irrep[...], wide, 0.0).astype(BF)
+            halfway = dot(wide, amps[g])
+            for p in range(2):
+                hall[p, :, q * 256 : q * 256 + MAIN] = halfway[
+                    :, p * 256 : p * 256 + MAIN
+                ].astype(BF)
+                dressed = jnp.where(lane == g * STRIDE + REST + 2 * p + 1, shifted, 0.0)
+                hall[p, :, q * 256 + MAIN : (q + 1) * 256] = (
+                    halfway[:, p * 256 + MAIN : (p + 1) * 256] + dressed
+                ).astype(BF)
+
+    out_rows = out.shape[1]
     lane2 = lax.broadcasted_iota(I32, (vir_total, 2 * MAIN), 1)
     tail = None
     for p in range(2):
@@ -189,9 +213,18 @@
         place = jnp.where(place < MAIN, place, place + p * 64)
         fold = jnp.where(lane2 == place, 1.0, 0.0).astype(BF)
         short = dot(value, fold)
-        out[p] = short[:, :MAIN].astype(BF)
+        for r in range(row_count):
+            stage[pl.ds(p * row_count + r, own, stride=out_rows), :] = short[
+                r * own : (r + 1) * own, :MAIN
+            ]
         tail = short[:, MAIN:] if tail is None else tail + short[:, MAIN:]
-    out[2] = tail.astype(BF)
+    for r in range(row_count):
+        stage[pl.ds(2 * row_count + r, own, stride=out_rows), :] = tail[
+            r * own : (r + 1) * own
+        ]
+    for t in range(3 * row_count, out_rows):
+        stage[pl.ds(t, own, stride=out_rows), :] = jnp.zeros((own, MAIN), F32)
+    out[...] = stage[...].reshape(out.shape).astype(BF)
 
 
 def over_rep(value):
@@ -234,7 +267,9 @@
         out_shape=jax.ShapeDtypeStruct((3, row_count, MAIN), F32),
         name="amp",
     )(vir_irrep, occ_irrep, pair_list, amplitudes.transpose(1, 0, 2), vir_irrep)
+    amp_rows = 32
     amp_send = over_rep(amp_send).astype(BF).reshape(3 * row_count, MAIN)
+    amp_send = jnp.pad(amp_send, ((0, amp_rows - 3 * row_count), (0, 0)))
 
     rows = 2
     packed = pl.pallas_call(
@@ -245,17 +280,19 @@
             in_specs=[
                 pl.BlockSpec((rows, q_local, vir_total), lambda i, *s: (i, 0, 0)),
                 pl.BlockSpec((rows, occ_total, q_local), lambda i, *s: (i, 0, 0)),
+                pl.BlockSpec((occ_total, vir_total), lambda i, *s: (0, 0)),
                 pl.BlockSpec((vir_total,), lambda i, *s: (0,)),
                 pl.BlockSpec(chol_irrep.shape, lambda i, *s: (0,)),
             ],
-            out_specs=pl.BlockSpec((8, rows, blk_count, MAIN), lambda i, *s: (0, i, 0, 0)),
+            out_specs=pl.BlockSpec((blk_count, 8 * rows, MAIN), lambda i, *s: (0, i, 0)),
             scratch_shapes=[
                 pltpu.VMEM((vir_total, 2 * MAIN), BF),
                 pltpu.VMEM((q_local, MAIN), I32),
                 pltpu.VMEM((occ_total, MAIN), BF),
+                pltpu.VMEM((blk_count * 8 * rows, MAIN), F32),
             ],
         ),
-        out_shape=jax.ShapeDtypeStruct((8, row_count, blk_count, MAIN), BF),
+        out_shape=jax.ShapeDtypeStruct((blk_count, 8 * row_count + amp_rows, MAIN), BF),
         cost_estimate=pl.CostEstimate(
             flops=2 * q_local * row_count * vir_total * 256,
             bytes_accessed=2 * q_local * row_count * vir_total,
@@ -268,22 +305,21 @@
         pair_list,
         chol_vv.transpose(1, 0, 2),
         chol_ov.transpose(2, 1, 0),
+        singles,
         vir_irrep,
         chol_irrep,
     )
-    packed = packed.reshape(8 * row_count, blk_count, MAIN).transpose(1, 0, 2)
 
     def swap(value):
         return lax.all_to_all(value, "blk", split_axis=0, concat_axis=0, tiled=False)
 
-    got = swap(
-        jnp.concatenate(
-            [packed, jnp.broadcast_to(amp_send[None], (blk_count,) + amp_send.shape)], axis=1
-        )
-    )
-    vir_irrep, singles, pair_list = lax.optimization_barrier(
-        (vir_irrep, singles, pair_list, packed)
-    )[:3]
+    packed = lax.dynamic_update_slice(
+        packed,
+        jnp.broadcast_to(amp_send[None], (blk_count,) + amp_send.shape),
+        (0, 8 * row_count, 0),
+    )
+    got = swap(packed)
+    vir_irrep, pair_list = lax.optimization_barrier((vir_irrep, pair_list, packed))[:2]
     starts = jnp.sum(
         (vir_irrep[None, :] < jnp.arange(8, dtype=I32)[:, None]).astype(I32), axis=1
     )
@@ -300,13 +336,11 @@
     pair_first = pair_list[:, 0]
     pair_second = pair_list[:, 1]
     pair_sym = jnp.bitwise_xor(occ_irrep[pair_first], occ_irrep[pair_second])
-    occ_rows = pair_list.reshape(-1)
-    occ_labels = occ_irrep[occ_rows]
     amp_mask = (
         jnp.bitwise_xor(row_irrep[None, :, None], col_irrep[None, None, :])
         == pair_sym[:, None, None]
     )
-    got = got.transpose(1, 0, 2).reshape(11, vir_total, MAIN)
+    got = got.transpose(1, 0, 2)
 
     def mixed(x):
         return x.reshape(blk_count, row_count).T.reshape(vir_total)
@@ -316,22 +350,6 @@
     own_irrep = lax.dynamic_index_in_dim(
         q_irrep.reshape(q_own, blk_count), blk_pos, axis=1, keepdims=False
     )
-    single_rows = jnp.where(
-        occ_labels[:, None] == vir_irrep[None, :], singles[occ_rows], jnp.zeros((), singles.dtype)
-    ).astype(F32)
-    single_rows = single_rows.reshape(4, blk_count, row_count).transpose(0, 2, 1)
-    single_rows = jnp.pad(single_rows.reshape(4, vir_total), ((0, 4), (0, 0)))
-    first = CYCLE_LANE
-    lane_row = jnp.arange(2 * MAIN, dtype=I32)
-    occ_lanes = jnp.where(
-        lane_row == first,
-        occ_labels[1],
-        jnp.where(
-            lane_row == first + 1,
-            occ_labels[3],
-            jnp.where(lane_row == MAIN + first, occ_labels[0], occ_labels[2]),
-        ),
-    )[None, :]
     smem = pl.BlockSpec(memory_space=pltpu.SMEM)
     vmem = pl.BlockSpec(memory_space=pltpu.VMEM)
     tables = (
@@ -339,29 +357,26 @@
         irrep_mixed[None, :],
         pos_mixed[:, None],
         pos_mixed[None, :],
-        single_rows,
-        occ_lanes,
     )
 
     part = pl.pallas_call(
         pair_kernel,
-        in_specs=[smem, smem] + [vmem] * 7,
+        in_specs=[smem, smem] + [vmem] * 5,
         out_specs=vmem,
-        out_shape=jax.ShapeDtypeStruct((3, vir_total, MAIN), BF),
+        out_shape=jax.ShapeDtypeStruct((blk_count, 32, MAIN), BF),
         scratch_shapes=[
             pltpu.VMEM((vir_total, 4 * GROUPS * MAIN), BF),
             pltpu.VMEM((2, vir_total, 4 * GROUPS * MAIN), BF),
             pltpu.VMEM((GROUPS, vir_total, 4 * MAIN), BF),
             pltpu.VMEM((GROUPS, 2 * MAIN, vir_total), BF),
-            pltpu.VMEM((GROUPS, 2 * MAIN, 2 * MAIN), BF),
+            pltpu.VMEM((blk_count * 32, MAIN), F32),
         ],
         compiler_params=pltpu.CompilerParams(vmem_limit_bytes=LIMIT),
         name="ladder",
     )(own_irrep, pair_sym, got, *tables)
-    part = part.reshape(3 * row_count, blk_count, MAIN).transpose(1, 0, 2)
     part = swap(part)
     summed = over_rep(jnp.sum(part.astype(F32), axis=0))
-    summed = summed.reshape(3, row_count, MAIN)
+    summed = summed[: 3 * row_count].reshape(3, row_count, MAIN)
     short = jnp.stack(
         [
             jnp.concatenate([summed[p], summed[2, :, p * 64 : p * 64 + REST]], axis=1)

time: 123 us -> 121 us (0.984)
  waiting for transfers between devices: 52.7 us -> 57.6 us
  local copies, waits for them, and re-layouts: 12.7 us -> 8 us
  other arithmetic: 5.47 us -> 1.41 us
  Pallas kernels: 21.2 us -> 22.5 us
    all_to_all x2, waiting for transfers between devices: 48.5 us -> 52.8 us  [swap(): lax.all_to_all(value, 'blk', split_axis=0, concat_axis=0, tiled=False)]
    reshape x5 -> x2, local copies, waits for them, and re-layouts: 3.46 us -> 0.01 us  [the longest x1 0.01 us: per_device(): amp_send = over_rep(amp_send).astype(BF).reshape(3 * row_count, MAIN)]
    select_n x2 -> x0, other arithmetic: 2.55 us -> none  [the longest x1 2.55 us: per_device(): jnp.where(lane_row == first, occ_labels[1], jnp.where(lane_row == first +...]
    concatenate x1 -> x0, other arithmetic: 1.4 us -> none  [per_device(): jnp.concatenate([packed, jnp.broadcast_to(amp_send[None], (blk_count,) +...]
    gather x3 -> x0, local copies, waits for them, and re-layouts: 1.37 us -> none  [the longest x2 0.73 us: per_device(): singles[occ_rows]]
  transfers between devices with their start and end apart: 8 -> 8, of which waited for: 4 -> 4; matrix products, arithmetic and copies ran while one was open for 12% -> 6% of each run, Pallas kernels for 6% -> 7%
where the time goes in v5:
time: 121 us; the launch traced here: 120 us
  waiting for transfers between devices  57.6 us (48%)
  starting transfers between devices  29.5 us (24%)
  Pallas kernels  22.5 us (19%)
  local copies, waits for them, and re-layouts  8 us (7%)
  other arithmetic  1.41 us (1%)
    all_to_all x2, waiting for transfers between devices, swap(): lax.all_to_all(value, 'blk', split_axis=0, concat_axis=0, tiled=False)  52.8 us
    all_to_all x2, starting transfers between devices, swap(): lax.all_to_all(value, 'blk', split_axis=0, concat_axis=0, tiled=False)  20.8 us
    pallas_call x1, Pallas kernels, per_device(): pl.pallas_call(pair_kernel, in_specs=[smem, smem] + [vmem] * 5, out_specs...  11.5 us
    ppermute x6, starting transfers between devices, over_rep(): lax.ppermute(value, 'rep', [(i, (i + k) % 4) for i in range(4)])  8.64 us
    pallas_call x1, Pallas kernels, per_device(): pl.pallas_call(pack_kernel, grid_spec=pltpu.PrefetchScalarGridSpec(num_sc...  8.17 us
    ppermute x6, waiting for transfers between devices, over_rep(): lax.ppermute(value, 'rep', [(i, (i + k) % 4) for i in range(4)])  4.87 us
    pallas_call x1, Pallas kernels, per_device(): pl.pallas_call(amp_kernel, grid_spec=pltpu.PrefetchScalarGridSpec(num_sca...  2.78 us
  transfers between devices with their start and end apart: 8, of which 4 were waited for; matrix products, arithmetic and copies ran while one was open for 6% of the time, Pallas kernels for 7%

profile of v5, /device:TPU:6, one launch (start us, length us, event | category | flops | bytes accessed | tf_op | source)
XLA Modules:
  0.0 120.0 jit_solution(13457941838056275711)
XLA Ops:
  0.6 0.0 copy-start
  0.6 2.8 %amp.1 = f32[3,10,128]{2,1,0:T(8,128)} custom-call(s32[640]{0:T(1024)} %vir_irrep.3, s32[100]{0:T(128)} %occ_s.3, s32[2,2]{1,0:T(2,128)} %pair_s.3, f32[10,2,160]{2,1,0:T(2,128)} %bitcast.35, s32[640]{0:T(1024)} %vir_irrep.3), custom_call_target="tpu_custom_call" | custom-call | tf_op jit(solution)/shard_map/amp/pallas_call | solution.py:256
  3.4 3.0 %collective-permute-start.2 = (f32[3,10,128]{2,1,0:T(8,128)}, f32[3,10,128]{2,1,0:T(8,128)S(1)}, u32[]{:S(2)}, u32[]{:S(2)}) collective-permute-start(f32[3,10,128]{2,1,0:T(8,128)} %amp.1), channel_id=1, source_target_pairs={{0,3},{1,0},{2,1},{3,2},{4,7},{5,4},{6,5},{7,6},{8,11},{9,8},{10,9... | collective-permute-start | bytes 46088 | tf_op jit(solution)/shard_map/ppermute | solution.py:233
  6.4 0.6 collective-permute-start.1
  7.1 1.0 collective-permute-start
  8.0 8.2 %pack.1 = bf16[64,112,128]{2,1,0:T(8,128)(2,1)} custom-call(s32[640]{0:T(1024)} %vir_irrep.3, s32[100]{0:T(128)} %occ_s.3, s32[2,2]{1,0:T(2,128)} %pair_s.3, bf16[10,384,640]{2,1,0:T(8,128)(2,1)} %bitcast.31, bf16[10,100,384]{2,1,0:T(8,128)(2,1)} %bitcast.32, bf16[100,640]{1,0:T(8,128)(2,1)} %singles.1, s32[640]{0:T(1024)} %vir_irrep.3, s32[1536]{0:T(1024)} %chol_irrep.1), custom_call_target="tpu_custom_call" | custom-call | flops 1258291200 | bytes 4915200 | tf_op jit(solution)/shard_map/pack/pallas_call | solution.py:275
  16.2 0.0 collective-permute-done
  16.3 0.9 broadcast_dynamic-update-slice_fusion
  17.2 12.3 %all-to-all-start = ((bf16[64,112,128]{2,1,0:T(8,128)(2,1)}), bf16[64,112,128]{2,1,0:T(8,128)(2,1)S(1)}, u32[]{:S(2)}, u32[]{:S(2)}) async-start(bf16[64,112,128]{2,1,0:T(8,128)(2,1)} %broadcast_dynamic-update-slice_fusion), calls=%async_computation | async-start | bytes 3670016 | tf_op jit(solution)/shard_map/all_to_all | solution.py:314
  29.5 0.8 dynamic_slice.25
  30.3 0.1 reshape.105
  30.4 0.2 dynamic-slice_reduce_fusion.q_irrep
  30.6 0.1 reshape.106
  30.7 0.1 copy.39
  30.8 0.1 broadcast_in_dim_reshape.13.col_irrep
  30.9 0.3 broadcast_in_dim_reshape.16.row_irrep
  31.2 0.1 convert_reduce_fusion.1
  31.3 0.1 select_reduce_fusion
  31.4 0.1 reduce_sum.31
  31.5 0.1 copy.41
  31.6 0.1 broadcast_in_dim_reshape.15.col_pos
  31.7 0.3 broadcast_in_dim_reshape.17.row_pos
  32.0 0.2 fusion.11
  32.2 0.6 gather_fusion.1
  32.8 0.6 gather_fusion
  33.5 39.2 %all-to-all-done = bf16[64,112,128]{2,1,0:T(8,128)(2,1)S(1)} async-done(((bf16[64,112,128]{2,1,0:T(8,128)(2,1)}), bf16[64,112,128]{2,1,0:T(8,128)(2,1)S(1)}, u32[]{:S(2)}, u32[]{:S(2)}) %all-to-all-start) | async-done | bytes 1835040 | tf_op jit(solution)/shard_map/all_to_all | solution.py:314
  72.6 0.5 copy.48
  73.1 11.5 %ladder.1 = bf16[64,32,128]{2,1,0:T(8,128)(2,1)} custom-call(s32[6]{0:T(128)S(1)} %dynamic-slice_reduce_fusion.q_irrep, s32[2]{0:T(128)S(1)} %xor.24.pair_sym, bf16[112,64,128]{2,1,0:T(8,128)(2,1)S(1)} %bitcast.30, s32[640,1]{1,0:T(8,128)S(1)} %broadcast_in_dim_reshape.16.row_irrep, s32[1,640]{1,0:T(1,128)S(1)} %broadcast_in_dim_reshape.13.col_irrep, ...), custom_call_target="tpu_custom_call" | custom-call | tf_op jit(solution)/shard_map/ladder/pallas_call | solution.py:362
  84.6 8.5 %all-to-all-start.1 = ((bf16[64,32,128]{2,1,0:T(8,128)(2,1)}), bf16[64,32,128]{2,1,0:T(8,128)(2,1)S(1)}, u32[]{:S(2)}, u32[]{:S(2)}) async-start(bf16[64,32,128]{2,1,0:T(8,128)(2,1)} %ladder.1), calls=%async_computation.1 | async-start | bytes 1048576 | tf_op jit(solution)/shard_map/all_to_all | solution.py:314
  93.1 0.8 dynamic_slice.27
  93.9 0.8 dynamic_slice.28
  94.7 0.1 dynamic_slice.22
  94.7 0.1 dynamic_slice.23
  94.8 0.6 gather_fusion.3
  95.5 0.6 gather_fusion.2
  96.1 0.1 broadcast_subtract_fusion
  96.2 0.1 broadcast_xor_fusion
  96.2 13.6 %all-to-all-done.1 = bf16[64,32,128]{2,1,0:T(8,128)(2,1)S(1)} async-done(((bf16[64,32,128]{2,1,0:T(8,128)(2,1)}), bf16[64,32,128]{2,1,0:T(8,128)(2,1)S(1)}, u32[]{:S(2)}, u32[]{:S(2)}) %all-to-all-start.1) | async-done | bytes 524320 | tf_op jit(solution)/shard_map/all_to_all | solution.py:314
  109.8 0.1 convert_reduce_fusion
  109.9 2.3 %collective-permute-start.5 = (f32[32,128]{1,0:T(8,128)S(1)}, f32[32,128]{1,0:T(8,128)S(1)}, u32[]{:S(2)}, u32[]{:S(2)}) collective-permute-start(f32[32,128]{1,0:T(8,128)S(1)} %convert_reduce_fusion), channel_id=1, source_target_pairs={{0,3},{1,0},{2,1},{3,2},{4,7},{5,4},{6,5},{7,6},{8,11},{9,8},{10,9... | collective-permute-start | bytes 49160 | tf_op jit(solution)/shard_map/ppermute | solution.py:233
  112.3 1.7 %collective-permute-start.4 = (f32[32,128]{1,0:T(8,128)S(1)}, f32[32,128]{1,0:T(8,128)S(1)}, u32[]{:S(2)}, u32[]{:S(2)}) collective-permute-start(f32[32,128]{1,0:T(8,128)S(1)} %convert_reduce_fusion), channel_id=1, source_target_pairs={{0,2},{1,3},{2,0},{3,1},{4,6},{5,7},{6,4},{7,5},{8,10},{9,11},{10,... | collective-permute-start | bytes 49160 | tf_op jit(solution)/shard_map/ppermute | solution.py:233
  114.0 0.0 collective-permute-start.3
  114.0 0.1 dynamic_slice.24
  114.1 3.5 %collective-permute-done.4 = f32[32,128]{1,0:T(8,128)S(1)} collective-permute-done((f32[32,128]{1,0:T(8,128)S(1)}, f32[32,128]{1,0:T(8,128)S(1)}, u32[]{:S(2)}, u32[]{:S(2)}) %collective-permute-start.4) | collective-permute-done | bytes 16416 | tf_op jit(solution)/shard_map/ppermute | solution.py:233
  117.5 1.4 %collective-permute-done.3 = f32[32,128]{1,0:T(8,128)S(1)} collective-permute-done((f32[32,128]{1,0:T(8,128)S(1)}, f32[32,128]{1,0:T(8,128)S(1)}, u32[]{:S(2)}, u32[]{:S(2)}) %collective-permute-start.3) | collective-permute-done | bytes 16416 | tf_op jit(solution)/shard_map/ppermute | solution.py:233
  119.0 0.1 slice_bitcast_fusion.1
  119.0 0.2 fusion.1
  119.3 0.7 fusion.9
  (28 shorter events, 0.1 us)
Async XLA Ops:
  0.6 94.2 %copy-start = (f32[100]{0:T(128)S(1)}, f32[100]{0:T(128)}, u32[]{:S(2)}) copy-start(f32[100]{0:T(128)} %param.14) | copy-start | bytes 1204
  3.4 12.8 %collective-permute-start.2 = (f32[3,10,128]{2,1,0:T(8,128)}, f32[3,10,128]{2,1,0:T(8,128)S(1)}, u32[]{:S(2)}, u32[]{:S(2)}) collective-permute-start(f32[3,10,128]{2,1,0:T(8,128)} %amp.1), channel_id=1, source_target_pairs={{0,3},{1,0},{2,1},{3,2},{4,7},{5,4},{6,5},{7,6},{8,11},{9,8},{10,9... | collective-permute-start | bytes 46088 | tf_op jit(solution)/shard_map/ppermute | solution.py:233
  6.4 9.8 %collective-permute-start.1 = (f32[3,10,128]{2,1,0:T(8,128)}, f32[3,10,128]{2,1,0:T(8,128)S(1)}, u32[]{:S(2)}, u32[]{:S(2)}) collective-permute-start(f32[3,10,128]{2,1,0:T(8,128)} %amp.1), channel_id=1, source_target_pairs={{0,2},{1,3},{2,0},{3,1},{4,6},{5,7},{6,4},{7,5},{8,10},{9,11},{10,... | collective-permute-start | bytes 46088 | tf_op jit(solution)/shard_map/ppermute | solution.py:233
  7.1 9.2 %collective-permute-start = (f32[3,10,128]{2,1,0:T(8,128)}, f32[3,10,128]{2,1,0:T(8,128)S(1)}, u32[]{:S(2)}, u32[]{:S(2)}) collective-permute-start(f32[3,10,128]{2,1,0:T(8,128)} %amp.1), channel_id=1, source_target_pairs={{0,1},{1,2},{2,3},{3,0},{4,5},{5,6},{6,7},{7,4},{8,9},{9,10},{10,1... | collective-permute-start | bytes 46088 | tf_op jit(solution)/shard_map/ppermute | solution.py:233
  8.0 8.2 %copy-start.3 = (f32[3,10,128]{2,1,0:T(8,128)S(1)}, f32[3,10,128]{2,1,0:T(8,128)}, u32[]{:S(2)}) copy-start(f32[3,10,128]{2,1,0:T(8,128)} %amp.1) | copy-start | bytes 46084
  17.2 13.4 %copy-start.2 = (s32[640]{0:T(1024)S(1)}, s32[640]{0:T(1024)}, u32[]{:S(2)}) copy-start(s32[640]{0:T(1024)} %vir_irrep.3) | copy-start | bytes 7684
  17.2 14.7 %copy-start.5 = (s32[2,2]{1,0:T(2,128)S(1)}, s32[2,2]{1,0:T(2,128)}, u32[]{:S(2)}) copy-start(s32[2,2]{1,0:T(2,128)} %pair_s.3) | copy-start | bytes 52
  17.2 14.9 %copy-start.1 = (s32[100]{0:T(128)S(1)}, s32[100]{0:T(128)}, u32[]{:S(2)}) copy-start(s32[100]{0:T(128)} %occ_s.3) | copy-start | bytes 1204
  17.2 55.4 %all-to-all-start = ((bf16[64,112,128]{2,1,0:T(8,128)(2,1)}), bf16[64,112,128]{2,1,0:T(8,128)(2,1)S(1)}, u32[]{:S(2)}, u32[]{:S(2)}) async-start(bf16[64,112,128]{2,1,0:T(8,128)(2,1)} %broadcast_dynamic-update-slice_fusion), calls=%async_computation | async-start | bytes 3670016 | tf_op jit(solution)/shard_map/all_to_all | solution.py:314
  84.6 34.7 %copy-start.4 = (f32[2,10,160]{2,0,1:T(2,128)S(1)}, f32[2,10,160]{2,0,1:T(2,128)}, u32[]{:S(2)}) copy-start(f32[2,10,160]{2,0,1:T(2,128)} %param.10) | copy-start | bytes 38404
  84.6 25.2 %all-to-all-start.1 = ((bf16[64,32,128]{2,1,0:T(8,128)(2,1)}), bf16[64,32,128]{2,1,0:T(8,128)(2,1)S(1)}, u32[]{:S(2)}, u32[]{:S(2)}) async-start(bf16[64,32,128]{2,1,0:T(8,128)(2,1)} %ladder.1), calls=%async_computation.1 | async-start | bytes 1048576 | tf_op jit(solution)/shard_map/all_to_all | solution.py:314
  109.9 4.1 %collective-permute-start.5 = (f32[32,128]{1,0:T(8,128)S(1)}, f32[32,128]{1,0:T(8,128)S(1)}, u32[]{:S(2)}, u32[]{:S(2)}) collective-permute-start(f32[32,128]{1,0:T(8,128)S(1)} %convert_reduce_fusion), channel_id=1, source_target_pairs={{0,3},{1,0},{2,1},{3,2},{4,7},{5,4},{6,5},{7,6},{8,11},{9,8},{10,9... | collective-permute-start | bytes 49160 | tf_op jit(solution)/shard_map/ppermute | solution.py:233
  112.3 5.2 %collective-permute-start.4 = (f32[32,128]{1,0:T(8,128)S(1)}, f32[32,128]{1,0:T(8,128)S(1)}, u32[]{:S(2)}, u32[]{:S(2)}) collective-permute-start(f32[32,128]{1,0:T(8,128)S(1)} %convert_reduce_fusion), channel_id=1, source_target_pairs={{0,2},{1,3},{2,0},{3,1},{4,6},{5,7},{6,4},{7,5},{8,10},{9,11},{10,... | collective-permute-start | bytes 49160 | tf_op jit(solution)/shard_map/ppermute | solution.py:233
  114.0 4.9 %collective-permute-start.3 = (f32[32,128]{1,0:T(8,128)S(1)}, f32[32,128]{1,0:T(8,128)S(1)}, u32[]{:S(2)}, u32[]{:S(2)}) collective-permute-start(f32[32,128]{1,0:T(8,128)S(1)} %convert_reduce_fusion), channel_id=1, source_target_pairs={{0,1},{1,2},{2,3},{3,0},{4,5},{5,6},{6,7},{7,4},{8,9},{9,10},{10,1... | collective-permute-start | bytes 49160 | tf_op jit(solution)/shard_map/ppermute | solution.py:233

commit v6 on v5

--- a/solution.py
+++ b/solution.py
@@ -22,11 +22,10 @@
 
 
 def run_positions(irrep):
-    place = lax.broadcasted_iota(I32, irrep.shape, 1)
-    for label in range(7):
-        count = jnp.sum(jnp.where(irrep == label, 1.0, 0.0), axis=1, keepdims=True)
-        place = place - jnp.where(irrep > label, count.astype(I32), 0)
-    return place
+    label = lax.broadcasted_iota(I32, (8, irrep.shape[1]), 0)
+    count = jnp.sum(jnp.where(irrep == label, 1.0, 0.0), axis=1, keepdims=True)
+    start = jnp.sum(jnp.where(irrep > label, count, 0.0), axis=0, keepdims=True)
+    return lax.broadcasted_iota(I32, irrep.shape, 1) - start.astype(I32)
 
 
 def pack_kernel(
@@ -49,7 +48,8 @@
     rows, q_local, vir_total = chol.shape
     occ_total = ov.shape[1]
     own = out.shape[0]
-    per_row = out.shape[1] // rows
+    out_rows = out.shape[1]
+    per_row = 2 * GROUPS + 2
 
     @pl.when(step == 0)
     def _():
@@ -98,7 +98,7 @@
         )
         rest = mine[:, MAIN:] + jnp.where(wants[k] == occ_label, extra, 0.0)
         for q in range(2 * GROUPS):
-            stage[pl.ds(k * per_row + q, own, stride=rows * per_row), :] = mine[
+            stage[pl.ds((step * rows + k) * per_row + q, own, stride=out_rows), :] = mine[
                 q * own : (q + 1) * own, :MAIN
             ]
         for u in range(2):
@@ -106,12 +106,15 @@
             for g in range(1, GROUPS):
                 part = rest[(u * GROUPS + g) * own : (u * GROUPS + g + 1) * own]
                 total = total + pltpu.roll(part, g * STRIDE, 1)
-            at = k * per_row + 2 * GROUPS + u
-            stage[pl.ds(at, own, stride=rows * per_row), :] = total
-    out[...] = stage[...].reshape(out.shape).astype(BF)
-
-
-def amp_kernel(vir_s, occ_s, pair_s, amp, vir_irrep, out):
+            at = (step * rows + k) * per_row + 2 * GROUPS + u
+            stage[pl.ds(at, own, stride=out_rows), :] = total
+
+    @pl.when(step == pl.num_programs(0) - 1)
+    def _():
+        out[...] = stage[...].reshape(out.shape).astype(BF)
+
+
+def amp_kernel(occ_s, pair_s, amp, vir_irrep, out):
     row_count, pair_count, col_count = amp.shape
     rep_pos = lax.axis_index("rep")
     first_row = lax.axis_index("blk") * row_count
@@ -125,10 +128,11 @@
         col_place = jnp.where(rep_pos == k, place[:, cols], col_place)
     lane = lax.broadcasted_iota(I32, (2 * MAIN, col_count), 0)
     fold = jnp.where(lane == col_place, 1.0, 0.0).astype(BF)
-    row = lax.broadcasted_iota(I32, (row_count, 1), 0)
-    row_irrep = jnp.zeros((row_count, 1), I32)
-    for k in range(row_count):
-        row_irrep = jnp.where(row == k, vir_s[first_row + k], row_irrep)
+    column = lax.broadcasted_iota(I32, (row_count, vir_line.shape[1]), 1)
+    row = lax.broadcasted_iota(I32, (row_count, vir_line.shape[1]), 0)
+    row_irrep = jnp.sum(
+        jnp.where(column == row + first_row, vir_line.astype(F32), 0.0), axis=1, keepdims=True
+    ).astype(I32)
     for p in range(pair_count):
         sym = jnp.bitwise_xor(occ_s[pair_s[p, 0]], occ_s[pair_s[p, 1]])
         want = jnp.bitwise_xor(row_irrep, sym)
@@ -141,7 +145,10 @@
 def pair_kernel(
     q_irrep,
     pair_sym,
+    core,
     got,
+    amp_mine,
+    amp_other,
     row_irrep,
     col_irrep,
     row_pos,
@@ -152,6 +159,7 @@
     amps,
     unfold,
     stage,
+    halves,
 ):
     vir_total = row_irrep.shape[0]
     own = got.shape[1]
@@ -163,12 +171,18 @@
     for g in range(GROUPS):
         place = jnp.where(column < MAIN, column, column + g * STRIDE)
         unfold[g] = jnp.where(index == place, 1.0, 0.0).astype(BF)
-    amp_at = row_count * per_row
+    halves[0] = amp_mine[...]
+    halves[1] = amp_other[...]
+    half_rows = amp_mine.shape[0]
+
+    def amp_row(t):
+        return halves[jnp.bitwise_xor(core[0], t // half_rows), t % half_rows]
+
     for r in range(row_count):
         here = slice(r * own, (r + 1) * own)
-        rest_amp = got[amp_at + 2 * row_count + r].astype(F32)
+        rest_amp = amp_row(2 * row_count + r).astype(F32)
         for p in range(2):
-            main_amp = got[amp_at + p * row_count + r]
+            main_amp = amp_row(p * row_count + r)
             for g in range(GROUPS):
                 shift = (g * STRIDE - p * 64) % MAIN
                 moved = pltpu.roll(rest_amp, shift, 1) if shift else rest_amp
@@ -256,7 +270,7 @@
     amp_send = pl.pallas_call(
         amp_kernel,
         grid_spec=pltpu.PrefetchScalarGridSpec(
-            num_scalar_prefetch=3,
+            num_scalar_prefetch=2,
             grid=(1,),
             in_specs=[
                 pl.BlockSpec((row_count, 2, col_count), lambda i, *s: (0, 0, 0)),
@@ -266,12 +280,12 @@
         ),
         out_shape=jax.ShapeDtypeStruct((3, row_count, MAIN), F32),
         name="amp",
-    )(vir_irrep, occ_irrep, pair_list, amplitudes.transpose(1, 0, 2), vir_irrep)
+    )(occ_irrep, pair_list, amplitudes.transpose(1, 0, 2), vir_irrep)
     amp_rows = 32
     amp_send = over_rep(amp_send).astype(BF).reshape(3 * row_count, MAIN)
     amp_send = jnp.pad(amp_send, ((0, amp_rows - 3 * row_count), (0, 0)))
 
-    rows = 2
+    rows = 5
     packed = pl.pallas_call(
         pack_kernel,
         grid_spec=pltpu.PrefetchScalarGridSpec(
@@ -284,15 +298,15 @@
                 pl.BlockSpec((vir_total,), lambda i, *s: (0,)),
                 pl.BlockSpec(chol_irrep.shape, lambda i, *s: (0,)),
             ],
-            out_specs=pl.BlockSpec((blk_count, 8 * rows, MAIN), lambda i, *s: (0, i, 0)),
+            out_specs=pl.BlockSpec((blk_count, 8 * row_count, MAIN), lambda i, *s: (0, 0, 0)),
             scratch_shapes=[
                 pltpu.VMEM((vir_total, 2 * MAIN), BF),
                 pltpu.VMEM((q_local, MAIN), I32),
                 pltpu.VMEM((occ_total, MAIN), BF),
-                pltpu.VMEM((blk_count * 8 * rows, MAIN), F32),
+                pltpu.VMEM((blk_count * 8 * row_count, MAIN), F32),
             ],
         ),
-        out_shape=jax.ShapeDtypeStruct((blk_count, 8 * row_count + amp_rows, MAIN), BF),
+        out_shape=jax.ShapeDtypeStruct((blk_count, 8 * row_count + amp_rows // 2, MAIN), BF),
         cost_estimate=pl.CostEstimate(
             flops=2 * q_local * row_count * vir_total * 256,
             bytes_accessed=2 * q_local * row_count * vir_total,
@@ -313,12 +327,14 @@
     def swap(value):
         return lax.all_to_all(value, "blk", split_axis=0, concat_axis=0, tiled=False)
 
-    packed = lax.dynamic_update_slice(
-        packed,
-        jnp.broadcast_to(amp_send[None], (blk_count,) + amp_send.shape),
-        (0, 8 * row_count, 0),
-    )
+    amp_half = amp_rows // 2
+    amp_send = jnp.broadcast_to(
+        amp_send.reshape(1, 2, amp_half, MAIN), (blk_count // 2, 2, amp_half, MAIN)
+    ).reshape(blk_count, amp_half, MAIN)
+    packed = lax.dynamic_update_slice(packed, amp_send, (0, 8 * row_count, 0))
     got = swap(packed)
+    amp_mine = got[:, 8 * row_count :].transpose(1, 0, 2)
+    amp_other = lax.ppermute(amp_mine, "blk", [(i, i ^ 1) for i in range(blk_count)])
     vir_irrep, pair_list = lax.optimization_barrier((vir_irrep, pair_list, packed))[:2]
     starts = jnp.sum(
         (vir_irrep[None, :] < jnp.arange(8, dtype=I32)[:, None]).astype(I32), axis=1
@@ -340,7 +356,7 @@
         jnp.bitwise_xor(row_irrep[None, :, None], col_irrep[None, None, :])
         == pair_sym[:, None, None]
     )
-    got = got.transpose(1, 0, 2)
+    got = got[:, : 8 * row_count].transpose(1, 0, 2)
 
     def mixed(x):
         return x.reshape(blk_count, row_count).T.reshape(vir_total)
@@ -361,7 +377,7 @@
 
     part = pl.pallas_call(
         pair_kernel,
-        in_specs=[smem, smem] + [vmem] * 5,
+        in_specs=[smem, smem, smem] + [vmem] * 7,
         out_specs=vmem,
         out_shape=jax.ShapeDtypeStruct((blk_count, 32, MAIN), BF),
         scratch_shapes=[
@@ -370,10 +386,11 @@
             pltpu.VMEM((GROUPS, vir_total, 4 * MAIN), BF),
             pltpu.VMEM((GROUPS, 2 * MAIN, vir_total), BF),
             pltpu.VMEM((blk_count * 32, MAIN), F32),
+            pltpu.VMEM((2, amp_half, blk_count, MAIN), BF),
         ],
         compiler_params=pltpu.CompilerParams(vmem_limit_bytes=LIMIT),
         name="ladder",
-    )(own_irrep, pair_sym, got, *tables)
+    )(own_irrep, pair_sym, (blk_pos & 1)[None], got, amp_mine, amp_other, *tables)
     part = swap(part)
     summed = over_rep(jnp.sum(part.astype(F32), axis=0))
     summed = summed[: 3 * row_count].reshape(3, row_count, MAIN)

time: 121 us -> 117 us (0.967)
  waiting for transfers between devices: 57.6 us -> 54.6 us
    all_to_all x2, waiting for transfers between devices: 52.8 us -> 49.8 us  [swap(): lax.all_to_all(value, 'blk', split_axis=0, concat_axis=0, tiled=False)]
    ppermute x0 -> x1, starting transfers between devices: none -> 2.48 us  [per_device(): lax.ppermute(amp_mine, 'blk', [(i, i ^ 1) for i in range(blk_count)])]
    all_to_all x2, starting transfers between devices: 20.8 us -> 18.7 us  [swap(): lax.all_to_all(value, 'blk', split_axis=0, concat_axis=0, tiled=False)]
  transfers between devices with their start and end apart: 8 -> 9, of which waited for: 4 -> 4; matrix products, arithmetic and copies ran while one was open for 6% -> 6% of each run, Pallas kernels for 7% -> 6%
where the time goes in v6:
time: 117 us; the launch traced here: 116 us
  waiting for transfers between devices  54.6 us (47%)
  starting transfers between devices  29.8 us (25%)
  Pallas kernels  21.6 us (18%)
  local copies, waits for them, and re-layouts  7.91 us (7%)
  other arithmetic  1.41 us (1%)
    all_to_all x2, waiting for transfers between devices, swap(): lax.all_to_all(value, 'blk', split_axis=0, concat_axis=0, tiled=False)  49.8 us
    all_to_all x2, starting transfers between devices, swap(): lax.all_to_all(value, 'blk', split_axis=0, concat_axis=0, tiled=False)  18.7 us
    pallas_call x1, Pallas kernels, per_device(): pl.pallas_call(pair_kernel, in_specs=[smem, smem, smem] + [vmem] * 7, out...  11.6 us
    ppermute x6, starting transfers between devices, over_rep(): lax.ppermute(value, 'rep', [(i, (i + k) % 4) for i in range(4)])  8.65 us
    pallas_call x1, Pallas kernels, per_device(): pl.pallas_call(pack_kernel, grid_spec=pltpu.PrefetchScalarGridSpec(num_sc...  7.28 us
    ppermute x6, waiting for transfers between devices, over_rep(): lax.ppermute(value, 'rep', [(i, (i + k) % 4) for i in range(4)])  4.87 us
    pallas_call x1, Pallas kernels, per_device(): pl.pallas_call(amp_kernel, grid_spec=pltpu.PrefetchScalarGridSpec(num_sca...  2.79 us
    ppermute x1, starting transfers between devices, per_device(): lax.ppermute(amp_mine, 'blk', [(i, i ^ 1) for i in range(blk_count)])  2.48 us
  transfers between devices with their start and end apart: 9, of which 4 were waited for; matrix products, arithmetic and copies ran while one was open for 6% of the time, Pallas kernels for 6%

profile of v6, /device:TPU:6, one launch (start us, length us, event | category | flops | bytes accessed | tf_op | source)
XLA Modules:
  0.0 116.5 jit_solution(17573701174410659379)
XLA Ops:
  0.6 2.8 %amp.1 = f32[3,10,128]{2,1,0:T(8,128)} custom-call(s32[100]{0:T(128)} %occ_s.3, s32[2,2]{1,0:T(2,128)} %pair_s.3, f32[10,2,160]{2,1,0:T(2,128)} %bitcast.44, s32[640]{0:T(1024)} %vir_irrep.3), custom_call_target="tpu_custom_call" | custom-call | tf_op jit(solution)/shard_map/amp/pallas_call | solution.py:270
  3.4 3.0 %collective-permute-start.2 = (f32[3,10,128]{2,1,0:T(8,128)}, f32[3,10,128]{2,1,0:T(8,128)S(1)}, u32[]{:S(2)}, u32[]{:S(2)}) collective-permute-start(f32[3,10,128]{2,1,0:T(8,128)} %amp.1), channel_id=1, source_target_pairs={{0,3},{1,0},{2,1},{3,2},{4,7},{5,4},{6,5},{7,6},{8,11},{9,8},{10,9... | collective-permute-start | bytes 46088 | tf_op jit(solution)/shard_map/ppermute | solution.py:247
  6.4 0.6 collective-permute-start.1
  7.1 1.0 collective-permute-start
  8.1 7.3 %pack.1 = bf16[64,96,128]{2,1,0:T(8,128)(2,1)} custom-call(s32[640]{0:T(1024)} %vir_irrep.3, s32[100]{0:T(128)} %occ_s.3, s32[2,2]{1,0:T(2,128)} %pair_s.3, bf16[10,384,640]{2,1,0:T(8,128)(2,1)} %bitcast.39, bf16[10,100,384]{2,1,0:T(8,128)(2,1)} %bitcast.41, bf16[100,640]{1,0:T(8,128)(2,1)} %singles.1, s32[640]{0:T(1024)} %vir_irrep.3, s32[1536]{0:T(1024)} %chol_irrep.1), custom_call_target="tpu_custom_call" | custom-call | flops 1258291200 | bytes 4915200 | tf_op jit(solution)/shard_map/pack/pallas_call | solution.py:289
  15.5 0.8 constant_dynamic-update-slice_fusion
  16.2 12.3 %all-to-all-start = ((bf16[64,96,128]{2,1,0:T(8,128)(2,1)}), bf16[64,96,128]{2,1,0:T(8,128)(2,1)S(1)}, u32[]{:S(2)}, u32[]{:S(2)}) async-start(bf16[64,96,128]{2,1,0:T(8,128)(2,1)} %constant_dynamic-update-slice_fusion), calls=%async_computation | async-start | bytes 3145728 | tf_op jit(solution)/shard_map/all_to_all | solution.py:328
  28.6 0.8 dynamic_slice.25
  29.3 0.1 reshape.110
  29.4 0.2 dynamic-slice_reduce_fusion.q_irrep
  29.6 0.1 convert_reduce_fusion.1
  29.7 0.1 select_reduce_fusion
  29.8 0.1 reduce_sum.31
  29.9 36.2 %all-to-all-done = bf16[64,96,128]{2,1,0:T(8,128)(2,1)S(1)} async-done(((bf16[64,96,128]{2,1,0:T(8,128)(2,1)}), bf16[64,96,128]{2,1,0:T(8,128)(2,1)S(1)}, u32[]{:S(2)}, u32[]{:S(2)}) %all-to-all-start) | async-done | bytes 1572896 | tf_op jit(solution)/shard_map/all_to_all | solution.py:328
  66.1 0.1 copy.57
  66.2 2.5 %collective-permute-start.3 = (bf16[16,64,128]{2,1,0:T(8,128)(2,1)S(1)}, bf16[16,64,128]{2,1,0:T(8,128)(2,1)S(1)}, u32[]{:S(2)}, u32[]{:S(2)}) collective-permute-start(bf16[16,64,128]{2,1,0:T(8,128)(2,1)S(1)} %bitcast.37), channel_id=1, source_target_pairs={{0,4},{4,0},{8,12},{12,8},{16,20},{20,16},{24,28},{28,24},{32,36},... | collective-permute-start | bytes 786440 | tf_op jit(solution)/shard_map/ppermute | solution.py:337
  68.7 0.1 reshape.111
  68.8 0.1 copy.44
  68.9 0.1 broadcast_in_dim_reshape.13.col_irrep
  69.0 0.3 broadcast_in_dim_reshape.16.row_irrep
  69.3 0.1 copy.46
  69.3 0.1 broadcast_in_dim_reshape.15.col_pos
  69.4 0.3 broadcast_in_dim_reshape.17.row_pos
  69.7 0.2 fusion.11
  69.9 0.6 gather_fusion.1
  70.5 0.6 gather_fusion
  71.2 0.1 slice.48
  71.3 0.3 copy.56
  71.6 11.6 %ladder.1 = bf16[64,32,128]{2,1,0:T(8,128)(2,1)} custom-call(s32[6]{0:T(128)S(1)} %dynamic-slice_reduce_fusion.q_irrep, s32[2]{0:T(128)S(1)} %xor.24.pair_sym, s32[1]{0:T(128)} %bitcast.6.core, bf16[80,64,128]{2,1,0:T(8,128)(2,1)S(1)} %bitcast.36, bf16[16,64,128]{2,1,0:T(8,128)(2,1)S(1)} %bitcast.38, ...), custom_call_target="tpu_custom_call" | custom-call | tf_op jit(solution)/shard_map/ladder/pallas_call | solution.py:378
  83.2 6.4 %all-to-all-start.1 = ((bf16[64,32,128]{2,1,0:T(8,128)(2,1)}), bf16[64,32,128]{2,1,0:T(8,128)(2,1)S(1)}, u32[]{:S(2)}, u32[]{:S(2)}) async-start(bf16[64,32,128]{2,1,0:T(8,128)(2,1)} %ladder.1), calls=%async_computation.1 | async-start | bytes 1048576 | tf_op jit(solution)/shard_map/all_to_all | solution.py:328
  89.6 0.8 dynamic_slice.27
  90.4 0.8 dynamic_slice.28
  91.1 0.1 dynamic_slice.22
  91.2 0.1 dynamic_slice.23
  91.3 0.6 gather_fusion.3
  91.9 0.6 gather_fusion.2
  92.6 0.1 broadcast_subtract_fusion
  92.6 0.1 broadcast_xor_fusion
  92.7 13.6 %all-to-all-done.1 = bf16[64,32,128]{2,1,0:T(8,128)(2,1)S(1)} async-done(((bf16[64,32,128]{2,1,0:T(8,128)(2,1)}), bf16[64,32,128]{2,1,0:T(8,128)(2,1)S(1)}, u32[]{:S(2)}, u32[]{:S(2)}) %all-to-all-start.1) | async-done | bytes 524320 | tf_op jit(solution)/shard_map/all_to_all | solution.py:328
  106.3 0.1 convert_reduce_fusion
  106.4 2.3 %collective-permute-start.6 = (f32[32,128]{1,0:T(8,128)S(1)}, f32[32,128]{1,0:T(8,128)S(1)}, u32[]{:S(2)}, u32[]{:S(2)}) collective-permute-start(f32[32,128]{1,0:T(8,128)S(1)} %convert_reduce_fusion), channel_id=1, source_target_pairs={{0,3},{1,0},{2,1},{3,2},{4,7},{5,4},{6,5},{7,6},{8,11},{9,8},{10,9... | collective-permute-start | bytes 49160 | tf_op jit(solution)/shard_map/ppermute | solution.py:247
  108.8 1.7 %collective-permute-start.5 = (f32[32,128]{1,0:T(8,128)S(1)}, f32[32,128]{1,0:T(8,128)S(1)}, u32[]{:S(2)}, u32[]{:S(2)}) collective-permute-start(f32[32,128]{1,0:T(8,128)S(1)} %convert_reduce_fusion), channel_id=1, source_target_pairs={{0,2},{1,3},{2,0},{3,1},{4,6},{5,7},{6,4},{7,5},{8,10},{9,11},{10,... | collective-permute-start | bytes 49160 | tf_op jit(solution)/shard_map/ppermute | solution.py:247
  110.5 0.1 dynamic_slice.24
  110.5 3.5 %collective-permute-done.5 = f32[32,128]{1,0:T(8,128)S(1)} collective-permute-done((f32[32,128]{1,0:T(8,128)S(1)}, f32[32,128]{1,0:T(8,128)S(1)}, u32[]{:S(2)}, u32[]{:S(2)}) %collective-permute-start.5) | collective-permute-done | bytes 16416 | tf_op jit(solution)/shard_map/ppermute | solution.py:247
  114.0 1.4 %collective-permute-done.4 = f32[32,128]{1,0:T(8,128)S(1)} collective-permute-done((f32[32,128]{1,0:T(8,128)S(1)}, f32[32,128]{1,0:T(8,128)S(1)}, u32[]{:S(2)}, u32[]{:S(2)}) %collective-permute-start.4) | collective-permute-done | bytes 16416 | tf_op jit(solution)/shard_map/ppermute | solution.py:247
  115.4 0.1 slice_bitcast_fusion.1
  115.5 0.2 fusion.1
  115.7 0.7 fusion.9
  (34 shorter events, 0.2 us)
Async XLA Ops:
  0.6 90.7 %copy-start = (f32[100]{0:T(128)S(1)}, f32[100]{0:T(128)}, u32[]{:S(2)}) copy-start(f32[100]{0:T(128)} %param.14) | copy-start | bytes 1204
  3.4 11.9 %collective-permute-start.2 = (f32[3,10,128]{2,1,0:T(8,128)}, f32[3,10,128]{2,1,0:T(8,128)S(1)}, u32[]{:S(2)}, u32[]{:S(2)}) collective-permute-start(f32[3,10,128]{2,1,0:T(8,128)} %amp.1), channel_id=1, source_target_pairs={{0,3},{1,0},{2,1},{3,2},{4,7},{5,4},{6,5},{7,6},{8,11},{9,8},{10,9... | collective-permute-start | bytes 46088 | tf_op jit(solution)/shard_map/ppermute | solution.py:247
  6.4 8.9 %collective-permute-start.1 = (f32[3,10,128]{2,1,0:T(8,128)}, f32[3,10,128]{2,1,0:T(8,128)S(1)}, u32[]{:S(2)}, u32[]{:S(2)}) collective-permute-start(f32[3,10,128]{2,1,0:T(8,128)} %amp.1), channel_id=1, source_target_pairs={{0,2},{1,3},{2,0},{3,1},{4,6},{5,7},{6,4},{7,5},{8,10},{9,11},{10,... | collective-permute-start | bytes 46088 | tf_op jit(solution)/shard_map/ppermute | solution.py:247
  7.1 8.3 %collective-permute-start = (f32[3,10,128]{2,1,0:T(8,128)}, f32[3,10,128]{2,1,0:T(8,128)S(1)}, u32[]{:S(2)}, u32[]{:S(2)}) collective-permute-start(f32[3,10,128]{2,1,0:T(8,128)} %amp.1), channel_id=1, source_target_pairs={{0,1},{1,2},{2,3},{3,0},{4,5},{5,6},{6,7},{7,4},{8,9},{9,10},{10,1... | collective-permute-start | bytes 46088 | tf_op jit(solution)/shard_map/ppermute | solution.py:247
  8.1 7.3 %copy-start.3 = (f32[3,10,128]{2,1,0:T(8,128)S(1)}, f32[3,10,128]{2,1,0:T(8,128)}, u32[]{:S(2)}) copy-start(f32[3,10,128]{2,1,0:T(8,128)} %amp.1) | copy-start | bytes 46084
  16.2 13.4 %copy-start.2 = (s32[640]{0:T(1024)S(1)}, s32[640]{0:T(1024)}, u32[]{:S(2)}) copy-start(s32[640]{0:T(1024)} %vir_irrep.3) | copy-start | bytes 7684
  16.2 49.9 %all-to-all-start = ((bf16[64,96,128]{2,1,0:T(8,128)(2,1)}), bf16[64,96,128]{2,1,0:T(8,128)(2,1)S(1)}, u32[]{:S(2)}, u32[]{:S(2)}) async-start(bf16[64,96,128]{2,1,0:T(8,128)(2,1)} %constant_dynamic-update-slice_fusion), calls=%async_computation | async-start | bytes 3145728 | tf_op jit(solution)/shard_map/all_to_all | solution.py:328
  28.5 41.2 %copy-start.5 = (s32[2,2]{1,0:T(2,128)S(1)}, s32[2,2]{1,0:T(2,128)}, u32[]{:S(2)}) copy-start(s32[2,2]{1,0:T(2,128)} %pair_s.3) | copy-start | bytes 52
  28.5 41.4 %copy-start.1 = (s32[100]{0:T(128)S(1)}, s32[100]{0:T(128)}, u32[]{:S(2)}) copy-start(s32[100]{0:T(128)} %occ_s.3) | copy-start | bytes 1204
  66.2 5.4 %collective-permute-start.3 = (bf16[16,64,128]{2,1,0:T(8,128)(2,1)S(1)}, bf16[16,64,128]{2,1,0:T(8,128)(2,1)S(1)}, u32[]{:S(2)}, u32[]{:S(2)}) collective-permute-start(bf16[16,64,128]{2,1,0:T(8,128)(2,1)S(1)} %bitcast.37), channel_id=1, source_target_pairs={{0,4},{4,0},{8,12},{12,8},{16,20},{20,16},{24,28},{28,24},{32,36},... | collective-permute-start | bytes 786440 | tf_op jit(solution)/shard_map/ppermute | solution.py:337
  83.2 32.5 %copy-start.4 = (f32[2,10,160]{2,0,1:T(2,128)S(1)}, f32[2,10,160]{2,0,1:T(2,128)}, u32[]{:S(2)}) copy-start(f32[2,10,160]{2,0,1:T(2,128)} %param.10) | copy-start | bytes 38404
  83.2 23.1 %all-to-all-start.1 = ((bf16[64,32,128]{2,1,0:T(8,128)(2,1)}), bf16[64,32,128]{2,1,0:T(8,128)(2,1)S(1)}, u32[]{:S(2)}, u32[]{:S(2)}) async-start(bf16[64,32,128]{2,1,0:T(8,128)(2,1)} %ladder.1), calls=%async_computation.1 | async-start | bytes 1048576 | tf_op jit(solution)/shard_map/all_to_all | solution.py:328
  106.4 4.1 %collective-permute-start.6 = (f32[32,128]{1,0:T(8,128)S(1)}, f32[32,128]{1,0:T(8,128)S(1)}, u32[]{:S(2)}, u32[]{:S(2)}) collective-permute-start(f32[32,128]{1,0:T(8,128)S(1)} %convert_reduce_fusion), channel_id=1, source_target_pairs={{0,3},{1,0},{2,1},{3,2},{4,7},{5,4},{6,5},{7,6},{8,11},{9,8},{10,9... | collective-permute-start | bytes 49160 | tf_op jit(solution)/shard_map/ppermute | solution.py:247
  108.8 5.2 %collective-permute-start.5 = (f32[32,128]{1,0:T(8,128)S(1)}, f32[32,128]{1,0:T(8,128)S(1)}, u32[]{:S(2)}, u32[]{:S(2)}) collective-permute-start(f32[32,128]{1,0:T(8,128)S(1)} %convert_reduce_fusion), channel_id=1, source_target_pairs={{0,2},{1,3},{2,0},{3,1},{4,6},{5,7},{6,4},{7,5},{8,10},{9,11},{10,... | collective-permute-start | bytes 49160 | tf_op jit(solution)/shard_map/ppermute | solution.py:247
  110.4 4.9 %collective-permute-start.4 = (f32[32,128]{1,0:T(8,128)S(1)}, f32[32,128]{1,0:T(8,128)S(1)}, u32[]{:S(2)}, u32[]{:S(2)}) collective-permute-start(f32[32,128]{1,0:T(8,128)S(1)} %convert_reduce_fusion), channel_id=1, source_target_pairs={{0,1},{1,2},{2,3},{3,0},{4,5},{5,6},{6,7},{7,4},{8,9},{9,10},{10,1... | collective-permute-start | bytes 49160 | tf_op jit(solution)/shard_map/ppermute | solution.py:247

commit v7 on v6

--- a/solution.py
+++ b/solution.py
@@ -153,7 +153,8 @@
     col_irrep,
     row_pos,
     col_pos,
-    out,
+    keep,
+    give,
     ball,
     hall,
     amps,
@@ -216,7 +217,7 @@
                     halfway[:, p * 256 + MAIN : (p + 1) * 256] + dressed
                 ).astype(BF)
 
-    out_rows = out.shape[1]
+    out_rows = keep.shape[1]
     lane2 = lax.broadcasted_iota(I32, (vir_total, 2 * MAIN), 1)
     tail = None
     for p in range(2):
@@ -238,7 +239,10 @@
         ]
     for t in range(3 * row_count, out_rows):
         stage[pl.ds(t, own, stride=out_rows), :] = jnp.zeros((own, MAIN), F32)
-    out[...] = stage[...].reshape(out.shape).astype(BF)
+    sums = stage[...].reshape(own // 2, 2, out_rows, MAIN)
+    even = core[0] == 0
+    keep[...] = jnp.where(even, sums[:, 0], sums[:, 1])
+    give[...] = jnp.where(even, sums[:, 1], sums[:, 0]).astype(BF)
 
 
 def over_rep(value):
@@ -324,17 +328,15 @@
         chol_irrep,
     )
 
-    def swap(value):
-        return lax.all_to_all(value, "blk", split_axis=0, concat_axis=0, tiled=False)
+    siblings = [(i, i ^ 1) for i in range(blk_count)]
 
     amp_half = amp_rows // 2
     amp_send = jnp.broadcast_to(
         amp_send.reshape(1, 2, amp_half, MAIN), (blk_count // 2, 2, amp_half, MAIN)
     ).reshape(blk_count, amp_half, MAIN)
     packed = lax.dynamic_update_slice(packed, amp_send, (0, 8 * row_count, 0))
-    got = swap(packed)
+    got = lax.all_to_all(packed, "blk", split_axis=0, concat_axis=0, tiled=False)
     amp_mine = got[:, 8 * row_count :].transpose(1, 0, 2)
-    amp_other = lax.ppermute(amp_mine, "blk", [(i, i ^ 1) for i in range(blk_count)])
     vir_irrep, pair_list = lax.optimization_barrier((vir_irrep, pair_list, packed))[:2]
     starts = jnp.sum(
         (vir_irrep[None, :] < jnp.arange(8, dtype=I32)[:, None]).astype(I32), axis=1
@@ -375,11 +377,18 @@
         pos_mixed[None, :],
     )
 
-    part = pl.pallas_call(
+    amp_mine, own_irrep, pair_sym, tables = lax.optimization_barrier(
+        (amp_mine, own_irrep, pair_sym, tables)
+    )
+    amp_other = lax.ppermute(amp_mine, "blk", siblings)
+    keep, give = pl.pallas_call(
         pair_kernel,
         in_specs=[smem, smem, smem] + [vmem] * 7,
-        out_specs=vmem,
-        out_shape=jax.ShapeDtypeStruct((blk_count, 32, MAIN), BF),
+        out_specs=(vmem, vmem),
+        out_shape=(
+            jax.ShapeDtypeStruct((blk_count // 2, 32, MAIN), F32),
+            jax.ShapeDtypeStruct((blk_count // 2, 32, MAIN), BF),
+        ),
         scratch_shapes=[
             pltpu.VMEM((vir_total, 4 * GROUPS * MAIN), BF),
             pltpu.VMEM((2, vir_total, 4 * GROUPS * MAIN), BF),
@@ -391,7 +400,11 @@
         compiler_params=pltpu.CompilerParams(vmem_limit_bytes=LIMIT),
         name="ladder",
     )(own_irrep, pair_sym, (blk_pos & 1)[None], got, amp_mine, amp_other, *tables)
-    part = swap(part)
+    part = (keep + lax.ppermute(give, "blk", siblings).astype(F32)).astype(BF)
+    sides = [list(range(k, blk_count, 2)) for k in range(2)]
+    part = lax.all_to_all(
+        part, "blk", split_axis=0, concat_axis=0, axis_index_groups=sides, tiled=False
+    )
     summed = over_rep(jnp.sum(part.astype(F32), axis=0))
     summed = summed[: 3 * row_count].reshape(3, row_count, MAIN)
     short = jnp.stack(

time: 117 us -> 112 us (0.957); the launches traced: 116 us -> 110 us
  waiting for transfers between devices: 54.6 us -> 48.2 us
    all_to_all x2, waiting for transfers between devices: 49.8 us -> 41.8 us  [the longest x1 34.1 us: per_device(): lax.all_to_all(packed, 'blk', split_axis=0, concat_axis=0, tiled=False)]
    ppermute x1 -> x2, waiting for transfers between devices: 0.01 us -> 1.53 us  [the longest x1 1.17 us: per_device(): part = (keep + lax.ppermute(give, 'blk', siblings).astype(F32)).astype(BF)]
    ppermute x1 -> x2, starting transfers between devices: 2.48 us -> 2.93 us  [the longest x1 2.48 us: per_device(): amp_other = lax.ppermute(amp_mine, 'blk', siblings)]
  transfers between devices with their start and end apart: 9 -> 10, of which waited for: 4 -> 6; matrix products, arithmetic and copies ran while one was open for 6% -> 7% of each run, Pallas kernels for 6% -> 7%
where the time goes in v7:
time: 112 us; the launch traced here: 110 us
  waiting for transfers between devices  48.2 us (43%)
  starting transfers between devices  29.8 us (27%)
  Pallas kernels  20.9 us (19%)
  local copies, waits for them, and re-layouts  7.89 us (7%)
  other arithmetic  2.15 us (2%)
    all_to_all x1, waiting for transfers between devices, per_device(): lax.all_to_all(packed, 'blk', split_axis=0, concat_axis=0, tiled=False)  34.1 us
    all_to_all x1, starting transfers between devices, per_device(): lax.all_to_all(packed, 'blk', split_axis=0, concat_axis=0, tiled=False)  12.3 us
    pallas_call x1, Pallas kernels, per_device(): pl.pallas_call(pair_kernel, in_specs=[smem, smem, smem] + [vmem] * 7, out...  10.8 us
    ppermute x6, starting transfers between devices, over_rep(): lax.ppermute(value, 'rep', [(i, (i + k) % 4) for i in range(4)])  8.65 us
    all_to_all x1, waiting for transfers between devices, per_device(): lax.all_to_all(part, 'blk', split_axis=0, concat_axis=0, axis_index_group...  7.73 us
    pallas_call x1, Pallas kernels, per_device(): pl.pallas_call(pack_kernel, grid_spec=pltpu.PrefetchScalarGridSpec(num_sc...  7.31 us
    all_to_all x1, starting transfers between devices, per_device(): lax.all_to_all(part, 'blk', split_axis=0, concat_axis=0, axis_index_group...  5.93 us
    ppermute x6, waiting for transfers between devices, over_rep(): lax.ppermute(value, 'rep', [(i, (i + k) % 4) for i in range(4)])  4.87 us
  transfers between devices with their start and end apart: 10, of which 6 were waited for; matrix products, arithmetic and copies ran while one was open for 7% of the time, Pallas kernels for 7%

profile of v7, /device:TPU:6, one launch (start us, length us, event | category | flops | bytes accessed | tf_op | source)
XLA Modules:
  0.0 109.9 jit_solution(2220821410253646896)
XLA Ops:
  0.6 2.8 %amp.1 = f32[3,10,128]{2,1,0:T(8,128)} custom-call(s32[100]{0:T(128)} %occ_s.3, s32[2,2]{1,0:T(2,128)} %pair_s.3, f32[10,2,160]{2,1,0:T(2,128)} %bitcast.44, s32[640]{0:T(1024)} %vir_irrep.3), custom_call_target="tpu_custom_call" | custom-call | tf_op jit(solution)/shard_map/amp/pallas_call | solution.py:274
  3.4 3.0 %collective-permute-start.2 = (f32[3,10,128]{2,1,0:T(8,128)}, f32[3,10,128]{2,1,0:T(8,128)S(1)}, u32[]{:S(2)}, u32[]{:S(2)}) collective-permute-start(f32[3,10,128]{2,1,0:T(8,128)} %amp.1), channel_id=1, source_target_pairs={{0,3},{1,0},{2,1},{3,2},{4,7},{5,4},{6,5},{7,6},{8,11},{9,8},{10,9... | collective-permute-start | bytes 46088 | tf_op jit(solution)/shard_map/ppermute | solution.py:251
  6.4 0.6 collective-permute-start.1
  7.1 1.0 collective-permute-start
  8.1 7.3 %pack.1 = bf16[64,96,128]{2,1,0:T(8,128)(2,1)} custom-call(s32[640]{0:T(1024)} %vir_irrep.3, s32[100]{0:T(128)} %occ_s.3, s32[2,2]{1,0:T(2,128)} %pair_s.3, bf16[10,384,640]{2,1,0:T(8,128)(2,1)} %bitcast.39, bf16[10,100,384]{2,1,0:T(8,128)(2,1)} %bitcast.41, bf16[100,640]{1,0:T(8,128)(2,1)} %singles.1, s32[640]{0:T(1024)} %vir_irrep.3, s32[1536]{0:T(1024)} %chol_irrep.1), custom_call_target="tpu_custom_call" | custom-call | flops 1258291200 | bytes 4915200 | tf_op jit(solution)/shard_map/pack/pallas_call | solution.py:293
  15.5 0.8 constant_dynamic-update-slice_fusion
  16.3 12.3 %all-to-all-start = ((bf16[64,96,128]{2,1,0:T(8,128)(2,1)}), bf16[64,96,128]{2,1,0:T(8,128)(2,1)S(1)}, u32[]{:S(2)}, u32[]{:S(2)}) async-start(bf16[64,96,128]{2,1,0:T(8,128)(2,1)} %constant_dynamic-update-slice_fusion), calls=%async_computation | async-start | bytes 3145728 | tf_op jit(solution)/shard_map/all_to_all | solution.py:338
  28.6 0.8 dynamic_slice.25
  29.4 0.1 reshape.110
  29.4 0.2 dynamic-slice_reduce_fusion.q_irrep
  29.6 0.1 convert_reduce_fusion.1
  29.8 0.1 select_reduce_fusion
  29.8 0.1 reduce_sum.31
  30.1 0.1 broadcast_in_dim_reshape.15.col_pos
  30.1 0.1 broadcast_in_dim_reshape.14
  30.2 0.1 reshape.111
  30.4 0.1 broadcast_in_dim_reshape.13.col_irrep
  30.5 0.1 broadcast_in_dim_reshape.12
  30.6 0.2 fusion.11
  30.8 0.6 gather_fusion.1
  31.5 0.6 gather_fusion
  32.1 34.1 %all-to-all-done = bf16[64,96,128]{2,1,0:T(8,128)(2,1)S(1)} async-done(((bf16[64,96,128]{2,1,0:T(8,128)(2,1)}), bf16[64,96,128]{2,1,0:T(8,128)(2,1)S(1)}, u32[]{:S(2)}, u32[]{:S(2)}) %all-to-all-start) | async-done | bytes 1572896 | tf_op jit(solution)/shard_map/all_to_all | solution.py:338
  66.3 2.5 %collective-permute-start.3 = (bf16[16,64,128]{2,1,0:T(8,128)(2,1)S(1)}, bf16[16,64,128]{2,1,0:T(8,128)(2,1)S(1)}, u32[]{:S(2)}, u32[]{:S(2)}) collective-permute-start(bf16[16,64,128]{2,1,0:T(8,128)(2,1)S(1)} %bitcast.37), channel_id=1, source_target_pairs={{0,4},{4,0},{8,12},{12,8},{16,20},{20,16},{24,28},{28,24},{32,36},... | collective-permute-start | bytes 786440 | tf_op jit(solution)/shard_map/ppermute | solution.py:383
  68.7 0.1 slice.49
  68.8 0.3 copy.56
  69.2 0.2 copy.48.row_irrep
  69.3 0.2 copy.49.row_pos
  69.5 0.4 collective-permute-done.3.amp_other
  69.9 10.8 %ladder.1 = (f32[32,32,128]{2,1,0:T(8,128)S(1)}, bf16[32,32,128]{2,1,0:T(8,128)(2,1)S(1)}) custom-call(s32[6]{0:T(128)S(1)} %dynamic-slice_reduce_fusion.q_irrep, s32[2]{0:T(128)S(1)} %xor.28.pair_sym, s32[1]{0:T(128)} %bitcast.9.core, bf16[80,64,128]{2,1,0:T(8,128)(2,1)S(1)} %bitcast.36, bf16[16,64,128]{2,1,0:T(8,128)(2,1)S(1)} %bitcast.38, ...), custom_call_target="tpu_custom_call" | custom-call | tf_op jit(solution)/shard_map/ladder/pallas_call | solution.py:384
  80.7 0.5 collective-permute-start.4
  81.1 1.2 %collective-permute-done.4 = bf16[32,32,128]{2,1,0:T(8,128)(2,1)S(1)} collective-permute-done((bf16[32,32,128]{2,1,0:T(8,128)(2,1)S(1)}, bf16[32,32,128]{2,1,0:T(8,128)(2,1)S(1)}, u32[]{:S(2)}, u32[]{:S(2)}) %collective-permute-start.4) | collective-permute-done | bytes 262176 | tf_op jit(solution)/shard_map/ppermute | solution.py:403
  82.3 0.8 add_convert_fusion
  83.1 5.9 %all-to-all-start.1 = ((bf16[32,32,128]{2,1,0:T(8,128)(2,1)}), bf16[32,32,128]{2,1,0:T(8,128)(2,1)S(1)}, u32[]{:S(2)}, u32[]{:S(2)}) async-start(bf16[32,32,128]{2,1,0:T(8,128)(2,1)} %add_convert_fusion), calls=%async_computation.1 | async-start | bytes 524288 | tf_op jit(solution)/shard_map/all_to_all | solution.py:405
  89.0 0.8 dynamic_slice.27
  89.8 0.8 dynamic_slice.28
  90.5 0.1 dynamic_slice.22
  90.6 0.1 dynamic_slice.23
  90.7 0.6 gather_fusion.3
  91.3 0.6 gather_fusion.2
  92.0 0.1 broadcast_subtract_fusion
  92.1 7.7 %all-to-all-done.1 = bf16[32,32,128]{2,1,0:T(8,128)(2,1)S(1)} async-done(((bf16[32,32,128]{2,1,0:T(8,128)(2,1)}), bf16[32,32,128]{2,1,0:T(8,128)(2,1)S(1)}, u32[]{:S(2)}, u32[]{:S(2)}) %all-to-all-start.1) | async-done | bytes 262176 | tf_op jit(solution)/shard_map/all_to_all | solution.py:405
  99.9 2.3 %collective-permute-start.7 = (f32[32,128]{1,0:T(8,128)S(1)}, f32[32,128]{1,0:T(8,128)S(1)}, u32[]{:S(2)}, u32[]{:S(2)}) collective-permute-start(f32[32,128]{1,0:T(8,128)S(1)} %convert_reduce_fusion), channel_id=1, source_target_pairs={{0,3},{1,0},{2,1},{3,2},{4,7},{5,4},{6,5},{7,6},{8,11},{9,8},{10,9... | collective-permute-start | bytes 49160 | tf_op jit(solution)/shard_map/ppermute | solution.py:251
  102.2 1.7 %collective-permute-start.6 = (f32[32,128]{1,0:T(8,128)S(1)}, f32[32,128]{1,0:T(8,128)S(1)}, u32[]{:S(2)}, u32[]{:S(2)}) collective-permute-start(f32[32,128]{1,0:T(8,128)S(1)} %convert_reduce_fusion), channel_id=1, source_target_pairs={{0,2},{1,3},{2,0},{3,1},{4,6},{5,7},{6,4},{7,5},{8,10},{9,11},{10,... | collective-permute-start | bytes 49160 | tf_op jit(solution)/shard_map/ppermute | solution.py:251
  103.9 0.1 dynamic_slice.24
  104.0 3.5 %collective-permute-done.6 = f32[32,128]{1,0:T(8,128)S(1)} collective-permute-done((f32[32,128]{1,0:T(8,128)S(1)}, f32[32,128]{1,0:T(8,128)S(1)}, u32[]{:S(2)}, u32[]{:S(2)}) %collective-permute-start.6) | collective-permute-done | bytes 16416 | tf_op jit(solution)/shard_map/ppermute | solution.py:251
  107.5 1.4 %collective-permute-done.5 = f32[32,128]{1,0:T(8,128)S(1)} collective-permute-done((f32[32,128]{1,0:T(8,128)S(1)}, f32[32,128]{1,0:T(8,128)S(1)}, u32[]{:S(2)}, u32[]{:S(2)}) %collective-permute-start.5) | collective-permute-done | bytes 16416 | tf_op jit(solution)/shard_map/ppermute | solution.py:251
  109.0 0.2 fusion.1
  109.2 0.7 fusion.9
  (39 shorter events, 0.6 us)
Async XLA Ops:
  0.6 90.1 %copy-start = (f32[100]{0:T(128)S(1)}, f32[100]{0:T(128)}, u32[]{:S(2)}) copy-start(f32[100]{0:T(128)} %param.14) | copy-start | bytes 1204
  3.4 11.9 %collective-permute-start.2 = (f32[3,10,128]{2,1,0:T(8,128)}, f32[3,10,128]{2,1,0:T(8,128)S(1)}, u32[]{:S(2)}, u32[]{:S(2)}) collective-permute-start(f32[3,10,128]{2,1,0:T(8,128)} %amp.1), channel_id=1, source_target_pairs={{0,3},{1,0},{2,1},{3,2},{4,7},{5,4},{6,5},{7,6},{8,11},{9,8},{10,9... | collective-permute-start | bytes 46088 | tf_op jit(solution)/shard_map/ppermute | solution.py:251
  6.4 8.9 %collective-permute-start.1 = (f32[3,10,128]{2,1,0:T(8,128)}, f32[3,10,128]{2,1,0:T(8,128)S(1)}, u32[]{:S(2)}, u32[]{:S(2)}) collective-permute-start(f32[3,10,128]{2,1,0:T(8,128)} %amp.1), channel_id=1, source_target_pairs={{0,2},{1,3},{2,0},{3,1},{4,6},{5,7},{6,4},{7,5},{8,10},{9,11},{10,... | collective-permute-start | bytes 46088 | tf_op jit(solution)/shard_map/ppermute | solution.py:251
  7.1 8.3 %collective-permute-start = (f32[3,10,128]{2,1,0:T(8,128)}, f32[3,10,128]{2,1,0:T(8,128)S(1)}, u32[]{:S(2)}, u32[]{:S(2)}) collective-permute-start(f32[3,10,128]{2,1,0:T(8,128)} %amp.1), channel_id=1, source_target_pairs={{0,1},{1,2},{2,3},{3,0},{4,5},{5,6},{6,7},{7,4},{8,9},{9,10},{10,1... | collective-permute-start | bytes 46088 | tf_op jit(solution)/shard_map/ppermute | solution.py:251
  8.0 7.3 %copy-start.3 = (f32[3,10,128]{2,1,0:T(8,128)S(1)}, f32[3,10,128]{2,1,0:T(8,128)}, u32[]{:S(2)}) copy-start(f32[3,10,128]{2,1,0:T(8,128)} %amp.1) | copy-start | bytes 46084
  16.3 13.4 %copy-start.2 = (s32[640]{0:T(1024)S(1)}, s32[640]{0:T(1024)}, u32[]{:S(2)}) copy-start(s32[640]{0:T(1024)} %vir_irrep.3) | copy-start | bytes 7684
  16.3 14.3 %copy-start.5 = (s32[2,2]{1,0:T(2,128)S(1)}, s32[2,2]{1,0:T(2,128)}, u32[]{:S(2)}) copy-start(s32[2,2]{1,0:T(2,128)} %pair_s.3) | copy-start | bytes 52
  16.3 14.5 %copy-start.1 = (s32[100]{0:T(128)S(1)}, s32[100]{0:T(128)}, u32[]{:S(2)}) copy-start(s32[100]{0:T(128)} %occ_s.3) | copy-start | bytes 1204
  16.3 49.9 %all-to-all-start = ((bf16[64,96,128]{2,1,0:T(8,128)(2,1)}), bf16[64,96,128]{2,1,0:T(8,128)(2,1)S(1)}, u32[]{:S(2)}, u32[]{:S(2)}) async-start(bf16[64,96,128]{2,1,0:T(8,128)(2,1)} %constant_dynamic-update-slice_fusion), calls=%async_computation | async-start | bytes 3145728 | tf_op jit(solution)/shard_map/all_to_all | solution.py:338
  66.3 3.6 %collective-permute-start.3 = (bf16[16,64,128]{2,1,0:T(8,128)(2,1)S(1)}, bf16[16,64,128]{2,1,0:T(8,128)(2,1)S(1)}, u32[]{:S(2)}, u32[]{:S(2)}) collective-permute-start(bf16[16,64,128]{2,1,0:T(8,128)(2,1)S(1)} %bitcast.37), channel_id=1, source_target_pairs={{0,4},{4,0},{8,12},{12,8},{16,20},{20,16},{24,28},{28,24},{32,36},... | collective-permute-start | bytes 786440 | tf_op jit(solution)/shard_map/ppermute | solution.py:383
  80.7 1.6 %collective-permute-start.4 = (bf16[32,32,128]{2,1,0:T(8,128)(2,1)S(1)}, bf16[32,32,128]{2,1,0:T(8,128)(2,1)S(1)}, u32[]{:S(2)}, u32[]{:S(2)}) collective-permute-start(bf16[32,32,128]{2,1,0:T(8,128)(2,1)S(1)} %get-tuple-element.23), channel_id=1, source_target_pairs={{0,4},{4,0},{8,12},{12,8},{16,20},{20,16},{24,28},{28,24},{32,36},... | collective-permute-start | bytes 786440 | tf_op jit(solution)/shard_map/ppermute | solution.py:403
  82.3 26.9 %copy-start.4 = (f32[2,10,160]{2,0,1:T(2,128)S(1)}, f32[2,10,160]{2,0,1:T(2,128)}, u32[]{:S(2)}) copy-start(f32[2,10,160]{2,0,1:T(2,128)} %param.10) | copy-start | bytes 38404
  83.1 16.8 %all-to-all-start.1 = ((bf16[32,32,128]{2,1,0:T(8,128)(2,1)}), bf16[32,32,128]{2,1,0:T(8,128)(2,1)S(1)}, u32[]{:S(2)}, u32[]{:S(2)}) async-start(bf16[32,32,128]{2,1,0:T(8,128)(2,1)} %add_convert_fusion), calls=%async_computation.1 | async-start | bytes 524288 | tf_op jit(solution)/shard_map/all_to_all | solution.py:405
  99.9 4.1 %collective-permute-start.7 = (f32[32,128]{1,0:T(8,128)S(1)}, f32[32,128]{1,0:T(8,128)S(1)}, u32[]{:S(2)}, u32[]{:S(2)}) collective-permute-start(f32[32,128]{1,0:T(8,128)S(1)} %convert_reduce_fusion), channel_id=1, source_target_pairs={{0,3},{1,0},{2,1},{3,2},{4,7},{5,4},{6,5},{7,6},{8,11},{9,8},{10,9... | collective-permute-start | bytes 49160 | tf_op jit(solution)/shard_map/ppermute | solution.py:251
  102.2 5.2 %collective-permute-start.6 = (f32[32,128]{1,0:T(8,128)S(1)}, f32[32,128]{1,0:T(8,128)S(1)}, u32[]{:S(2)}, u32[]{:S(2)}) collective-permute-start(f32[32,128]{1,0:T(8,128)S(1)} %convert_reduce_fusion), channel_id=1, source_target_pairs={{0,2},{1,3},{2,0},{3,1},{4,6},{5,7},{6,4},{7,5},{8,10},{9,11},{10,... | collective-permute-start | bytes 49160 | tf_op jit(solution)/shard_map/ppermute | solution.py:251
  103.9 4.9 %collective-permute-start.5 = (f32[32,128]{1,0:T(8,128)S(1)}, f32[32,128]{1,0:T(8,128)S(1)}, u32[]{:S(2)}, u32[]{:S(2)}) collective-permute-start(f32[32,128]{1,0:T(8,128)S(1)} %convert_reduce_fusion), channel_id=1, source_target_pairs={{0,1},{1,2},{2,3},{3,0},{4,5},{5,6},{6,7},{7,4},{8,9},{9,10},{10,1... | collective-permute-start | bytes 49160 | tf_op jit(solution)/shard_map/ppermute | solution.py:251

commit v8 on v7

--- a/solution.py
+++ b/solution.py
@@ -250,6 +250,12 @@
     for k in (1, 2, 3):
         total = total + lax.ppermute(value, "rep", [(i, (i + k) % 4) for i in range(4)])
     return total
+
+
+def over_rep_pairs(value):
+    for partner in ((1, 0, 3, 2), (3, 2, 1, 0)):
+        value = value + lax.ppermute(value, "rep", list(enumerate(partner)))
+    return value
 
 
 def per_device(
@@ -405,7 +411,7 @@
     part = lax.all_to_all(
         part, "blk", split_axis=0, concat_axis=0, axis_index_groups=sides, tiled=False
     )
-    summed = over_rep(jnp.sum(part.astype(F32), axis=0))
+    summed = over_rep_pairs(jnp.sum(part.astype(F32), axis=0))
     summed = summed[: 3 * row_count].reshape(3, row_count, MAIN)
     short = jnp.stack(
         [

time: 112 us -> 112 us (level)
    ppermute x6 -> x3, waiting for transfers between devices: 4.87 us -> 0.01 us  [over_rep(): lax.ppermute(value, 'rep', [(i, (i + k) % 4) for i in range(4)])]
    ppermute x0 -> x2, waiting for transfers between devices: none -> 4.36 us  [over_rep_pairs(): value = value + lax.ppermute(value, 'rep', list(enumerate(partner)))]
    ppermute x0 -> x2, starting transfers between devices: none -> 4.26 us  [over_rep_pairs(): value = value + lax.ppermute(value, 'rep', list(enumerate(partner)))]
    ppermute x6 -> x3, starting transfers between devices: 8.65 us -> 4.61 us  [over_rep(): lax.ppermute(value, 'rep', [(i, (i + k) % 4) for i in range(4)])]
  transfers between devices with their start and end apart: 10 -> 9, of which waited for: 6 -> 6; matrix products, arithmetic and copies ran while one was open for 7% -> 7% of each run, Pallas kernels for 7% -> 7%
where the time goes in v8:
time: 112 us; the launch traced here: 110 us
  waiting for transfers between devices  47.8 us (43%)
  starting transfers between devices  30 us (27%)
  Pallas kernels  20.8 us (19%)
  local copies, waits for them, and re-layouts  7.88 us (7%)
  other arithmetic  2.14 us (2%)
    all_to_all x1, waiting for transfers between devices, per_device(): lax.all_to_all(packed, 'blk', split_axis=0, concat_axis=0, tiled=False)  34.1 us
    all_to_all x1, starting transfers between devices, per_device(): lax.all_to_all(packed, 'blk', split_axis=0, concat_axis=0, tiled=False)  12.3 us
    pallas_call x1, Pallas kernels, per_device(): pl.pallas_call(pair_kernel, in_specs=[smem, smem, smem] + [vmem] * 7, out...  10.8 us
    all_to_all x1, waiting for transfers between devices, per_device(): lax.all_to_all(part, 'blk', split_axis=0, concat_axis=0, axis_index_group...  7.81 us
    pallas_call x1, Pallas kernels, per_device(): pl.pallas_call(pack_kernel, grid_spec=pltpu.PrefetchScalarGridSpec(num_sc...  7.28 us
    all_to_all x1, starting transfers between devices, per_device(): lax.all_to_all(part, 'blk', split_axis=0, concat_axis=0, axis_index_group...  5.93 us
    ppermute x3, starting transfers between devices, over_rep(): lax.ppermute(value, 'rep', [(i, (i + k) % 4) for i in range(4)])  4.61 us
    ppermute x2, waiting for transfers between devices, over_rep_pairs(): value = value + lax.ppermute(value, 'rep', list(enumerate(partner)))  4.36 us
  transfers between devices with their start and end apart: 9, of which 6 were waited for; matrix products, arithmetic and copies ran while one was open for 7% of the time, Pallas kernels for 7%

profile of v8, /device:TPU:6, one launch (start us, length us, event | category | flops | bytes accessed | tf_op | source)
XLA Modules:
  0.0 109.7 jit_solution(9260579767171984808)
XLA Ops:
  0.6 2.8 %amp.1 = f32[3,10,128]{2,1,0:T(8,128)} custom-call(s32[100]{0:T(128)} %occ_s.3, s32[2,2]{1,0:T(2,128)} %pair_s.3, f32[10,2,160]{2,1,0:T(2,128)} %bitcast.44, s32[640]{0:T(1024)} %vir_irrep.3), custom_call_target="tpu_custom_call" | custom-call | tf_op jit(solution)/shard_map/amp/pallas_call | solution.py:280
  3.4 3.0 %collective-permute-start.2 = (f32[3,10,128]{2,1,0:T(8,128)}, f32[3,10,128]{2,1,0:T(8,128)S(1)}, u32[]{:S(2)}, u32[]{:S(2)}) collective-permute-start(f32[3,10,128]{2,1,0:T(8,128)} %amp.1), channel_id=1, source_target_pairs={{0,3},{1,0},{2,1},{3,2},{4,7},{5,4},{6,5},{7,6},{8,11},{9,8},{10,9... | collective-permute-start | bytes 46088 | tf_op jit(solution)/shard_map/ppermute | solution.py:251
  6.4 0.6 collective-permute-start.1
  7.1 1.0 collective-permute-start
  8.0 7.3 %pack.1 = bf16[64,96,128]{2,1,0:T(8,128)(2,1)} custom-call(s32[640]{0:T(1024)} %vir_irrep.3, s32[100]{0:T(128)} %occ_s.3, s32[2,2]{1,0:T(2,128)} %pair_s.3, bf16[10,384,640]{2,1,0:T(8,128)(2,1)} %bitcast.39, bf16[10,100,384]{2,1,0:T(8,128)(2,1)} %bitcast.41, bf16[100,640]{1,0:T(8,128)(2,1)} %singles.1, s32[640]{0:T(1024)} %vir_irrep.3, s32[1536]{0:T(1024)} %chol_irrep.1), custom_call_target="tpu_custom_call" | custom-call | flops 1258291200 | bytes 4915200 | tf_op jit(solution)/shard_map/pack/pallas_call | solution.py:299
  15.4 0.8 constant_dynamic-update-slice_fusion
  16.2 12.3 %all-to-all-start = ((bf16[64,96,128]{2,1,0:T(8,128)(2,1)}), bf16[64,96,128]{2,1,0:T(8,128)(2,1)S(1)}, u32[]{:S(2)}, u32[]{:S(2)}) async-start(bf16[64,96,128]{2,1,0:T(8,128)(2,1)} %constant_dynamic-update-slice_fusion), calls=%async_computation | async-start | bytes 3145728 | tf_op jit(solution)/shard_map/all_to_all | solution.py:344
  28.6 0.8 dynamic_slice.25
  29.3 0.1 reshape.110
  29.4 0.2 dynamic-slice_reduce_fusion.q_irrep
  29.6 0.1 convert_reduce_fusion.1
  29.7 0.1 select_reduce_fusion
  29.8 0.1 reduce_sum.31
  30.0 0.1 broadcast_in_dim_reshape.15.col_pos
  30.1 0.1 broadcast_in_dim_reshape.14
  30.2 0.1 reshape.111
  30.3 0.1 copy.43
  30.4 0.1 broadcast_in_dim_reshape.13.col_irrep
  30.5 0.1 broadcast_in_dim_reshape.12
  30.6 0.2 fusion.11
  30.8 0.6 gather_fusion.1
  31.4 0.6 gather_fusion
  32.1 34.1 %all-to-all-done = bf16[64,96,128]{2,1,0:T(8,128)(2,1)S(1)} async-done(((bf16[64,96,128]{2,1,0:T(8,128)(2,1)}), bf16[64,96,128]{2,1,0:T(8,128)(2,1)S(1)}, u32[]{:S(2)}, u32[]{:S(2)}) %all-to-all-start) | async-done | bytes 1572896 | tf_op jit(solution)/shard_map/all_to_all | solution.py:344
  66.2 2.5 %collective-permute-start.3 = (bf16[16,64,128]{2,1,0:T(8,128)(2,1)S(1)}, bf16[16,64,128]{2,1,0:T(8,128)(2,1)S(1)}, u32[]{:S(2)}, u32[]{:S(2)}) collective-permute-start(bf16[16,64,128]{2,1,0:T(8,128)(2,1)S(1)} %bitcast.37), channel_id=1, source_target_pairs={{0,4},{4,0},{8,12},{12,8},{16,20},{20,16},{24,28},{28,24},{32,36},... | collective-permute-start | bytes 786440 | tf_op jit(solution)/shard_map/ppermute | solution.py:389
  68.7 0.1 slice.49
  68.8 0.3 copy.56
  69.1 0.2 copy.48.row_irrep
  69.3 0.2 copy.49.row_pos
  69.5 0.4 collective-permute-done.3.amp_other
  69.9 10.8 %ladder.1 = (f32[32,32,128]{2,1,0:T(8,128)S(1)}, bf16[32,32,128]{2,1,0:T(8,128)(2,1)S(1)}) custom-call(s32[6]{0:T(128)S(1)} %dynamic-slice_reduce_fusion.q_irrep, s32[2]{0:T(128)S(1)} %xor.28.pair_sym, s32[1]{0:T(128)} %bitcast.9.core, bf16[80,64,128]{2,1,0:T(8,128)(2,1)S(1)} %bitcast.36, bf16[16,64,128]{2,1,0:T(8,128)(2,1)S(1)} %bitcast.38, ...), custom_call_target="tpu_custom_call" | custom-call | tf_op jit(solution)/shard_map/ladder/pallas_call | solution.py:390
  80.6 0.5 collective-permute-start.4
  81.1 1.2 %collective-permute-done.4 = bf16[32,32,128]{2,1,0:T(8,128)(2,1)S(1)} collective-permute-done((bf16[32,32,128]{2,1,0:T(8,128)(2,1)S(1)}, bf16[32,32,128]{2,1,0:T(8,128)(2,1)S(1)}, u32[]{:S(2)}, u32[]{:S(2)}) %collective-permute-start.4) | collective-permute-done | bytes 262176 | tf_op jit(solution)/shard_map/ppermute | solution.py:409
  82.3 0.8 add_convert_fusion
  83.0 5.9 %all-to-all-start.1 = ((bf16[32,32,128]{2,1,0:T(8,128)(2,1)}), bf16[32,32,128]{2,1,0:T(8,128)(2,1)S(1)}, u32[]{:S(2)}, u32[]{:S(2)}) async-start(bf16[32,32,128]{2,1,0:T(8,128)(2,1)} %add_convert_fusion), calls=%async_computation.1 | async-start | bytes 524288 | tf_op jit(solution)/shard_map/all_to_all | solution.py:411
  89.0 0.8 dynamic_slice.27
  89.7 0.8 dynamic_slice.28
  90.5 0.1 dynamic_slice.22
  90.6 0.1 dynamic_slice.23
  90.6 0.6 gather_fusion.3
  91.3 0.6 gather_fusion.2
  92.0 7.8 %all-to-all-done.1 = bf16[32,32,128]{2,1,0:T(8,128)(2,1)S(1)} async-done(((bf16[32,32,128]{2,1,0:T(8,128)(2,1)}), bf16[32,32,128]{2,1,0:T(8,128)(2,1)S(1)}, u32[]{:S(2)}, u32[]{:S(2)}) %all-to-all-start.1) | async-done | bytes 262176 | tf_op jit(solution)/shard_map/all_to_all | solution.py:411
  99.9 2.0 %collective-permute-start.5 = (f32[32,128]{1,0:T(8,128)S(1)}, f32[32,128]{1,0:T(8,128)S(1)}, u32[]{:S(2)}, u32[]{:S(2)}) collective-permute-start(f32[32,128]{1,0:T(8,128)S(1)} %convert_reduce_fusion), channel_id=1, source_target_pairs={{0,1},{1,0},{2,3},{3,2},{4,5},{5,4},{6,7},{7,6},{8,9},{9,8},{10,11... | collective-permute-start | bytes 49160 | tf_op jit(solution)/shard_map/ppermute | solution.py:257
  101.9 1.8 %collective-permute-done.5 = f32[32,128]{1,0:T(8,128)S(1)} collective-permute-done((f32[32,128]{1,0:T(8,128)S(1)}, f32[32,128]{1,0:T(8,128)S(1)}, u32[]{:S(2)}, u32[]{:S(2)}) %collective-permute-start.5) | collective-permute-done | bytes 16416 | tf_op jit(solution)/shard_map/ppermute | solution.py:257
  103.7 2.3 %collective-permute-start.6 = (f32[32,128]{1,0:T(8,128)S(1)}, f32[32,128]{1,0:T(8,128)S(1)}, u32[]{:S(2)}, u32[]{:S(2)}) collective-permute-start(f32[32,128]{1,0:T(8,128)S(1)} %add.67), channel_id=1, source_target_pairs={{0,3},{1,2},{2,1},{3,0},{4,7},{5,6},{6,5},{7,4},{8,11},{9,10},{10,... | collective-permute-start | bytes 49160 | tf_op jit(solution)/shard_map/ppermute | solution.py:257
  106.0 0.1 dynamic_slice.24
  106.0 2.6 %collective-permute-done.6 = f32[32,128]{1,0:T(8,128)S(1)} collective-permute-done((f32[32,128]{1,0:T(8,128)S(1)}, f32[32,128]{1,0:T(8,128)S(1)}, u32[]{:S(2)}, u32[]{:S(2)}) %collective-permute-start.6) | collective-permute-done | bytes 16416 | tf_op jit(solution)/shard_map/ppermute | solution.py:257
  108.7 0.2 fusion.1
  109.0 0.7 fusion.9
  (38 shorter events, 0.6 us)
Async XLA Ops:
  0.6 90.0 %copy-start = (f32[100]{0:T(128)S(1)}, f32[100]{0:T(128)}, u32[]{:S(2)}) copy-start(f32[100]{0:T(128)} %param.14) | copy-start | bytes 1204
  3.4 11.9 %collective-permute-start.2 = (f32[3,10,128]{2,1,0:T(8,128)}, f32[3,10,128]{2,1,0:T(8,128)S(1)}, u32[]{:S(2)}, u32[]{:S(2)}) collective-permute-start(f32[3,10,128]{2,1,0:T(8,128)} %amp.1), channel_id=1, source_target_pairs={{0,3},{1,0},{2,1},{3,2},{4,7},{5,4},{6,5},{7,6},{8,11},{9,8},{10,9... | collective-permute-start | bytes 46088 | tf_op jit(solution)/shard_map/ppermute | solution.py:251
  6.4 8.9 %collective-permute-start.1 = (f32[3,10,128]{2,1,0:T(8,128)}, f32[3,10,128]{2,1,0:T(8,128)S(1)}, u32[]{:S(2)}, u32[]{:S(2)}) collective-permute-start(f32[3,10,128]{2,1,0:T(8,128)} %amp.1), channel_id=1, source_target_pairs={{0,2},{1,3},{2,0},{3,1},{4,6},{5,7},{6,4},{7,5},{8,10},{9,11},{10,... | collective-permute-start | bytes 46088 | tf_op jit(solution)/shard_map/ppermute | solution.py:251
  7.1 8.3 %collective-permute-start = (f32[3,10,128]{2,1,0:T(8,128)}, f32[3,10,128]{2,1,0:T(8,128)S(1)}, u32[]{:S(2)}, u32[]{:S(2)}) collective-permute-start(f32[3,10,128]{2,1,0:T(8,128)} %amp.1), channel_id=1, source_target_pairs={{0,1},{1,2},{2,3},{3,0},{4,5},{5,6},{6,7},{7,4},{8,9},{9,10},{10,1... | collective-permute-start | bytes 46088 | tf_op jit(solution)/shard_map/ppermute | solution.py:251
  8.0 7.3 %copy-start.3 = (f32[3,10,128]{2,1,0:T(8,128)S(1)}, f32[3,10,128]{2,1,0:T(8,128)}, u32[]{:S(2)}) copy-start(f32[3,10,128]{2,1,0:T(8,128)} %amp.1) | copy-start | bytes 46084
  16.2 13.4 %copy-start.2 = (s32[640]{0:T(1024)S(1)}, s32[640]{0:T(1024)}, u32[]{:S(2)}) copy-start(s32[640]{0:T(1024)} %vir_irrep.3) | copy-start | bytes 7684
  16.2 14.3 %copy-start.5 = (s32[2,2]{1,0:T(2,128)S(1)}, s32[2,2]{1,0:T(2,128)}, u32[]{:S(2)}) copy-start(s32[2,2]{1,0:T(2,128)} %pair_s.3) | copy-start | bytes 52
  16.2 14.5 %copy-start.1 = (s32[100]{0:T(128)S(1)}, s32[100]{0:T(128)}, u32[]{:S(2)}) copy-start(s32[100]{0:T(128)} %occ_s.3) | copy-start | bytes 1204
  16.2 49.9 %all-to-all-start = ((bf16[64,96,128]{2,1,0:T(8,128)(2,1)}), bf16[64,96,128]{2,1,0:T(8,128)(2,1)S(1)}, u32[]{:S(2)}, u32[]{:S(2)}) async-start(bf16[64,96,128]{2,1,0:T(8,128)(2,1)} %constant_dynamic-update-slice_fusion), calls=%async_computation | async-start | bytes 3145728 | tf_op jit(solution)/shard_map/all_to_all | solution.py:344
  66.2 3.6 %collective-permute-start.3 = (bf16[16,64,128]{2,1,0:T(8,128)(2,1)S(1)}, bf16[16,64,128]{2,1,0:T(8,128)(2,1)S(1)}, u32[]{:S(2)}, u32[]{:S(2)}) collective-permute-start(bf16[16,64,128]{2,1,0:T(8,128)(2,1)S(1)} %bitcast.37), channel_id=1, source_target_pairs={{0,4},{4,0},{8,12},{12,8},{16,20},{20,16},{24,28},{28,24},{32,36},... | collective-permute-start | bytes 786440 | tf_op jit(solution)/shard_map/ppermute | solution.py:389
  80.6 1.6 %collective-permute-start.4 = (bf16[32,32,128]{2,1,0:T(8,128)(2,1)S(1)}, bf16[32,32,128]{2,1,0:T(8,128)(2,1)S(1)}, u32[]{:S(2)}, u32[]{:S(2)}) collective-permute-start(bf16[32,32,128]{2,1,0:T(8,128)(2,1)S(1)} %get-tuple-element.23), channel_id=1, source_target_pairs={{0,4},{4,0},{8,12},{12,8},{16,20},{20,16},{24,28},{28,24},{32,36},... | collective-permute-start | bytes 786440 | tf_op jit(solution)/shard_map/ppermute | solution.py:409
  82.3 26.7 %copy-start.4 = (f32[2,10,160]{2,0,1:T(2,128)S(1)}, f32[2,10,160]{2,0,1:T(2,128)}, u32[]{:S(2)}) copy-start(f32[2,10,160]{2,0,1:T(2,128)} %param.10) | copy-start | bytes 38404
  83.0 16.8 %all-to-all-start.1 = ((bf16[32,32,128]{2,1,0:T(8,128)(2,1)}), bf16[32,32,128]{2,1,0:T(8,128)(2,1)S(1)}, u32[]{:S(2)}, u32[]{:S(2)}) async-start(bf16[32,32,128]{2,1,0:T(8,128)(2,1)} %add_convert_fusion), calls=%async_computation.1 | async-start | bytes 524288 | tf_op jit(solution)/shard_map/all_to_all | solution.py:411
  99.9 3.8 %collective-permute-start.5 = (f32[32,128]{1,0:T(8,128)S(1)}, f32[32,128]{1,0:T(8,128)S(1)}, u32[]{:S(2)}, u32[]{:S(2)}) collective-permute-start(f32[32,128]{1,0:T(8,128)S(1)} %convert_reduce_fusion), channel_id=1, source_target_pairs={{0,1},{1,0},{2,3},{3,2},{4,5},{5,4},{6,7},{7,6},{8,9},{9,8},{10,11... | collective-permute-start | bytes 49160 | tf_op jit(solution)/shard_map/ppermute | solution.py:257
  103.7 4.9 %collective-permute-start.6 = (f32[32,128]{1,0:T(8,128)S(1)}, f32[32,128]{1,0:T(8,128)S(1)}, u32[]{:S(2)}, u32[]{:S(2)}) collective-permute-start(f32[32,128]{1,0:T(8,128)S(1)} %add.67), channel_id=1, source_target_pairs={{0,3},{1,2},{2,1},{3,0},{4,7},{5,6},{6,5},{7,4},{8,11},{9,10},{10,... | collective-permute-start | bytes 49160 | tf_op jit(solution)/shard_map/ppermute | solution.py:257

commit v9 on v7

--- a/solution.py
+++ b/solution.py
@@ -271,17 +271,12 @@
     blk_count = vir_total // row_count
     q_own = q_local // blk_count
     occ_total = chol_ov.shape[1]
+    smem = pl.BlockSpec(memory_space=pltpu.SMEM)
+    vmem = pl.BlockSpec(memory_space=pltpu.VMEM)
     amp_send = pl.pallas_call(
         amp_kernel,
-        grid_spec=pltpu.PrefetchScalarGridSpec(
-            num_scalar_prefetch=2,
-            grid=(1,),
-            in_specs=[
-                pl.BlockSpec((row_count, 2, col_count), lambda i, *s: (0, 0, 0)),
-                pl.BlockSpec((vir_total,), lambda i, *s: (0,)),
-            ],
-            out_specs=pl.BlockSpec((3, row_count, MAIN), lambda i, *s: (0, 0, 0)),
-        ),
+        in_specs=[smem, smem, vmem, vmem],
+        out_specs=vmem,
         out_shape=jax.ShapeDtypeStruct((3, row_count, MAIN), F32),
         name="amp",
     )(occ_irrep, pair_list, amplitudes.transpose(1, 0, 2), vir_irrep)
@@ -292,24 +287,24 @@
     rows = 5
     packed = pl.pallas_call(
         pack_kernel,
-        grid_spec=pltpu.PrefetchScalarGridSpec(
-            num_scalar_prefetch=3,
-            grid=(row_count // rows,),
-            in_specs=[
-                pl.BlockSpec((rows, q_local, vir_total), lambda i, *s: (i, 0, 0)),
-                pl.BlockSpec((rows, occ_total, q_local), lambda i, *s: (i, 0, 0)),
-                pl.BlockSpec((occ_total, vir_total), lambda i, *s: (0, 0)),
-                pl.BlockSpec((vir_total,), lambda i, *s: (0,)),
-                pl.BlockSpec(chol_irrep.shape, lambda i, *s: (0,)),
-            ],
-            out_specs=pl.BlockSpec((blk_count, 8 * row_count, MAIN), lambda i, *s: (0, 0, 0)),
-            scratch_shapes=[
-                pltpu.VMEM((vir_total, 2 * MAIN), BF),
-                pltpu.VMEM((q_local, MAIN), I32),
-                pltpu.VMEM((occ_total, MAIN), BF),
-                pltpu.VMEM((blk_count * 8 * row_count, MAIN), F32),
-            ],
-        ),
+        grid=(row_count // rows,),
+        in_specs=[
+            smem,
+            smem,
+            smem,
+            pl.BlockSpec((rows, q_local, vir_total), lambda i: (i, 0, 0)),
+            pl.BlockSpec((rows, occ_total, q_local), lambda i: (i, 0, 0)),
+            pl.BlockSpec((occ_total, vir_total), lambda i: (0, 0)),
+            pl.BlockSpec((vir_total,), lambda i: (0,)),
+            pl.BlockSpec(chol_irrep.shape, lambda i: (0,)),
+        ],
+        out_specs=pl.BlockSpec((blk_count, 8 * row_count, MAIN), lambda i: (0, 0, 0)),
+        scratch_shapes=[
+            pltpu.VMEM((vir_total, 2 * MAIN), BF),
+            pltpu.VMEM((q_local, MAIN), I32),
+            pltpu.VMEM((occ_total, MAIN), BF),
+            pltpu.VMEM((blk_count * 8 * row_count, MAIN), F32),
+        ],
         out_shape=jax.ShapeDtypeStruct((blk_count, 8 * row_count + amp_rows // 2, MAIN), BF),
         cost_estimate=pl.CostEstimate(
             flops=2 * q_local * row_count * vir_total * 256,
@@ -368,8 +363,6 @@
     own_irrep = lax.dynamic_index_in_dim(
         q_irrep.reshape(q_own, blk_count), blk_pos, axis=1, keepdims=False
     )
-    smem = pl.BlockSpec(memory_space=pltpu.SMEM)
-    vmem = pl.BlockSpec(memory_space=pltpu.VMEM)
     tables = (
         irrep_mixed[:, None],
         irrep_mixed[None, :],

time: 112 us -> 110 us (0.982)
  Pallas kernels: 20.9 us -> 19.3 us
    pallas_call x2, Pallas kernels: 10.1 us -> 8.51 us  [the longest x1 6.45 us: per_device(): pl.pallas_call(pack_kernel, grid=(row_count // rows,), in_specs=[smem, sm...]
  transfers between devices with their start and end apart: 10 -> 10, of which waited for: 6 -> 6; matrix products, arithmetic and copies ran while one was open for 7% -> 7% of each run, Pallas kernels for 7% -> 6%
where the time goes in v9:
time: 110 us; the launch traced here: 108 us
  waiting for transfers between devices  48.2 us (44%)
  starting transfers between devices  29.8 us (27%)
  Pallas kernels  19.3 us (18%)
  local copies, waits for them, and re-layouts  7.89 us (7%)
  other arithmetic  2.14 us (2%)
    all_to_all x1, waiting for transfers between devices, per_device(): lax.all_to_all(packed, 'blk', split_axis=0, concat_axis=0, tiled=False)  34.1 us
    all_to_all x1, starting transfers between devices, per_device(): lax.all_to_all(packed, 'blk', split_axis=0, concat_axis=0, tiled=False)  12.3 us
    pallas_call x1, Pallas kernels, per_device(): pl.pallas_call(pair_kernel, in_specs=[smem, smem, smem] + [vmem] * 7, out...  10.8 us
    ppermute x6, starting transfers between devices, over_rep(): lax.ppermute(value, 'rep', [(i, (i + k) % 4) for i in range(4)])  8.66 us
    all_to_all x1, waiting for transfers between devices, per_device(): lax.all_to_all(part, 'blk', split_axis=0, concat_axis=0, axis_index_group...  7.74 us
    pallas_call x1, Pallas kernels, per_device(): pl.pallas_call(pack_kernel, grid=(row_count // rows,), in_specs=[smem, sm...  6.45 us
    all_to_all x1, starting transfers between devices, per_device(): lax.all_to_all(part, 'blk', split_axis=0, concat_axis=0, axis_index_group...  5.93 us
    ppermute x6, waiting for transfers between devices, over_rep(): lax.ppermute(value, 'rep', [(i, (i + k) % 4) for i in range(4)])  4.87 us
  transfers between devices with their start and end apart: 10, of which 6 were waited for; matrix products, arithmetic and copies ran while one was open for 7% of the time, Pallas kernels for 6%

profile of v9, /device:TPU:6, one launch (start us, length us, event | category | flops | bytes accessed | tf_op | source)
XLA Modules:
  0.0 108.4 jit_solution(6982886339500076079)
XLA Ops:
  0.6 2.1 %amp.1 = f32[3,10,128]{2,1,0:T(8,128)} custom-call(s32[100]{0:T(128)} %occ_s.3, s32[2,2]{1,0:T(2,128)} %pair_s.3, f32[10,2,160]{2,1,0:T(2,128)} %bitcast.44, s32[640]{0:T(1024)} %vir_irrep.3), custom_call_target="tpu_custom_call" | custom-call | tf_op jit(solution)/shard_map/amp/pallas_call | solution.py:276
  2.7 3.0 %collective-permute-start.2 = (f32[3,10,128]{2,1,0:T(8,128)}, f32[3,10,128]{2,1,0:T(8,128)S(1)}, u32[]{:S(2)}, u32[]{:S(2)}) collective-permute-start(f32[3,10,128]{2,1,0:T(8,128)} %amp.1), channel_id=1, source_target_pairs={{0,3},{1,0},{2,1},{3,2},{4,7},{5,4},{6,5},{7,6},{8,11},{9,8},{10,9... | collective-permute-start | bytes 46088 | tf_op jit(solution)/shard_map/ppermute | solution.py:251
  5.7 0.6 collective-permute-start.1
  6.4 1.0 collective-permute-start
  7.3 6.4 %pack.1 = bf16[64,96,128]{2,1,0:T(8,128)(2,1)} custom-call(s32[640]{0:T(1024)} %vir_irrep.3, s32[100]{0:T(128)} %occ_s.3, s32[2,2]{1,0:T(2,128)} %pair_s.3, bf16[10,384,640]{2,1,0:T(8,128)(2,1)} %bitcast.39, bf16[10,100,384]{2,1,0:T(8,128)(2,1)} %bitcast.41, bf16[100,640]{1,0:T(8,128)(2,1)} %singles.1, s32[640]{0:T(1024)} %vir_irrep.3, s32[1536]{0:T(1024)} %chol_irrep.1), custom_call_target="tpu_custom_call" | custom-call | flops 1258291200 | bytes 4915200 | tf_op jit(solution)/shard_map/pack/pallas_call | solution.py:288
  13.9 0.8 constant_dynamic-update-slice_fusion
  14.7 12.3 %all-to-all-start = ((bf16[64,96,128]{2,1,0:T(8,128)(2,1)}), bf16[64,96,128]{2,1,0:T(8,128)(2,1)S(1)}, u32[]{:S(2)}, u32[]{:S(2)}) async-start(bf16[64,96,128]{2,1,0:T(8,128)(2,1)} %constant_dynamic-update-slice_fusion), calls=%async_computation | async-start | bytes 3145728 | tf_op jit(solution)/shard_map/all_to_all | solution.py:333
  27.0 0.8 dynamic_slice.25
  27.8 0.1 reshape.110
  27.9 0.2 dynamic-slice_reduce_fusion.q_irrep
  28.1 0.1 convert_reduce_fusion.1
  28.2 0.1 select_reduce_fusion
  28.3 0.1 reduce_sum.31
  28.5 0.1 broadcast_in_dim_reshape.15.col_pos
  28.6 0.1 broadcast_in_dim_reshape.14
  28.6 0.1 reshape.111
  28.9 0.1 broadcast_in_dim_reshape.13.col_irrep
  28.9 0.1 broadcast_in_dim_reshape.12
  29.0 0.2 fusion.11
  29.2 0.6 gather_fusion.1
  29.9 0.6 gather_fusion
  30.5 34.1 %all-to-all-done = bf16[64,96,128]{2,1,0:T(8,128)(2,1)S(1)} async-done(((bf16[64,96,128]{2,1,0:T(8,128)(2,1)}), bf16[64,96,128]{2,1,0:T(8,128)(2,1)S(1)}, u32[]{:S(2)}, u32[]{:S(2)}) %all-to-all-start) | async-done | bytes 1572896 | tf_op jit(solution)/shard_map/all_to_all | solution.py:333
  64.7 2.5 %collective-permute-start.3 = (bf16[16,64,128]{2,1,0:T(8,128)(2,1)S(1)}, bf16[16,64,128]{2,1,0:T(8,128)(2,1)S(1)}, u32[]{:S(2)}, u32[]{:S(2)}) collective-permute-start(bf16[16,64,128]{2,1,0:T(8,128)(2,1)S(1)} %bitcast.37), channel_id=1, source_target_pairs={{0,4},{4,0},{8,12},{12,8},{16,20},{20,16},{24,28},{28,24},{32,36},... | collective-permute-start | bytes 786440 | tf_op jit(solution)/shard_map/ppermute | solution.py:376
  67.2 0.1 slice.49
  67.2 0.3 copy.56
  67.6 0.2 copy.48.row_irrep
  67.8 0.2 copy.49.row_pos
  68.0 0.4 collective-permute-done.3.amp_other
  68.3 10.8 %ladder.1 = (f32[32,32,128]{2,1,0:T(8,128)S(1)}, bf16[32,32,128]{2,1,0:T(8,128)(2,1)S(1)}) custom-call(s32[6]{0:T(128)S(1)} %dynamic-slice_reduce_fusion.q_irrep, s32[2]{0:T(128)S(1)} %xor.28.pair_sym, s32[1]{0:T(128)} %bitcast.9.core, bf16[80,64,128]{2,1,0:T(8,128)(2,1)S(1)} %bitcast.36, bf16[16,64,128]{2,1,0:T(8,128)(2,1)S(1)} %bitcast.38, ...), custom_call_target="tpu_custom_call" | custom-call | tf_op jit(solution)/shard_map/ladder/pallas_call | solution.py:377
  79.1 0.5 collective-permute-start.4
  79.6 1.2 %collective-permute-done.4 = bf16[32,32,128]{2,1,0:T(8,128)(2,1)S(1)} collective-permute-done((bf16[32,32,128]{2,1,0:T(8,128)(2,1)S(1)}, bf16[32,32,128]{2,1,0:T(8,128)(2,1)S(1)}, u32[]{:S(2)}, u32[]{:S(2)}) %collective-permute-start.4) | collective-permute-done | bytes 262176 | tf_op jit(solution)/shard_map/ppermute | solution.py:396
  80.7 0.8 add_convert_fusion
  81.5 5.9 %all-to-all-start.1 = ((bf16[32,32,128]{2,1,0:T(8,128)(2,1)}), bf16[32,32,128]{2,1,0:T(8,128)(2,1)S(1)}, u32[]{:S(2)}, u32[]{:S(2)}) async-start(bf16[32,32,128]{2,1,0:T(8,128)(2,1)} %add_convert_fusion), calls=%async_computation.1 | async-start | bytes 524288 | tf_op jit(solution)/shard_map/all_to_all | solution.py:398
  87.4 0.8 dynamic_slice.27
  88.2 0.8 dynamic_slice.28
  89.0 0.1 dynamic_slice.22
  89.0 0.1 dynamic_slice.23
  89.1 0.6 gather_fusion.3
  89.7 0.6 gather_fusion.2
  90.4 0.1 broadcast_subtract_fusion
  90.5 7.7 %all-to-all-done.1 = bf16[32,32,128]{2,1,0:T(8,128)(2,1)S(1)} async-done(((bf16[32,32,128]{2,1,0:T(8,128)(2,1)}), bf16[32,32,128]{2,1,0:T(8,128)(2,1)S(1)}, u32[]{:S(2)}, u32[]{:S(2)}) %all-to-all-start.1) | async-done | bytes 262176 | tf_op jit(solution)/shard_map/all_to_all | solution.py:398
  98.3 2.4 %collective-permute-start.7 = (f32[32,128]{1,0:T(8,128)S(1)}, f32[32,128]{1,0:T(8,128)S(1)}, u32[]{:S(2)}, u32[]{:S(2)}) collective-permute-start(f32[32,128]{1,0:T(8,128)S(1)} %convert_reduce_fusion), channel_id=1, source_target_pairs={{0,3},{1,0},{2,1},{3,2},{4,7},{5,4},{6,5},{7,6},{8,11},{9,8},{10,9... | collective-permute-start | bytes 49160 | tf_op jit(solution)/shard_map/ppermute | solution.py:251
  100.7 1.7 %collective-permute-start.6 = (f32[32,128]{1,0:T(8,128)S(1)}, f32[32,128]{1,0:T(8,128)S(1)}, u32[]{:S(2)}, u32[]{:S(2)}) collective-permute-start(f32[32,128]{1,0:T(8,128)S(1)} %convert_reduce_fusion), channel_id=1, source_target_pairs={{0,2},{1,3},{2,0},{3,1},{4,6},{5,7},{6,4},{7,5},{8,10},{9,11},{10,... | collective-permute-start | bytes 49160 | tf_op jit(solution)/shard_map/ppermute | solution.py:251
  102.4 0.1 dynamic_slice.24
  102.5 3.5 %collective-permute-done.6 = f32[32,128]{1,0:T(8,128)S(1)} collective-permute-done((f32[32,128]{1,0:T(8,128)S(1)}, f32[32,128]{1,0:T(8,128)S(1)}, u32[]{:S(2)}, u32[]{:S(2)}) %collective-permute-start.6) | collective-permute-done | bytes 16416 | tf_op jit(solution)/shard_map/ppermute | solution.py:251
  105.9 1.4 %collective-permute-done.5 = f32[32,128]{1,0:T(8,128)S(1)} collective-permute-done((f32[32,128]{1,0:T(8,128)S(1)}, f32[32,128]{1,0:T(8,128)S(1)}, u32[]{:S(2)}, u32[]{:S(2)}) %collective-permute-start.5) | collective-permute-done | bytes 16416 | tf_op jit(solution)/shard_map/ppermute | solution.py:251
  107.4 0.2 fusion.1
  107.7 0.7 fusion.9
  (39 shorter events, 0.6 us)
Async XLA Ops:
  0.6 88.5 %copy-start = (f32[100]{0:T(128)S(1)}, f32[100]{0:T(128)}, u32[]{:S(2)}) copy-start(f32[100]{0:T(128)} %param.14) | copy-start | bytes 1204
  2.7 11.1 %collective-permute-start.2 = (f32[3,10,128]{2,1,0:T(8,128)}, f32[3,10,128]{2,1,0:T(8,128)S(1)}, u32[]{:S(2)}, u32[]{:S(2)}) collective-permute-start(f32[3,10,128]{2,1,0:T(8,128)} %amp.1), channel_id=1, source_target_pairs={{0,3},{1,0},{2,1},{3,2},{4,7},{5,4},{6,5},{7,6},{8,11},{9,8},{10,9... | collective-permute-start | bytes 46088 | tf_op jit(solution)/shard_map/ppermute | solution.py:251
  5.7 8.1 %collective-permute-start.1 = (f32[3,10,128]{2,1,0:T(8,128)}, f32[3,10,128]{2,1,0:T(8,128)S(1)}, u32[]{:S(2)}, u32[]{:S(2)}) collective-permute-start(f32[3,10,128]{2,1,0:T(8,128)} %amp.1), channel_id=1, source_target_pairs={{0,2},{1,3},{2,0},{3,1},{4,6},{5,7},{6,4},{7,5},{8,10},{9,11},{10,... | collective-permute-start | bytes 46088 | tf_op jit(solution)/shard_map/ppermute | solution.py:251
  6.4 7.4 %collective-permute-start = (f32[3,10,128]{2,1,0:T(8,128)}, f32[3,10,128]{2,1,0:T(8,128)S(1)}, u32[]{:S(2)}, u32[]{:S(2)}) collective-permute-start(f32[3,10,128]{2,1,0:T(8,128)} %amp.1), channel_id=1, source_target_pairs={{0,1},{1,2},{2,3},{3,0},{4,5},{5,6},{6,7},{7,4},{8,9},{9,10},{10,1... | collective-permute-start | bytes 46088 | tf_op jit(solution)/shard_map/ppermute | solution.py:251
  7.3 6.5 %copy-start.3 = (f32[3,10,128]{2,1,0:T(8,128)S(1)}, f32[3,10,128]{2,1,0:T(8,128)}, u32[]{:S(2)}) copy-start(f32[3,10,128]{2,1,0:T(8,128)} %amp.1) | copy-start | bytes 46084
  14.7 13.4 %copy-start.2 = (s32[640]{0:T(1024)S(1)}, s32[640]{0:T(1024)}, u32[]{:S(2)}) copy-start(s32[640]{0:T(1024)} %vir_irrep.3) | copy-start | bytes 7684
  14.7 14.3 %copy-start.5 = (s32[2,2]{1,0:T(2,128)S(1)}, s32[2,2]{1,0:T(2,128)}, u32[]{:S(2)}) copy-start(s32[2,2]{1,0:T(2,128)} %pair_s.3) | copy-start | bytes 52
  14.7 14.5 %copy-start.1 = (s32[100]{0:T(128)S(1)}, s32[100]{0:T(128)}, u32[]{:S(2)}) copy-start(s32[100]{0:T(128)} %occ_s.3) | copy-start | bytes 1204
  14.7 49.9 %all-to-all-start = ((bf16[64,96,128]{2,1,0:T(8,128)(2,1)}), bf16[64,96,128]{2,1,0:T(8,128)(2,1)S(1)}, u32[]{:S(2)}, u32[]{:S(2)}) async-start(bf16[64,96,128]{2,1,0:T(8,128)(2,1)} %constant_dynamic-update-slice_fusion), calls=%async_computation | async-start | bytes 3145728 | tf_op jit(solution)/shard_map/all_to_all | solution.py:333
  64.7 3.6 %collective-permute-start.3 = (bf16[16,64,128]{2,1,0:T(8,128)(2,1)S(1)}, bf16[16,64,128]{2,1,0:T(8,128)(2,1)S(1)}, u32[]{:S(2)}, u32[]{:S(2)}) collective-permute-start(bf16[16,64,128]{2,1,0:T(8,128)(2,1)S(1)} %bitcast.37), channel_id=1, source_target_pairs={{0,4},{4,0},{8,12},{12,8},{16,20},{20,16},{24,28},{28,24},{32,36},... | collective-permute-start | bytes 786440 | tf_op jit(solution)/shard_map/ppermute | solution.py:376
  79.1 1.6 %collective-permute-start.4 = (bf16[32,32,128]{2,1,0:T(8,128)(2,1)S(1)}, bf16[32,32,128]{2,1,0:T(8,128)(2,1)S(1)}, u32[]{:S(2)}, u32[]{:S(2)}) collective-permute-start(bf16[32,32,128]{2,1,0:T(8,128)(2,1)S(1)} %get-tuple-element.23), channel_id=1, source_target_pairs={{0,4},{4,0},{8,12},{12,8},{16,20},{20,16},{24,28},{28,24},{32,36},... | collective-permute-start | bytes 786440 | tf_op jit(solution)/shard_map/ppermute | solution.py:396
  80.7 26.9 %copy-start.4 = (f32[2,10,160]{2,0,1:T(2,128)S(1)}, f32[2,10,160]{2,0,1:T(2,128)}, u32[]{:S(2)}) copy-start(f32[2,10,160]{2,0,1:T(2,128)} %param.10) | copy-start | bytes 38404
  81.5 16.8 %all-to-all-start.1 = ((bf16[32,32,128]{2,1,0:T(8,128)(2,1)}), bf16[32,32,128]{2,1,0:T(8,128)(2,1)S(1)}, u32[]{:S(2)}, u32[]{:S(2)}) async-start(bf16[32,32,128]{2,1,0:T(8,128)(2,1)} %add_convert_fusion), calls=%async_computation.1 | async-start | bytes 524288 | tf_op jit(solution)/shard_map/all_to_all | solution.py:398
  98.3 4.1 %collective-permute-start.7 = (f32[32,128]{1,0:T(8,128)S(1)}, f32[32,128]{1,0:T(8,128)S(1)}, u32[]{:S(2)}, u32[]{:S(2)}) collective-permute-start(f32[32,128]{1,0:T(8,128)S(1)} %convert_reduce_fusion), channel_id=1, source_target_pairs={{0,3},{1,0},{2,1},{3,2},{4,7},{5,4},{6,5},{7,6},{8,11},{9,8},{10,9... | collective-permute-start | bytes 49160 | tf_op jit(solution)/shard_map/ppermute | solution.py:251
  100.7 5.2 %collective-permute-start.6 = (f32[32,128]{1,0:T(8,128)S(1)}, f32[32,128]{1,0:T(8,128)S(1)}, u32[]{:S(2)}, u32[]{:S(2)}) collective-permute-start(f32[32,128]{1,0:T(8,128)S(1)} %convert_reduce_fusion), channel_id=1, source_target_pairs={{0,2},{1,3},{2,0},{3,1},{4,6},{5,7},{6,4},{7,5},{8,10},{9,11},{10,... | collective-permute-start | bytes 49160 | tf_op jit(solution)/shard_map/ppermute | solution.py:251
  102.4 4.9 %collective-permute-start.5 = (f32[32,128]{1,0:T(8,128)S(1)}, f32[32,128]{1,0:T(8,128)S(1)}, u32[]{:S(2)}, u32[]{:S(2)}) collective-permute-start(f32[32,128]{1,0:T(8,128)S(1)} %convert_reduce_fusion), channel_id=1, source_target_pairs={{0,1},{1,2},{2,3},{3,0},{4,5},{5,6},{6,7},{7,4},{8,9},{9,10},{10,1... | collective-permute-start | bytes 49160 | tf_op jit(solution)/shard_map/ppermute | solution.py:251

commit v10 on v9

--- a/solution.py
+++ b/solution.py
@@ -143,9 +143,7 @@
 
 
 def pair_kernel(
-    q_irrep,
-    pair_sym,
-    core,
+    scalars,
     got,
     amp_mine,
     amp_other,
@@ -157,11 +155,14 @@
     give,
     ball,
     hall,
-    amps,
+    amp_main,
+    amp_rest,
     unfold,
     stage,
     halves,
 ):
+    q_count = 2 * GROUPS
+    core = scalars[q_count + 2]
     vir_total = row_irrep.shape[0]
     own = got.shape[1]
     row_count = vir_total // own
@@ -177,21 +178,19 @@
     half_rows = amp_mine.shape[0]
 
     def amp_row(t):
-        return halves[jnp.bitwise_xor(core[0], t // half_rows), t % half_rows]
+        return halves[jnp.bitwise_xor(core, t // half_rows), t % half_rows]
 
     for r in range(row_count):
         here = slice(r * own, (r + 1) * own)
         rest_amp = amp_row(2 * row_count + r).astype(F32)
         for p in range(2):
-            main_amp = amp_row(p * row_count + r)
+            cols = slice(p * MAIN, (p + 1) * MAIN)
+            amp_main[here, cols] = amp_row(p * row_count + r)
             for g in range(GROUPS):
                 shift = (g * STRIDE - p * 64) % MAIN
                 moved = pltpu.roll(rest_amp, shift, 1) if shift else rest_amp
                 inside = (lane >= g * STRIDE) & (lane < g * STRIDE + REST)
-                amps[g, here, p * 256 : p * 256 + MAIN] = main_amp
-                amps[g, here, p * 256 + MAIN : (p + 1) * 256] = jnp.where(
-                    inside, moved, 0.0
-                ).astype(BF)
+                amp_rest[g, here, cols] = jnp.where(inside, moved, 0.0).astype(BF)
         for q in range(2 * GROUPS):
             ball[here, q * 256 : q * 256 + MAIN] = got[r * per_row + q]
             ball[here, q * 256 + MAIN : (q + 1) * 256] = got[
@@ -204,17 +203,17 @@
         shifted = pltpu.roll(ball[:, at : at + MAIN].astype(F32), 1, 1)
         for g in range(GROUPS):
             q = u * GROUPS + g
-            want = jnp.bitwise_xor(row_irrep[...], q_irrep[q])
+            want = jnp.bitwise_xor(row_irrep[...], scalars[q])
             wide = dot(ball[:, q * 256 : (q + 1) * 256], unfold[g])
             wide = jnp.where(want == col_irrep[...], wide, 0.0).astype(BF)
-            halfway = dot(wide, amps[g])
+            half_main = dot(wide, amp_main[...])
+            half_rest = dot(wide, amp_rest[g])
             for p in range(2):
-                hall[p, :, q * 256 : q * 256 + MAIN] = halfway[
-                    :, p * 256 : p * 256 + MAIN
-                ].astype(BF)
+                cols = slice(p * MAIN, (p + 1) * MAIN)
+                hall[p, :, q * 256 : q * 256 + MAIN] = half_main[:, cols].astype(BF)
                 dressed = jnp.where(lane == g * STRIDE + REST + 2 * p + 1, shifted, 0.0)
                 hall[p, :, q * 256 + MAIN : (q + 1) * 256] = (
-                    halfway[:, p * 256 + MAIN : (p + 1) * 256] + dressed
+                    half_rest[:, cols] + dressed
                 ).astype(BF)
 
     out_rows = keep.shape[1]
@@ -222,7 +221,7 @@
     tail = None
     for p in range(2):
         value = lax.dot_general(hall[p], ball[...], NT, preferred_element_type=F32)
-        want = jnp.bitwise_xor(row_irrep[...], pair_sym[p])
+        want = jnp.bitwise_xor(row_irrep[...], scalars[q_count + p])
         value = jnp.where(want == col_irrep[...], value, 0.0).astype(BF)
         place = row_pos[...]
         place = jnp.where(place < MAIN, place, place + p * 64)
@@ -240,7 +239,7 @@
     for t in range(3 * row_count, out_rows):
         stage[pl.ds(t, own, stride=out_rows), :] = jnp.zeros((own, MAIN), F32)
     sums = stage[...].reshape(own // 2, 2, out_rows, MAIN)
-    even = core[0] == 0
+    even = core == 0
     keep[...] = jnp.where(even, sums[:, 0], sums[:, 1])
     give[...] = jnp.where(even, sums[:, 1], sums[:, 0]).astype(BF)
 
@@ -370,13 +369,12 @@
         pos_mixed[None, :],
     )
 
-    amp_mine, own_irrep, pair_sym, tables = lax.optimization_barrier(
-        (amp_mine, own_irrep, pair_sym, tables)
-    )
+    scalars = jnp.concatenate([own_irrep, pair_sym, (blk_pos & 1)[None]])
+    amp_mine, scalars, tables = lax.optimization_barrier((amp_mine, scalars, tables))
     amp_other = lax.ppermute(amp_mine, "blk", siblings)
     keep, give = pl.pallas_call(
         pair_kernel,
-        in_specs=[smem, smem, smem] + [vmem] * 7,
+        in_specs=[smem] + [vmem] * 7,
         out_specs=(vmem, vmem),
         out_shape=(
             jax.ShapeDtypeStruct((blk_count // 2, 32, MAIN), F32),
@@ -385,14 +383,15 @@
         scratch_shapes=[
             pltpu.VMEM((vir_total, 4 * GROUPS * MAIN), BF),
             pltpu.VMEM((2, vir_total, 4 * GROUPS * MAIN), BF),
-            pltpu.VMEM((GROUPS, vir_total, 4 * MAIN), BF),
+            pltpu.VMEM((vir_total, 2 * MAIN), BF),
+            pltpu.VMEM((GROUPS, vir_total, 2 * MAIN), BF),
             pltpu.VMEM((GROUPS, 2 * MAIN, vir_total), BF),
             pltpu.VMEM((blk_count * 32, MAIN), F32),
             pltpu.VMEM((2, amp_half, blk_count, MAIN), BF),
         ],
         compiler_params=pltpu.CompilerParams(vmem_limit_bytes=LIMIT),
         name="ladder",
-    )(own_irrep, pair_sym, (blk_pos & 1)[None], got, amp_mine, amp_other, *tables)
+    )(scalars, got, amp_mine, amp_other, *tables)
     part = (keep + lax.ppermute(give, "blk", siblings).astype(F32)).astype(BF)
     sides = [list(range(k, blk_count, 2)) for k in range(2)]
     part = lax.all_to_all(

time: 110 us -> 110 us (level)
  no operation moved by 1% of the time
where the time goes in v10:
time: 110 us; the launch traced here: 108 us
  waiting for transfers between devices  48.1 us (44%)
  starting transfers between devices  29.8 us (27%)
  Pallas kernels  19.2 us (17%)
  local copies, waits for them, and re-layouts  7.88 us (7%)
  other arithmetic  2.22 us (2%)
    all_to_all x1, waiting for transfers between devices, per_device(): lax.all_to_all(packed, 'blk', split_axis=0, concat_axis=0, tiled=False)  34 us
    all_to_all x1, starting transfers between devices, per_device(): lax.all_to_all(packed, 'blk', split_axis=0, concat_axis=0, tiled=False)  12.3 us
    pallas_call x1, Pallas kernels, per_device(): pl.pallas_call(pair_kernel, in_specs=[smem] + [vmem] * 7, out_specs=(vmem...  10.7 us
    ppermute x6, starting transfers between devices, over_rep(): lax.ppermute(value, 'rep', [(i, (i + k) % 4) for i in range(4)])  8.66 us
    all_to_all x1, waiting for transfers between devices, per_device(): lax.all_to_all(part, 'blk', split_axis=0, concat_axis=0, axis_index_group...  7.73 us
    pallas_call x1, Pallas kernels, per_device(): pl.pallas_call(pack_kernel, grid=(row_count // rows,), in_specs=[smem, sm...  6.45 us
    all_to_all x1, starting transfers between devices, per_device(): lax.all_to_all(part, 'blk', split_axis=0, concat_axis=0, axis_index_group...  5.93 us
    ppermute x6, waiting for transfers between devices, over_rep(): lax.ppermute(value, 'rep', [(i, (i + k) % 4) for i in range(4)])  4.87 us
  transfers between devices with their start and end apart: 10, of which 6 were waited for; matrix products, arithmetic and copies ran while one was open for 7% of the time, Pallas kernels for 6%

profile of v10, /device:TPU:6, one launch (start us, length us, event | category | flops | bytes accessed | tf_op | source)
XLA Modules:
  0.0 108.3 jit_solution(13200233343678737679)
XLA Ops:
  0.6 2.1 %amp.1 = f32[3,10,128]{2,1,0:T(8,128)} custom-call(s32[100]{0:T(128)} %occ_s.3, s32[2,2]{1,0:T(2,128)} %pair_s.3, f32[10,2,160]{2,1,0:T(2,128)} %bitcast.44, s32[640]{0:T(1024)} %vir_irrep.3), custom_call_target="tpu_custom_call" | custom-call | tf_op jit(solution)/shard_map/amp/pallas_call | solution.py:275
  2.7 3.0 %collective-permute-start.2 = (f32[3,10,128]{2,1,0:T(8,128)}, f32[3,10,128]{2,1,0:T(8,128)S(1)}, u32[]{:S(2)}, u32[]{:S(2)}) collective-permute-start(f32[3,10,128]{2,1,0:T(8,128)} %amp.1), channel_id=1, source_target_pairs={{0,3},{1,0},{2,1},{3,2},{4,7},{5,4},{6,5},{7,6},{8,11},{9,8},{10,9... | collective-permute-start | bytes 46088 | tf_op jit(solution)/shard_map/ppermute | solution.py:250
  5.7 0.6 collective-permute-start.1
  6.4 1.0 collective-permute-start
  7.3 6.4 %pack.1 = bf16[64,96,128]{2,1,0:T(8,128)(2,1)} custom-call(s32[640]{0:T(1024)} %vir_irrep.3, s32[100]{0:T(128)} %occ_s.3, s32[2,2]{1,0:T(2,128)} %pair_s.3, bf16[10,384,640]{2,1,0:T(8,128)(2,1)} %bitcast.39, bf16[10,100,384]{2,1,0:T(8,128)(2,1)} %bitcast.41, bf16[100,640]{1,0:T(8,128)(2,1)} %singles.1, s32[640]{0:T(1024)} %vir_irrep.3, s32[1536]{0:T(1024)} %chol_irrep.1), custom_call_target="tpu_custom_call" | custom-call | flops 1258291200 | bytes 4915200 | tf_op jit(solution)/shard_map/pack/pallas_call | solution.py:287
  13.9 0.8 constant_dynamic-update-slice_fusion
  14.7 12.3 %all-to-all-start = ((bf16[64,96,128]{2,1,0:T(8,128)(2,1)}), bf16[64,96,128]{2,1,0:T(8,128)(2,1)S(1)}, u32[]{:S(2)}, u32[]{:S(2)}) async-start(bf16[64,96,128]{2,1,0:T(8,128)(2,1)} %constant_dynamic-update-slice_fusion), calls=%async_computation | async-start | bytes 3145728 | tf_op jit(solution)/shard_map/all_to_all | solution.py:332
  27.0 0.8 dynamic_slice.25
  27.8 0.1 reshape.110
  27.9 0.2 dynamic-slice_reduce_fusion
  28.1 0.1 convert_reduce_fusion.1
  28.2 0.1 select_reduce_fusion
  28.3 0.1 reduce_sum.31
  28.5 0.1 broadcast_in_dim_reshape.15.col_pos
  28.6 0.1 broadcast_in_dim_reshape.14
  28.6 0.1 reshape.111
  28.9 0.1 broadcast_in_dim_reshape.13.col_irrep
  28.9 0.1 broadcast_in_dim_reshape.12
  29.0 0.2 fusion.11
  29.2 0.6 gather_fusion.1
  29.9 0.6 gather_fusion
  30.5 0.1 pad_add_fusion.scalars
  30.6 34.0 %all-to-all-done = bf16[64,96,128]{2,1,0:T(8,128)(2,1)S(1)} async-done(((bf16[64,96,128]{2,1,0:T(8,128)(2,1)}), bf16[64,96,128]{2,1,0:T(8,128)(2,1)S(1)}, u32[]{:S(2)}, u32[]{:S(2)}) %all-to-all-start) | async-done | bytes 1572896 | tf_op jit(solution)/shard_map/all_to_all | solution.py:332
  64.7 2.5 %collective-permute-start.3 = (bf16[16,64,128]{2,1,0:T(8,128)(2,1)S(1)}, bf16[16,64,128]{2,1,0:T(8,128)(2,1)S(1)}, u32[]{:S(2)}, u32[]{:S(2)}) collective-permute-start(bf16[16,64,128]{2,1,0:T(8,128)(2,1)S(1)} %bitcast.37), channel_id=1, source_target_pairs={{0,4},{4,0},{8,12},{12,8},{16,20},{20,16},{24,28},{28,24},{32,36},... | collective-permute-start | bytes 786440 | tf_op jit(solution)/shard_map/ppermute | solution.py:374
  67.2 0.1 slice.49
  67.2 0.3 copy.56
  67.6 0.2 copy.48.row_irrep
  67.8 0.2 copy.49.row_pos
  68.0 0.4 collective-permute-done.3.amp_other
  68.3 10.7 %ladder.1 = (f32[32,32,128]{2,1,0:T(8,128)S(1)}, bf16[32,32,128]{2,1,0:T(8,128)(2,1)S(1)}) custom-call(s32[9]{0:T(128)S(1)} %pad_add_fusion.scalars, bf16[80,64,128]{2,1,0:T(8,128)(2,1)S(1)} %bitcast.36, bf16[16,64,128]{2,1,0:T(8,128)(2,1)S(1)} %bitcast.38, bf16[16,64,128]{2,1,0:T(8,128)(2,1)S(1)} %collective-permute-done.3.amp_other, ...), custom_call_target="tpu_custom_call" | custom-call | tf_op jit(solution)/shard_map/ladder/pallas_call | solution.py:375
  79.0 0.5 collective-permute-start.4
  79.5 1.2 %collective-permute-done.4 = bf16[32,32,128]{2,1,0:T(8,128)(2,1)S(1)} collective-permute-done((bf16[32,32,128]{2,1,0:T(8,128)(2,1)S(1)}, bf16[32,32,128]{2,1,0:T(8,128)(2,1)S(1)}, u32[]{:S(2)}, u32[]{:S(2)}) %collective-permute-start.4) | collective-permute-done | bytes 262176 | tf_op jit(solution)/shard_map/ppermute | solution.py:395
  80.6 0.8 add_convert_fusion
  81.4 5.9 %all-to-all-start.1 = ((bf16[32,32,128]{2,1,0:T(8,128)(2,1)}), bf16[32,32,128]{2,1,0:T(8,128)(2,1)S(1)}, u32[]{:S(2)}, u32[]{:S(2)}) async-start(bf16[32,32,128]{2,1,0:T(8,128)(2,1)} %add_convert_fusion), calls=%async_computation.1 | async-start | bytes 524288 | tf_op jit(solution)/shard_map/all_to_all | solution.py:397
  87.4 0.8 dynamic_slice.27
  88.1 0.8 dynamic_slice.28
  88.9 0.1 dynamic_slice.22
  89.0 0.1 dynamic_slice.23
  89.0 0.6 gather_fusion.3
  89.7 0.6 gather_fusion.2
  90.5 7.7 %all-to-all-done.1 = bf16[32,32,128]{2,1,0:T(8,128)(2,1)S(1)} async-done(((bf16[32,32,128]{2,1,0:T(8,128)(2,1)}), bf16[32,32,128]{2,1,0:T(8,128)(2,1)S(1)}, u32[]{:S(2)}, u32[]{:S(2)}) %all-to-all-start.1) | async-done | bytes 262176 | tf_op jit(solution)/shard_map/all_to_all | solution.py:397
  98.3 2.3 %collective-permute-start.7 = (f32[32,128]{1,0:T(8,128)S(1)}, f32[32,128]{1,0:T(8,128)S(1)}, u32[]{:S(2)}, u32[]{:S(2)}) collective-permute-start(f32[32,128]{1,0:T(8,128)S(1)} %convert_reduce_fusion), channel_id=1, source_target_pairs={{0,3},{1,0},{2,1},{3,2},{4,7},{5,4},{6,5},{7,6},{8,11},{9,8},{10,9... | collective-permute-start | bytes 49160 | tf_op jit(solution)/shard_map/ppermute | solution.py:250
  100.6 1.7 %collective-permute-start.6 = (f32[32,128]{1,0:T(8,128)S(1)}, f32[32,128]{1,0:T(8,128)S(1)}, u32[]{:S(2)}, u32[]{:S(2)}) collective-permute-start(f32[32,128]{1,0:T(8,128)S(1)} %convert_reduce_fusion), channel_id=1, source_target_pairs={{0,2},{1,3},{2,0},{3,1},{4,6},{5,7},{6,4},{7,5},{8,10},{9,11},{10,... | collective-permute-start | bytes 49160 | tf_op jit(solution)/shard_map/ppermute | solution.py:250
  102.3 0.1 dynamic_slice.24
  102.4 3.5 %collective-permute-done.6 = f32[32,128]{1,0:T(8,128)S(1)} collective-permute-done((f32[32,128]{1,0:T(8,128)S(1)}, f32[32,128]{1,0:T(8,128)S(1)}, u32[]{:S(2)}, u32[]{:S(2)}) %collective-permute-start.6) | collective-permute-done | bytes 16416 | tf_op jit(solution)/shard_map/ppermute | solution.py:250
  105.8 1.4 %collective-permute-done.5 = f32[32,128]{1,0:T(8,128)S(1)} collective-permute-done((f32[32,128]{1,0:T(8,128)S(1)}, f32[32,128]{1,0:T(8,128)S(1)}, u32[]{:S(2)}, u32[]{:S(2)}) %collective-permute-start.5) | collective-permute-done | bytes 16416 | tf_op jit(solution)/shard_map/ppermute | solution.py:250
  107.4 0.2 fusion.1
  107.6 0.7 fusion.9
  (40 shorter events, 0.7 us)
Async XLA Ops:
  0.6 88.4 %copy-start = (f32[100]{0:T(128)S(1)}, f32[100]{0:T(128)}, u32[]{:S(2)}) copy-start(f32[100]{0:T(128)} %param.14) | copy-start | bytes 1204
  2.7 11.1 %collective-permute-start.2 = (f32[3,10,128]{2,1,0:T(8,128)}, f32[3,10,128]{2,1,0:T(8,128)S(1)}, u32[]{:S(2)}, u32[]{:S(2)}) collective-permute-start(f32[3,10,128]{2,1,0:T(8,128)} %amp.1), channel_id=1, source_target_pairs={{0,3},{1,0},{2,1},{3,2},{4,7},{5,4},{6,5},{7,6},{8,11},{9,8},{10,9... | collective-permute-start | bytes 46088 | tf_op jit(solution)/shard_map/ppermute | solution.py:250
  5.7 8.1 %collective-permute-start.1 = (f32[3,10,128]{2,1,0:T(8,128)}, f32[3,10,128]{2,1,0:T(8,128)S(1)}, u32[]{:S(2)}, u32[]{:S(2)}) collective-permute-start(f32[3,10,128]{2,1,0:T(8,128)} %amp.1), channel_id=1, source_target_pairs={{0,2},{1,3},{2,0},{3,1},{4,6},{5,7},{6,4},{7,5},{8,10},{9,11},{10,... | collective-permute-start | bytes 46088 | tf_op jit(solution)/shard_map/ppermute | solution.py:250
  6.4 7.4 %collective-permute-start = (f32[3,10,128]{2,1,0:T(8,128)}, f32[3,10,128]{2,1,0:T(8,128)S(1)}, u32[]{:S(2)}, u32[]{:S(2)}) collective-permute-start(f32[3,10,128]{2,1,0:T(8,128)} %amp.1), channel_id=1, source_target_pairs={{0,1},{1,2},{2,3},{3,0},{4,5},{5,6},{6,7},{7,4},{8,9},{9,10},{10,1... | collective-permute-start | bytes 46088 | tf_op jit(solution)/shard_map/ppermute | solution.py:250
  7.3 6.5 %copy-start.3 = (f32[3,10,128]{2,1,0:T(8,128)S(1)}, f32[3,10,128]{2,1,0:T(8,128)}, u32[]{:S(2)}) copy-start(f32[3,10,128]{2,1,0:T(8,128)} %amp.1) | copy-start | bytes 46084
  14.7 13.4 %copy-start.2 = (s32[640]{0:T(1024)S(1)}, s32[640]{0:T(1024)}, u32[]{:S(2)}) copy-start(s32[640]{0:T(1024)} %vir_irrep.3) | copy-start | bytes 7684
  14.7 14.3 %copy-start.5 = (s32[2,2]{1,0:T(2,128)S(1)}, s32[2,2]{1,0:T(2,128)}, u32[]{:S(2)}) copy-start(s32[2,2]{1,0:T(2,128)} %pair_s.3) | copy-start | bytes 52
  14.7 14.5 %copy-start.1 = (s32[100]{0:T(128)S(1)}, s32[100]{0:T(128)}, u32[]{:S(2)}) copy-start(s32[100]{0:T(128)} %occ_s.3) | copy-start | bytes 1204
  14.7 49.9 %all-to-all-start = ((bf16[64,96,128]{2,1,0:T(8,128)(2,1)}), bf16[64,96,128]{2,1,0:T(8,128)(2,1)S(1)}, u32[]{:S(2)}, u32[]{:S(2)}) async-start(bf16[64,96,128]{2,1,0:T(8,128)(2,1)} %constant_dynamic-update-slice_fusion), calls=%async_computation | async-start | bytes 3145728 | tf_op jit(solution)/shard_map/all_to_all | solution.py:332
  64.7 3.6 %collective-permute-start.3 = (bf16[16,64,128]{2,1,0:T(8,128)(2,1)S(1)}, bf16[16,64,128]{2,1,0:T(8,128)(2,1)S(1)}, u32[]{:S(2)}, u32[]{:S(2)}) collective-permute-start(bf16[16,64,128]{2,1,0:T(8,128)(2,1)S(1)} %bitcast.37), channel_id=1, source_target_pairs={{0,4},{4,0},{8,12},{12,8},{16,20},{20,16},{24,28},{28,24},{32,36},... | collective-permute-start | bytes 786440 | tf_op jit(solution)/shard_map/ppermute | solution.py:374
  79.0 1.6 %collective-permute-start.4 = (bf16[32,32,128]{2,1,0:T(8,128)(2,1)S(1)}, bf16[32,32,128]{2,1,0:T(8,128)(2,1)S(1)}, u32[]{:S(2)}, u32[]{:S(2)}) collective-permute-start(bf16[32,32,128]{2,1,0:T(8,128)(2,1)S(1)} %get-tuple-element.21), channel_id=1, source_target_pairs={{0,4},{4,0},{8,12},{12,8},{16,20},{20,16},{24,28},{28,24},{32,36},... | collective-permute-start | bytes 786440 | tf_op jit(solution)/shard_map/ppermute | solution.py:395
  80.6 26.9 %copy-start.4 = (f32[2,10,160]{2,0,1:T(2,128)S(1)}, f32[2,10,160]{2,0,1:T(2,128)}, u32[]{:S(2)}) copy-start(f32[2,10,160]{2,0,1:T(2,128)} %param.10) | copy-start | bytes 38404
  81.4 16.8 %all-to-all-start.1 = ((bf16[32,32,128]{2,1,0:T(8,128)(2,1)}), bf16[32,32,128]{2,1,0:T(8,128)(2,1)S(1)}, u32[]{:S(2)}, u32[]{:S(2)}) async-start(bf16[32,32,128]{2,1,0:T(8,128)(2,1)} %add_convert_fusion), calls=%async_computation.1 | async-start | bytes 524288 | tf_op jit(solution)/shard_map/all_to_all | solution.py:397
  98.3 4.1 %collective-permute-start.7 = (f32[32,128]{1,0:T(8,128)S(1)}, f32[32,128]{1,0:T(8,128)S(1)}, u32[]{:S(2)}, u32[]{:S(2)}) collective-permute-start(f32[32,128]{1,0:T(8,128)S(1)} %convert_reduce_fusion), channel_id=1, source_target_pairs={{0,3},{1,0},{2,1},{3,2},{4,7},{5,4},{6,5},{7,6},{8,11},{9,8},{10,9... | collective-permute-start | bytes 49160 | tf_op jit(solution)/shard_map/ppermute | solution.py:250
  100.6 5.2 %collective-permute-start.6 = (f32[32,128]{1,0:T(8,128)S(1)}, f32[32,128]{1,0:T(8,128)S(1)}, u32[]{:S(2)}, u32[]{:S(2)}) collective-permute-start(f32[32,128]{1,0:T(8,128)S(1)} %convert_reduce_fusion), channel_id=1, source_target_pairs={{0,2},{1,3},{2,0},{3,1},{4,6},{5,7},{6,4},{7,5},{8,10},{9,11},{10,... | collective-permute-start | bytes 49160 | tf_op jit(solution)/shard_map/ppermute | solution.py:250
  102.3 4.9 %collective-permute-start.5 = (f32[32,128]{1,0:T(8,128)S(1)}, f32[32,128]{1,0:T(8,128)S(1)}, u32[]{:S(2)}, u32[]{:S(2)}) collective-permute-start(f32[32,128]{1,0:T(8,128)S(1)} %convert_reduce_fusion), channel_id=1, source_target_pairs={{0,1},{1,2},{2,3},{3,0},{4,5},{5,6},{6,7},{7,4},{8,9},{9,10},{10,1... | collective-permute-start | bytes 49160 | tf_op jit(solution)/shard_map/ppermute | solution.py:250

commit v11 on v10

--- a/solution.py
+++ b/solution.py
@@ -147,10 +147,8 @@
     got,
     amp_mine,
     amp_other,
-    row_irrep,
-    col_irrep,
-    row_pos,
-    col_pos,
+    row_code,
+    col_code,
     keep,
     give,
     ball,
@@ -163,13 +161,15 @@
 ):
     q_count = 2 * GROUPS
     core = scalars[q_count + 2]
-    vir_total = row_irrep.shape[0]
+    vir_total = row_code.shape[0]
+    row_irrep, row_pos = row_code[...] >> 10, row_code[...] & 1023
+    col_irrep, col_pos = col_code[...] >> 10, col_code[...] & 1023
     own = got.shape[1]
     row_count = vir_total // own
     per_row = 2 * GROUPS + 2
     lane = lax.broadcasted_iota(I32, (own, MAIN), 1)
     index = lax.broadcasted_iota(I32, (2 * MAIN, vir_total), 0)
-    column = col_pos[...]
+    column = col_pos
     for g in range(GROUPS):
         place = jnp.where(column < MAIN, column, column + g * STRIDE)
         unfold[g] = jnp.where(index == place, 1.0, 0.0).astype(BF)
@@ -203,9 +203,9 @@
         shifted = pltpu.roll(ball[:, at : at + MAIN].astype(F32), 1, 1)
         for g in range(GROUPS):
             q = u * GROUPS + g
-            want = jnp.bitwise_xor(row_irrep[...], scalars[q])
+            want = jnp.bitwise_xor(row_irrep, scalars[q])
             wide = dot(ball[:, q * 256 : (q + 1) * 256], unfold[g])
-            wide = jnp.where(want == col_irrep[...], wide, 0.0).astype(BF)
+            wide = jnp.where(want == col_irrep, wide, 0.0).astype(BF)
             half_main = dot(wide, amp_main[...])
             half_rest = dot(wide, amp_rest[g])
             for p in range(2):
@@ -221,9 +221,9 @@
     tail = None
     for p in range(2):
         value = lax.dot_general(hall[p], ball[...], NT, preferred_element_type=F32)
-        want = jnp.bitwise_xor(row_irrep[...], scalars[q_count + p])
-        value = jnp.where(want == col_irrep[...], value, 0.0).astype(BF)
-        place = row_pos[...]
+        want = jnp.bitwise_xor(row_irrep, scalars[q_count + p])
+        value = jnp.where(want == col_irrep, value, 0.0).astype(BF)
+        place = row_pos
         place = jnp.where(place < MAIN, place, place + p * 64)
         fold = jnp.where(lane2 == place, 1.0, 0.0).astype(BF)
         short = dot(value, fold)
@@ -357,16 +357,13 @@
     def mixed(x):
         return x.reshape(blk_count, row_count).T.reshape(vir_total)
 
-    irrep_mixed = mixed(vir_irrep)
-    pos_mixed = mixed(vir_pos)
+    code = mixed(vir_irrep * 1024 + vir_pos)
     own_irrep = lax.dynamic_index_in_dim(
         q_irrep.reshape(q_own, blk_count), blk_pos, axis=1, keepdims=False
     )
     tables = (
-        irrep_mixed[:, None],
-        irrep_mixed[None, :],
-        pos_mixed[:, None],
-        pos_mixed[None, :],
+        code[:, None],
+        code[None, :],
     )
 
     scalars = jnp.concatenate([own_irrep, pair_sym, (blk_pos & 1)[None]])
@@ -374,7 +371,7 @@
     amp_other = lax.ppermute(amp_mine, "blk", siblings)
     keep, give = pl.pallas_call(
         pair_kernel,
-        in_specs=[smem] + [vmem] * 7,
+        in_specs=[smem] + [vmem] * 5,
         out_specs=(vmem, vmem),
         out_shape=(
             jax.ShapeDtypeStruct((blk_count // 2, 32, MAIN), F32),

time: 110 us -> 110 us (level)
  transfers between devices with their start and end apart: 10 -> 10, of which waited for: 6 -> 6; matrix products, arithmetic and copies ran while one was open for 7% -> 6% of each run, Pallas kernels for 6% -> 6%
where the time goes in v11:
time: 110 us; the launch traced here: 108 us
  waiting for transfers between devices  48.7 us (44%)
  starting transfers between devices  29.8 us (27%)
  Pallas kernels  19.1 us (17%)
  local copies, waits for them, and re-layouts  7.33 us (7%)
  other arithmetic  2.2 us (2%)
    all_to_all x1, waiting for transfers between devices, per_device(): lax.all_to_all(packed, 'blk', split_axis=0, concat_axis=0, tiled=False)  34.4 us
    all_to_all x1, starting transfers between devices, per_device(): lax.all_to_all(packed, 'blk', split_axis=0, concat_axis=0, tiled=False)  12.3 us
    pallas_call x1, Pallas kernels, per_device(): pl.pallas_call(pair_kernel, in_specs=[smem] + [vmem] * 5, out_specs=(vmem...  10.7 us
    ppermute x6, starting transfers between devices, over_rep(): lax.ppermute(value, 'rep', [(i, (i + k) % 4) for i in range(4)])  8.64 us
    all_to_all x1, waiting for transfers between devices, per_device(): lax.all_to_all(part, 'blk', split_axis=0, concat_axis=0, axis_index_group...  7.81 us
    pallas_call x1, Pallas kernels, per_device(): pl.pallas_call(pack_kernel, grid=(row_count // rows,), in_specs=[smem, sm...  6.44 us
    all_to_all x1, starting transfers between devices, per_device(): lax.all_to_all(part, 'blk', split_axis=0, concat_axis=0, axis_index_group...  5.93 us
    ppermute x6, waiting for transfers between devices, over_rep(): lax.ppermute(value, 'rep', [(i, (i + k) % 4) for i in range(4)])  4.81 us
  transfers between devices with their start and end apart: 10, of which 6 were waited for; matrix products, arithmetic and copies ran while one was open for 6% of the time, Pallas kernels for 6%

profile of v11, /device:TPU:6, one launch (start us, length us, event | category | flops | bytes accessed | tf_op | source)
XLA Modules:
  0.0 108.2 jit_solution(7478806720216429736)
XLA Ops:
  0.6 2.1 %amp.1 = f32[3,10,128]{2,1,0:T(8,128)} custom-call(s32[100]{0:T(128)} %occ_s.3, s32[2,2]{1,0:T(2,128)} %pair_s.3, f32[10,2,160]{2,1,0:T(2,128)} %bitcast.42, s32[640]{0:T(1024)} %vir_irrep.3), custom_call_target="tpu_custom_call" | custom-call | tf_op jit(solution)/shard_map/amp/pallas_call | solution.py:275
  2.7 3.0 %collective-permute-start.2 = (f32[3,10,128]{2,1,0:T(8,128)}, f32[3,10,128]{2,1,0:T(8,128)S(1)}, u32[]{:S(2)}, u32[]{:S(2)}) collective-permute-start(f32[3,10,128]{2,1,0:T(8,128)} %amp.1), channel_id=1, source_target_pairs={{0,3},{1,0},{2,1},{3,2},{4,7},{5,4},{6,5},{7,6},{8,11},{9,8},{10,9... | collective-permute-start | bytes 46088 | tf_op jit(solution)/shard_map/ppermute | solution.py:250
  5.7 0.6 collective-permute-start.1
  6.3 1.0 collective-permute-start
  7.3 6.4 %pack.1 = bf16[64,96,128]{2,1,0:T(8,128)(2,1)} custom-call(s32[640]{0:T(1024)} %vir_irrep.3, s32[100]{0:T(128)} %occ_s.3, s32[2,2]{1,0:T(2,128)} %pair_s.3, bf16[10,384,640]{2,1,0:T(8,128)(2,1)} %bitcast.37, bf16[10,100,384]{2,1,0:T(8,128)(2,1)} %bitcast.39, bf16[100,640]{1,0:T(8,128)(2,1)} %singles.1, s32[640]{0:T(1024)} %vir_irrep.3, s32[1536]{0:T(1024)} %chol_irrep.1), custom_call_target="tpu_custom_call" | custom-call | flops 1258291200 | bytes 4915200 | tf_op jit(solution)/shard_map/pack/pallas_call | solution.py:287
  13.9 0.8 constant_dynamic-update-slice_fusion
  14.7 12.3 %all-to-all-start = ((bf16[64,96,128]{2,1,0:T(8,128)(2,1)}), bf16[64,96,128]{2,1,0:T(8,128)(2,1)S(1)}, u32[]{:S(2)}, u32[]{:S(2)}) async-start(bf16[64,96,128]{2,1,0:T(8,128)(2,1)} %constant_dynamic-update-slice_fusion), calls=%async_computation | async-start | bytes 3145728 | tf_op jit(solution)/shard_map/all_to_all | solution.py:332
  27.0 0.8 dynamic_slice.25
  27.7 0.1 reshape.107
  27.8 0.2 dynamic-slice_reduce_fusion
  28.0 0.1 convert_reduce_fusion.1
  28.1 0.1 select_reduce_fusion
  28.2 0.1 reshape.108
  28.4 0.1 copy.34
  28.4 0.1 broadcast_in_dim_reshape.7.col_code
  28.5 0.1 broadcast_in_dim_reshape.6
  28.6 0.2 fusion.11
  28.8 0.6 gather_fusion.1
  29.5 0.6 gather_fusion
  30.1 0.1 pad_add_fusion.scalars
  30.2 34.4 %all-to-all-done = bf16[64,96,128]{2,1,0:T(8,128)(2,1)S(1)} async-done(((bf16[64,96,128]{2,1,0:T(8,128)(2,1)}), bf16[64,96,128]{2,1,0:T(8,128)(2,1)S(1)}, u32[]{:S(2)}, u32[]{:S(2)}) %all-to-all-start) | async-done | bytes 1572896 | tf_op jit(solution)/shard_map/all_to_all | solution.py:332
  64.6 2.5 %collective-permute-start.3 = (bf16[16,64,128]{2,1,0:T(8,128)(2,1)S(1)}, bf16[16,64,128]{2,1,0:T(8,128)(2,1)S(1)}, u32[]{:S(2)}, u32[]{:S(2)}) collective-permute-start(bf16[16,64,128]{2,1,0:T(8,128)(2,1)S(1)} %bitcast.35), channel_id=1, source_target_pairs={{0,4},{4,0},{8,12},{12,8},{16,20},{20,16},{24,28},{28,24},{32,36},... | collective-permute-start | bytes 786440 | tf_op jit(solution)/shard_map/ppermute | solution.py:371
  67.1 0.1 slice.49
  67.2 0.3 copy.44
  67.6 0.2 copy.37.row_code
  67.7 0.5 collective-permute-done.3.amp_other
  68.3 10.7 %ladder.1 = (f32[32,32,128]{2,1,0:T(8,128)S(1)}, bf16[32,32,128]{2,1,0:T(8,128)(2,1)S(1)}) custom-call(s32[9]{0:T(128)S(1)} %pad_add_fusion.scalars, bf16[80,64,128]{2,1,0:T(8,128)(2,1)S(1)} %bitcast.34, bf16[16,64,128]{2,1,0:T(8,128)(2,1)S(1)} %bitcast.36, bf16[16,64,128]{2,1,0:T(8,128)(2,1)S(1)} %collective-permute-done.3.amp_other, ...), custom_call_target="tpu_custom_call" | custom-call | tf_op jit(solution)/shard_map/ladder/pallas_call | solution.py:372
  78.9 0.5 collective-permute-start.4
  79.4 1.2 %collective-permute-done.4 = bf16[32,32,128]{2,1,0:T(8,128)(2,1)S(1)} collective-permute-done((bf16[32,32,128]{2,1,0:T(8,128)(2,1)S(1)}, bf16[32,32,128]{2,1,0:T(8,128)(2,1)S(1)}, u32[]{:S(2)}, u32[]{:S(2)}) %collective-permute-start.4) | collective-permute-done | bytes 262176 | tf_op jit(solution)/shard_map/ppermute | solution.py:392
  80.6 0.8 add_convert_fusion
  81.3 5.9 %all-to-all-start.1 = ((bf16[32,32,128]{2,1,0:T(8,128)(2,1)}), bf16[32,32,128]{2,1,0:T(8,128)(2,1)S(1)}, u32[]{:S(2)}, u32[]{:S(2)}) async-start(bf16[32,32,128]{2,1,0:T(8,128)(2,1)} %add_convert_fusion), calls=%async_computation.1 | async-start | bytes 524288 | tf_op jit(solution)/shard_map/all_to_all | solution.py:394
  87.3 0.8 dynamic_slice.27
  88.0 0.8 dynamic_slice.28
  88.8 0.1 dynamic_slice.22
  88.9 0.1 dynamic_slice.23
  89.0 0.6 gather_fusion.3
  89.6 0.6 gather_fusion.2
  90.2 0.1 broadcast_xor_fusion
  90.3 7.8 %all-to-all-done.1 = bf16[32,32,128]{2,1,0:T(8,128)(2,1)S(1)} async-done(((bf16[32,32,128]{2,1,0:T(8,128)(2,1)}), bf16[32,32,128]{2,1,0:T(8,128)(2,1)S(1)}, u32[]{:S(2)}, u32[]{:S(2)}) %all-to-all-start.1) | async-done | bytes 262176 | tf_op jit(solution)/shard_map/all_to_all | solution.py:394
  98.2 2.3 %collective-permute-start.7 = (f32[32,128]{1,0:T(8,128)S(1)}, f32[32,128]{1,0:T(8,128)S(1)}, u32[]{:S(2)}, u32[]{:S(2)}) collective-permute-start(f32[32,128]{1,0:T(8,128)S(1)} %convert_reduce_fusion), channel_id=1, source_target_pairs={{0,3},{1,0},{2,1},{3,2},{4,7},{5,4},{6,5},{7,6},{8,11},{9,8},{10,9... | collective-permute-start | bytes 49160 | tf_op jit(solution)/shard_map/ppermute | solution.py:250
  100.5 1.7 %collective-permute-start.6 = (f32[32,128]{1,0:T(8,128)S(1)}, f32[32,128]{1,0:T(8,128)S(1)}, u32[]{:S(2)}, u32[]{:S(2)}) collective-permute-start(f32[32,128]{1,0:T(8,128)S(1)} %convert_reduce_fusion), channel_id=1, source_target_pairs={{0,2},{1,3},{2,0},{3,1},{4,6},{5,7},{6,4},{7,5},{8,10},{9,11},{10,... | collective-permute-start | bytes 49160 | tf_op jit(solution)/shard_map/ppermute | solution.py:250
  102.2 0.1 broadcast_subtract_fusion
  102.3 0.1 dynamic_slice.24
  102.3 3.4 %collective-permute-done.6 = f32[32,128]{1,0:T(8,128)S(1)} collective-permute-done((f32[32,128]{1,0:T(8,128)S(1)}, f32[32,128]{1,0:T(8,128)S(1)}, u32[]{:S(2)}, u32[]{:S(2)}) %collective-permute-start.6) | collective-permute-done | bytes 16416 | tf_op jit(solution)/shard_map/ppermute | solution.py:250
  105.7 1.4 %collective-permute-done.5 = f32[32,128]{1,0:T(8,128)S(1)} collective-permute-done((f32[32,128]{1,0:T(8,128)S(1)}, f32[32,128]{1,0:T(8,128)S(1)}, u32[]{:S(2)}, u32[]{:S(2)}) %collective-permute-start.5) | collective-permute-done | bytes 16416 | tf_op jit(solution)/shard_map/ppermute | solution.py:250
  107.2 0.1 slice_bitcast_fusion.1
  107.2 0.2 fusion.1
  107.5 0.7 fusion.9
  (34 shorter events, 0.3 us)
Async XLA Ops:
  0.6 88.3 %copy-start = (f32[100]{0:T(128)S(1)}, f32[100]{0:T(128)}, u32[]{:S(2)}) copy-start(f32[100]{0:T(128)} %param.14) | copy-start | bytes 1204
  2.7 11.1 %collective-permute-start.2 = (f32[3,10,128]{2,1,0:T(8,128)}, f32[3,10,128]{2,1,0:T(8,128)S(1)}, u32[]{:S(2)}, u32[]{:S(2)}) collective-permute-start(f32[3,10,128]{2,1,0:T(8,128)} %amp.1), channel_id=1, source_target_pairs={{0,3},{1,0},{2,1},{3,2},{4,7},{5,4},{6,5},{7,6},{8,11},{9,8},{10,9... | collective-permute-start | bytes 46088 | tf_op jit(solution)/shard_map/ppermute | solution.py:250
  5.7 8.1 %collective-permute-start.1 = (f32[3,10,128]{2,1,0:T(8,128)}, f32[3,10,128]{2,1,0:T(8,128)S(1)}, u32[]{:S(2)}, u32[]{:S(2)}) collective-permute-start(f32[3,10,128]{2,1,0:T(8,128)} %amp.1), channel_id=1, source_target_pairs={{0,2},{1,3},{2,0},{3,1},{4,6},{5,7},{6,4},{7,5},{8,10},{9,11},{10,... | collective-permute-start | bytes 46088 | tf_op jit(solution)/shard_map/ppermute | solution.py:250
  6.3 7.4 %collective-permute-start = (f32[3,10,128]{2,1,0:T(8,128)}, f32[3,10,128]{2,1,0:T(8,128)S(1)}, u32[]{:S(2)}, u32[]{:S(2)}) collective-permute-start(f32[3,10,128]{2,1,0:T(8,128)} %amp.1), channel_id=1, source_target_pairs={{0,1},{1,2},{2,3},{3,0},{4,5},{5,6},{6,7},{7,4},{8,9},{9,10},{10,1... | collective-permute-start | bytes 46088 | tf_op jit(solution)/shard_map/ppermute | solution.py:250
  7.3 6.5 %copy-start.3 = (f32[3,10,128]{2,1,0:T(8,128)S(1)}, f32[3,10,128]{2,1,0:T(8,128)}, u32[]{:S(2)}) copy-start(f32[3,10,128]{2,1,0:T(8,128)} %amp.1) | copy-start | bytes 46084
  14.7 13.4 %copy-start.2 = (s32[640]{0:T(1024)S(1)}, s32[640]{0:T(1024)}, u32[]{:S(2)}) copy-start(s32[640]{0:T(1024)} %vir_irrep.3) | copy-start | bytes 7684
  14.7 13.9 %copy-start.5 = (s32[2,2]{1,0:T(2,128)S(1)}, s32[2,2]{1,0:T(2,128)}, u32[]{:S(2)}) copy-start(s32[2,2]{1,0:T(2,128)} %pair_s.3) | copy-start | bytes 52
  14.7 14.2 %copy-start.1 = (s32[100]{0:T(128)S(1)}, s32[100]{0:T(128)}, u32[]{:S(2)}) copy-start(s32[100]{0:T(128)} %occ_s.3) | copy-start | bytes 1204
  14.7 49.9 %all-to-all-start = ((bf16[64,96,128]{2,1,0:T(8,128)(2,1)}), bf16[64,96,128]{2,1,0:T(8,128)(2,1)S(1)}, u32[]{:S(2)}, u32[]{:S(2)}) async-start(bf16[64,96,128]{2,1,0:T(8,128)(2,1)} %constant_dynamic-update-slice_fusion), calls=%async_computation | async-start | bytes 3145728 | tf_op jit(solution)/shard_map/all_to_all | solution.py:332
  64.6 3.6 %collective-permute-start.3 = (bf16[16,64,128]{2,1,0:T(8,128)(2,1)S(1)}, bf16[16,64,128]{2,1,0:T(8,128)(2,1)S(1)}, u32[]{:S(2)}, u32[]{:S(2)}) collective-permute-start(bf16[16,64,128]{2,1,0:T(8,128)(2,1)S(1)} %bitcast.35), channel_id=1, source_target_pairs={{0,4},{4,0},{8,12},{12,8},{16,20},{20,16},{24,28},{28,24},{32,36},... | collective-permute-start | bytes 786440 | tf_op jit(solution)/shard_map/ppermute | solution.py:371
  78.9 1.6 %collective-permute-start.4 = (bf16[32,32,128]{2,1,0:T(8,128)(2,1)S(1)}, bf16[32,32,128]{2,1,0:T(8,128)(2,1)S(1)}, u32[]{:S(2)}, u32[]{:S(2)}) collective-permute-start(bf16[32,32,128]{2,1,0:T(8,128)(2,1)S(1)} %get-tuple-element.17), channel_id=1, source_target_pairs={{0,4},{4,0},{8,12},{12,8},{16,20},{20,16},{24,28},{28,24},{32,36},... | collective-permute-start | bytes 786440 | tf_op jit(solution)/shard_map/ppermute | solution.py:392
  80.6 26.9 %copy-start.4 = (f32[2,10,160]{2,0,1:T(2,128)S(1)}, f32[2,10,160]{2,0,1:T(2,128)}, u32[]{:S(2)}) copy-start(f32[2,10,160]{2,0,1:T(2,128)} %param.10) | copy-start | bytes 38404
  81.3 16.8 %all-to-all-start.1 = ((bf16[32,32,128]{2,1,0:T(8,128)(2,1)}), bf16[32,32,128]{2,1,0:T(8,128)(2,1)S(1)}, u32[]{:S(2)}, u32[]{:S(2)}) async-start(bf16[32,32,128]{2,1,0:T(8,128)(2,1)} %add_convert_fusion), calls=%async_computation.1 | async-start | bytes 524288 | tf_op jit(solution)/shard_map/all_to_all | solution.py:394
  98.2 4.2 %collective-permute-start.7 = (f32[32,128]{1,0:T(8,128)S(1)}, f32[32,128]{1,0:T(8,128)S(1)}, u32[]{:S(2)}, u32[]{:S(2)}) collective-permute-start(f32[32,128]{1,0:T(8,128)S(1)} %convert_reduce_fusion), channel_id=1, source_target_pairs={{0,3},{1,0},{2,1},{3,2},{4,7},{5,4},{6,5},{7,6},{8,11},{9,8},{10,9... | collective-permute-start | bytes 49160 | tf_op jit(solution)/shard_map/ppermute | solution.py:250
  100.5 5.2 %collective-permute-start.6 = (f32[32,128]{1,0:T(8,128)S(1)}, f32[32,128]{1,0:T(8,128)S(1)}, u32[]{:S(2)}, u32[]{:S(2)}) collective-permute-start(f32[32,128]{1,0:T(8,128)S(1)} %convert_reduce_fusion), channel_id=1, source_target_pairs={{0,2},{1,3},{2,0},{3,1},{4,6},{5,7},{6,4},{7,5},{8,10},{9,11},{10,... | collective-permute-start | bytes 49160 | tf_op jit(solution)/shard_map/ppermute | solution.py:250
  102.2 4.9 %collective-permute-start.5 = (f32[32,128]{1,0:T(8,128)S(1)}, f32[32,128]{1,0:T(8,128)S(1)}, u32[]{:S(2)}, u32[]{:S(2)}) collective-permute-start(f32[32,128]{1,0:T(8,128)S(1)} %convert_reduce_fusion), channel_id=1, source_target_pairs={{0,1},{1,2},{2,3},{3,0},{4,5},{5,6},{6,7},{7,4},{8,9},{9,10},{10,1... | collective-permute-start | bytes 49160 | tf_op jit(solution)/shard_map/ppermute | solution.py:250
